TPU v7x, 1024 devices: a whole 4x8x16 slice. The times are simulated.
1024 devices in a mesh: row: 32 (over y, z_hi), col: 32 (over x, z_lo, core).
Axes of the slice: x: 4, y: 8, z: 16 (z_hi: 4, z_lo: 4; z = z_hi * 4 + z_lo), core: 2. Of those that a mesh axis runs over, the one named last changes fastest.
Arguments:
- features: bfloat16 [131072, 256], P(('row', 'col')), may hold values from -6 to 6
- node_order: int32 [1024, 128], P(('row', 'col')), may hold values from 0 to 127, each once within a row
- tile_index: int32 [1024, 96], P(('row', 'col')), may hold values from 0 to 1023
- tile_count: int32 [1024], P(('row', 'col')), may hold values from 1 to 96, as said below
- tile_values: bfloat16 [1024, 96, 128, 128], P(('row', 'col')), may hold values from 0 to 0.022094727
- weight: bfloat16 [256, 256], replicated, may hold values from -0.375 to 0.375
- out_bias: float32 [256], replicated, may hold values from -3 to 3
- out_grad: bfloat16 [131072, 256], P(('row', 'col')), may hold values from -0.049560547 to 0.049560547
Outputs:
- activated: bfloat16 [131072, 256], P(('row', 'col'))
- weight_grad: float32 [256, 256], replicated
- bias_grad: float32 [256], replicated
Inputs may be any that keep to these rules, and one draw needn't show every extreme that they name: `node_order`: each device's row is an ordering of 0 to 127. `tile_index`: positions may repeat within a device's slots. `tile_count`: some device uses all 96 slots.
All inputs are finite; a program needn't handle non-finite values.
Results may differ from a plain program's by a relative error of at most 0.0053.
Values may be sent and summed in bfloat16 or wider, within the bound.
No kernel may reach another device: no remote copies, remote signals or barrier semaphores. Data moves between devices by JAX's collectives and lax.ppermute only.
A program may use at most 64 MiB of HBM per device.

v0:
```python
import math

import jax
import jax.numpy as jnp
from jax import lax
from jax.sharding import PartitionSpec as P


def block_sum(carry, tiles, sources, tile_rows, live):
    prods = jnp.einsum("kab,kbf->kaf", tiles, sources, preferred_element_type=jnp.float32)
    masked = jnp.where(live[:, None, None], prods, 0.0)
    return carry.at[tile_rows].add(masked)


def aggregate(source, tile_values, tile_index, tile_count, grid_out):
    slots = tile_index.shape[1]
    tile_side = tile_values.shape[2]
    feat_width = source.shape[1]
    grid_in = source.shape[0] // tile_side
    per_block = math.gcd(slots, 32)
    num_blocks = slots // per_block
    index_row = tile_index[0]
    tile_rows = (index_row // grid_in).reshape(num_blocks, per_block)
    tile_cols = (index_row % grid_in).reshape(num_blocks, per_block)
    live = (jnp.arange(slots, dtype=jnp.int32) < tile_count[0]).reshape(num_blocks, per_block)
    tiles_split = tile_values[0].reshape(num_blocks, per_block, tile_side, tile_side)
    source_split = source.reshape(grid_in, tile_side, feat_width)
    start_sum = jnp.zeros((grid_out, tile_side, feat_width), jnp.float32)

    def one_block(carry, pieces):
        tiles, cols_now, rows_now, live_now = pieces
        return (block_sum(carry, tiles, source_split[cols_now], rows_now, live_now), None)

    partial_value, _ = lax.scan(one_block, start_sum, (tiles_split, tile_cols, tile_rows, live))
    return partial_value.reshape(grid_out * tile_side, feat_width)


def local(features, node_order, tile_index, tile_count, tile_values, weight, out_bias, out_grad):
    own_rows, feat_width = features.shape
    tile_side = tile_values.shape[2]
    grid_out = lax.axis_size("col") * own_rows // tile_side
    order = node_order[0]
    clustered = features[order]
    source = lax.all_gather(clustered, "row", axis=0, tiled=True)
    partial_value = aggregate(source, tile_values, tile_index, tile_count, grid_out)
    aggregated = lax.psum_scatter(partial_value, "col", scatter_dimension=0, tiled=True)
    agg_round = aggregated.astype(jnp.bfloat16)
    pre_act = jnp.dot(agg_round, weight, preferred_element_type=jnp.float32) + out_bias
    sig = jax.nn.sigmoid(pre_act)
    act_clustered = (pre_act * sig).astype(jnp.bfloat16)
    activated = jnp.zeros_like(act_clustered).at[order].set(act_clustered)
    grad_clustered = out_grad[order].astype(jnp.float32)
    grad_pre = grad_clustered * sig * (1.0 + pre_act * (1.0 - sig))
    grad_round = grad_pre.astype(jnp.bfloat16)
    local_wgrad = lax.dot_general(
        agg_round, grad_round, (((0,), (0,)), ((), ())), preferred_element_type=jnp.float32
    )
    local_bgrad = jnp.sum(grad_pre, axis=0)
    weight_grad, bias_grad = lax.psum((local_wgrad, local_bgrad), ("row", "col"))
    return (activated, weight_grad, bias_grad)


def solution(mesh):
    return jax.shard_map(
        local,
        mesh=mesh,
        in_specs=(
            P(("row", "col"), None),
            P(("row", "col"), None),
            P(("row", "col"), None),
            P(("row", "col")),
            P(("row", "col"), None, None, None),
            P(),
            P(),
            P(("row", "col"), None),
        ),
        out_specs=(P(("row", "col"), None), P(), P()),
        check_vma=False,
    )
```

profile of v0, /device:TPU:1, one launch (start us, length us, event | category | flops | bytes accessed | tf_op | source)
XLA Modules:
  0.0 830.4 jit_solution(18034821154067991962)
XLA Ops:
  7.2 0.0 copy-start
  7.2 0.0 all-gather.3.cloned.1.call-start
  7.2 0.7 fusion.14
  7.9 2.2 gather_fusion.1
  10.2 0.0 all-gather.3.cloned.1.call-update
  10.2 0.0 reduce-scatter.2.cloned.1.call-start
  10.2 0.5 broadcast.126
  10.7 1.3 reduce.3
  12.1 0.1 squeeze.23
  12.8 125.2 %all-gather.3.cloned.1.call-done = bf16[4096,256]{1,0:T(8,128)(2,1)} async-done(((bf16[128,256]{1,0:T(8,128)(2,1)}), bf16[4096,256]{1,0:T(8,128)(2,1)}) %all-gather.3.cloned.1.call-update) | async-done | bytes 2097168 | tf_op jit(solution)/shard_map/all_gather | solution.py:44
  138.1 2.5 broadcast_in_dim.28
  140.5 48.3 %while.10 = (s32[]{:T(128)}, f32[32,128,256]{2,1,0:T(8,128)}, s32[3,32]{1,0:T(4,128)S(1)}, pred[3,32]{1,0:T(4,128)(4,1)S(1)}, bf16[3,32,128,128]{3,2,1,0:T(8,128...) while((s32[]{:T(128)}, f32[32,128,256]{2,1,0:T(8,128)}, s32[3,32]{1,0:T(4,128)S(1)}, ...), condition=%wide.region_2.3_spmd, body=%wide.region_0.2_spmd.sunk | while | flops 270533824 | bytes 24122940 | solution.py:34
  140.5 2.3 gather_fusion
  142.8 3.9 convolution_select_fusion.2
  146.7 10.0 %scatter_fusion = f32[32,128,256]{2,1,0:T(8,128)} fusion(f32[32,128,256]{2,1,0:T(8,128)} %get-tuple-element.117, s32[32]{0:T(128)S(1)} %get-tuple-element.106, f32[32,128,256]{2,1,0:T(8,128)} %convolution_select_fusion.2), kind=kCustom, calls=%fused_computation.3.clone.1 | custom fusion | flops 1048576 | bytes 12583040 | tf_op jit(solution)/shard_map/while/body/eval_jaxpr/scatter-add | solution.py:12
  156.7 2.3 gather_fusion
  159.0 3.8 convolution_select_fusion.2
  162.8 10.0 %scatter_fusion = f32[32,128,256]{2,1,0:T(8,128)} fusion(f32[32,128,256]{2,1,0:T(8,128)} %get-tuple-element.117, s32[32]{0:T(128)S(1)} %get-tuple-element.106, f32[32,128,256]{2,1,0:T(8,128)} %convolution_select_fusion.2), kind=kCustom, calls=%fused_computation.3.clone.1 | custom fusion | flops 1048576 | bytes 12583040 | tf_op jit(solution)/shard_map/while/body/eval_jaxpr/scatter-add | solution.py:12
  172.8 2.3 gather_fusion
  175.1 3.8 convolution_select_fusion.2
  179.0 9.9 %scatter_fusion = f32[32,128,256]{2,1,0:T(8,128)} fusion(f32[32,128,256]{2,1,0:T(8,128)} %get-tuple-element.117, s32[32]{0:T(128)S(1)} %get-tuple-element.106, f32[32,128,256]{2,1,0:T(8,128)} %convolution_select_fusion.2), kind=kCustom, calls=%fused_computation.3.clone.1 | custom fusion | flops 1048576 | bytes 12583040 | tf_op jit(solution)/shard_map/while/body/eval_jaxpr/scatter-add | solution.py:12
  188.8 0.0 copy-start.1
  188.8 0.0 copy-start.2
  188.8 0.0 reduce-scatter.2.cloned.1.call-update
  188.9 0.0 all-reduce.2.cloned.1.call-start
  188.9 0.8 copy-done.1
  189.7 0.8 gather_fusion.2
  190.5 149.7 %reduce-scatter.2.cloned.1.call-done = f32[128,256]{1,0:T(8,128)} async-done(((f32[4096,256]{1,0:T(8,128)}), f32[128,256]{1,0:T(8,128)}) %reduce-scatter.2.cloned.1.call-update) | async-done | bytes 131088 | tf_op jit(solution)/shard_map/reduce_scatter | solution.py:46
  340.3 0.0 copy-done
  340.3 0.0 copy-done.2
  340.3 1.1 fusion.15
  341.4 1.8 fusion.7
  343.2 0.0 all-reduce.2.cloned.1.call-update
  343.3 1.6 scatter_custom_fusion.1
  344.9 126.2 %psum.15 = f32[256]{0:T(256)} all-reduce(f32[256]{0:T(256)S(1)} %get-tuple-element.59), channel_id=1, replica_groups=mesh['row'=32,'col'=32] {'row','col'}, use_global_device_ids=true, to_apply=%region_7.8 | all-reduce | flops 256 | bytes 2048 | tf_op jit(solution)/shard_map/psum | solution.py:59
  471.1 351.0 %all-reduce.2.cloned.1.call-done = f32[256,256]{1,0:T(8,128)} async-done(((f32[256,256]{1,0:T(8,128)}), f32[256,256]{1,0:T(8,128)}) %all-reduce.2.cloned.1.call-update) | async-done | bytes 262160 | tf_op jit(solution)/shard_map/psum | solution.py:59
  822.2 1.7 copy.22
  (12 shorter events, 0.1 us)
Async XLA Ops:
  7.2 333.1 %copy-start = (bf16[256,256]{1,0:T(8,128)(2,1)S(1)}, bf16[256,256]{1,0:T(8,128)(2,1)}, u32[]{:S(2)}) copy-start(bf16[256,256]{1,0:T(8,128)(2,1)} %param.15) | copy-start | bytes 393220
  7.2 130.9 %all-gather.3.cloned.1.call-start = ((), (), s32[]{:S(2)}) async-start(), calls=%async_computation.3 | async-start | bytes 2162688 | tf_op jit(solution)/shard_map/all_gather | solution.py:44
  10.2 330.1 %reduce-scatter.2.cloned.1.call-start = ((), (), s32[]{:S(2)}) async-start(), calls=%async_computation.1 | async-start | bytes 4325376 | tf_op jit(solution)/shard_map/reduce_scatter | solution.py:46
  188.8 0.8 copy-start.1
  188.8 151.4 %copy-start.2 = (f32[256]{0:T(256)S(1)}, f32[256]{0:T(256)}, u32[]{:S(2)}) copy-start(f32[256]{0:T(256)} %param.16) | copy-start | bytes 3076
  188.9 633.3 %all-reduce.2.cloned.1.call-start = ((), (), s32[]{:S(2)}) async-start(), calls=%async_computation.2 | async-start | bytes 524288 | tf_op jit(solution)/shard_map/psum | solution.py:59
Sparse Core Ops, SparseCore 0:
  12.9 125.0 all-gather.2
  189.0 151.2 reduce-scatter.1
  346.3 475.8 all-reduce.1
where the time goes:
time: 832 us; the launch traced here: 830 us
  waiting for transfers between devices  626 us (75%)
  blocking collectives  126 us (15%)
  other arithmetic  33.5 us (4%)
  local copies, waits for them, and re-layouts  15.4 us (2%)
  matrix products  14.5 us (2%)
  between operations  14.4 us (2%)
    psum x1, waiting for transfers between devices, local(): lax.psum((local_wgrad, local_bgrad), ('row', 'col'))  351 us
    reduce_scatter x1, waiting for transfers between devices, local(): lax.psum_scatter(partial_value, 'col', scatter_dimension=0, tiled=True)  150 us
    psum x1, blocking collectives, local(): lax.psum((local_wgrad, local_bgrad), ('row', 'col'))  126 us
    all_gather x1, waiting for transfers between devices, local(): source = lax.all_gather(clustered, 'row', axis=0, tiled=True)  125 us
    scatter-add x3, other arithmetic, block_sum(): return carry.at[tile_rows].add(masked)  29.8 us
  transfers between devices with their start and end apart: 3, of which 3 were waited for; matrix products, arithmetic and copies ran while one was open for 1% of the time, Pallas kernels for 0%

commit v1 on v0

v1 whole, which is shorter than its diff:
```python
import jax
import jax.numpy as jnp
from jax import lax
from jax.experimental import pallas as pl
from jax.experimental.pallas import tpu as pltpu
from jax.sharding import Mesh, PartitionSpec as P

AXES = ("y", "zh", "x", "zl", "core")
COL = ("x", "zl", "core")
T = 128
F = 256
TILES = 96
GRID = 32
CHUNK = 16
UNROLL = 8
BF = jnp.bfloat16
F32 = jnp.float32


def cluster_body(order, feats, out):
    place = lax.broadcasted_iota(jnp.int32, (T, T), 0) == order[...]
    hot = place.astype(F32).astype(BF)
    out[...] = lax.dot_general(
        hot, feats[...], (((0,), (0,)), ((), ())), preferred_element_type=F32
    ).astype(BF)


def cluster(order, feats):
    return pl.pallas_call(
        cluster_body,
        out_shape=jax.ShapeDtypeStruct((T, F), BF),
        name="cluster",
    )(order, feats)


def tiles_body(me, index, count, *refs):
    tiles, pieces, out = refs[0], refs[1:10], refs[10]
    src, vals, acc, piece_sem, tile_sem = refs[11:]
    copies = []
    row = 0
    for i, piece in enumerate(pieces):
        rows = piece.shape[0]
        copies.append(pltpu.make_async_copy(piece, src.at[pl.ds(row, rows)], piece_sem.at[i]))
        row += rows
    loads = [
        pltpu.make_async_copy(tiles.at[pl.ds(c * CHUNK, CHUNK)], vals.at[pl.ds(c * CHUNK, CHUNK)], tile_sem.at[c])
        for c in range(TILES // CHUNK)
    ]
    for copy in copies + loads:
        copy.start()

    @pl.loop(0, GRID + 1)
    def _(r):
        acc[r] = jnp.zeros((T, F), F32)

    for copy in copies:
        copy.wait()
    used = count[0]
    here = me[0]
    for c, load in enumerate(loads):
        load.wait()

        @pl.loop(0, CHUNK // UNROLL)
        def _(g):
            first = c * CHUNK + g * UNROLL

            @pl.when(first < used)
            def _():
                for u in range(UNROLL):
                    k = first + u
                    at = index[0, k]
                    to = jnp.where(k < used, at // GRID, GRID)
                    col = at % GRID
                    slot = ((here - col // 4) & 7) * 4 + (col & 3)
                    start = pl.multiple_of(slot * T, T)
                    acc[to] += jnp.dot(vals[k], src[pl.ds(start, T), :], preferred_element_type=F32)

    @pl.loop(0, GRID)
    def _(r):
        out[(r & 1) * (GRID // 2) + (r >> 1)] = acc[r].astype(out.dtype)


def tile_sums(me, index, count, tiles, pieces):
    smem = pl.BlockSpec(memory_space=pltpu.SMEM)
    hbm = pl.BlockSpec(memory_space=pl.ANY)
    return pl.pallas_call(
        tiles_body,
        out_shape=jax.ShapeDtypeStruct((GRID, T, F), BF),
        in_specs=[smem] * 3 + [hbm] * (1 + len(pieces)),
        out_specs=pl.BlockSpec(memory_space=pltpu.VMEM),
        scratch_shapes=[
            pltpu.VMEM((GRID * T, F), BF),
            pltpu.VMEM((TILES, T, T), BF),
            pltpu.VMEM((GRID + 1, T, F), F32),
            pltpu.SemaphoreType.DMA((len(pieces),)),
            pltpu.SemaphoreType.DMA((TILES // CHUNK,)),
        ],
        compiler_params=pltpu.CompilerParams(vmem_limit_bytes=40 * 2**20),
        cost_estimate=pl.CostEstimate(
            flops=2 * TILES * T * T * F, bytes_accessed=8 * 2**20, transcendentals=0
        ),
        name="tile_sums",
    )(me, index, count, tiles, *pieces)


def finish_body(parts, order, weight, bias, out_grad, act_out, grads):
    total = parts[0].astype(F32)
    for i in range(1, parts.shape[0]):
        total += parts[i].astype(F32)
    agg = total.astype(BF)
    place = lax.broadcasted_iota(jnp.int32, (T, T), 0) == order[...]
    hot = place.astype(F32).astype(BF)
    pre = jnp.dot(agg, weight[...], preferred_element_type=F32) + bias[...]
    sig = jax.nn.sigmoid(pre)
    act = (pre * sig).astype(BF)
    act_out[...] = jnp.dot(hot, act, preferred_element_type=F32).astype(BF)
    cot = lax.dot_general(hot, out_grad[...], (((0,), (0,)), ((), ())), preferred_element_type=F32)
    grad = cot * sig * (1.0 + pre * (1.0 - sig))
    grads[:, :F] = lax.dot_general(
        agg, grad.astype(BF), (((0,), (0,)), ((), ())), preferred_element_type=F32
    )
    sums = jnp.sum(grad, axis=0, keepdims=True)
    grads[:, F:] = jnp.zeros((F, T), F32)
    grads[0:1, F:] = sums[:, :T]
    grads[8:9, F:] = sums[:, T:]


def finish(parts, order, weight, bias, out_grad):
    return pl.pallas_call(
        finish_body,
        out_shape=(jax.ShapeDtypeStruct((T, F), BF), jax.ShapeDtypeStruct((F, F + T), F32)),
        compiler_params=pltpu.CompilerParams(vmem_limit_bytes=40 * 2**20),
        name="finish",
    )(parts, order, weight, bias, out_grad)


def ring_gather(own):
    up = [(i, (i + 1) % 8) for i in range(8)]
    down = [(i, (i - 1) % 8) for i in range(8)]
    half = own.shape[0] // 2
    below, above = [own], [own]
    for _ in range(3):
        below.append(lax.ppermute(below[-1], "y", up))
        above.append(lax.ppermute(above[-1], "y", down))
    far = [lax.ppermute(below[-1][:half], "y", up), lax.ppermute(above[-1][half:], "y", down)]
    return below + far + above[:0:-1]


def local(features, node_order, tile_index, tile_count, tile_values, weight, out_bias, out_grad):
    clustered = cluster(node_order, features)
    near = lax.all_gather(clustered, "zh", axis=0, tiled=True)
    pieces = ring_gather(near)
    me = lax.axis_index("y").astype(jnp.int32).reshape(1)
    sums = tile_sums(me, tile_index, tile_count, tile_values[0], pieces)
    swapped = lax.all_to_all(sums, "core", 0, 0, tiled=True)
    half = GRID // 2
    paired = (swapped[:half].astype(F32) + swapped[half:].astype(F32)).astype(BF)
    parts = lax.all_to_all(paired, ("x", "zl"), 0, 0, tiled=True)
    activated, grads = finish(parts, node_order, weight, out_bias.reshape(1, F), out_grad)
    mine = lax.all_to_all(grads, COL, 0, 0, tiled=True).reshape(GRID, 8, F + T).sum(axis=0)
    mine = lax.psum(lax.psum(mine, "y"), "zh")
    whole = lax.all_to_all(jnp.tile(mine, (GRID, 1)), COL, 0, 0, tiled=True)
    bias_grad = jnp.concatenate([whole[0, F:], whole[8, F:]])
    return activated, whole[:, :F], bias_grad


def solution(mesh):
    fine = Mesh(mesh.devices.reshape(8, 4, 4, 4, 2), AXES)
    return jax.shard_map(
        local,
        mesh=fine,
        in_specs=(
            P(AXES, None),
            P(AXES, None),
            P(AXES, None),
            P(AXES),
            P(AXES, None, None, None),
            P(),
            P(),
            P(AXES, None),
        ),
        out_specs=(P(AXES, None), P(), P()),
        check_vma=False,
    )
```

time: 832 us -> 218 us (0.26)
  waiting for transfers between devices: 626 us -> 9.49 us
  blocking collectives: 126 us -> 163 us
  other arithmetic: 33.5 us -> 0.94 us
  starting transfers between devices: 0.12 us -> 30.1 us
  matrix products: 14.5 us -> 0 us
  between operations: 14.4 us -> 1.43 us
  local copies, waits for them, and re-layouts: 15.4 us -> 3.33 us
  Pallas kernels: 0 us -> 8.63 us
    psum x1 -> x0, waiting for transfers between devices: 351 us -> none  [local(): lax.psum((local_wgrad, local_bgrad), ('row', 'col'))]
    reduce_scatter x1 -> x0, waiting for transfers between devices: 150 us -> none  [local(): lax.psum_scatter(partial_value, 'col', scatter_dimension=0, tiled=True)]
    all_gather x1 -> x0, waiting for transfers between devices: 125 us -> none  [local(): source = lax.all_gather(clustered, 'row', axis=0, tiled=True)]
    all_to_all x0 -> x4, blocking collectives: none -> 93.3 us  [the longest x1 38.8 us: local(): parts = lax.all_to_all(paired, ('x', 'zl'), 0, 0, tiled=True)]
    psum x1 -> x2, blocking collectives: 126 us -> 40.7 us  [local(): mine = lax.psum(lax.psum(mine, 'y'), 'zh')]
    ppermute x0 -> x8, starting transfers between devices: none -> 30.1 us  [the longest x3 17.4 us: ring_gather(): above.append(lax.ppermute(above[-1], 'y', down))]
    scatter-add x3 -> x0, other arithmetic: 29.8 us -> none  [block_sum(): return carry.at[tile_rows].add(masked)]
    all_gather x0 -> x1, blocking collectives: none -> 29 us  [local(): near = lax.all_gather(clustered, 'zh', axis=0, tiled=True)]
  transfers between devices with their start and end apart: 3 -> 8, of which waited for: 3 -> 4; matrix products, arithmetic and copies ran while one was open for 1% -> 0% of each run, Pallas kernels for 0% -> 0%
where the time goes in v1:
time: 218 us; the launch traced here: 217 us
  blocking collectives  163 us (75%)
  starting transfers between devices  30.1 us (14%)
  waiting for transfers between devices  9.49 us (4%)
  Pallas kernels  8.63 us (4%)
  local copies, waits for them, and re-layouts  3.33 us (2%)
    psum x2, blocking collectives, local(): mine = lax.psum(lax.psum(mine, 'y'), 'zh')  40.7 us
    all_to_all x1, blocking collectives, local(): parts = lax.all_to_all(paired, ('x', 'zl'), 0, 0, tiled=True)  38.8 us
    all_gather x1, blocking collectives, local(): near = lax.all_gather(clustered, 'zh', axis=0, tiled=True)  29 us
    all_to_all x1, blocking collectives, local(): whole = lax.all_to_all(jnp.tile(mine, (GRID, 1)), COL, 0, 0, tiled=True)  27.8 us
    all_to_all x1, blocking collectives, local(): lax.all_to_all(grads, COL, 0, 0, tiled=True).reshape(GRID, 8, F + T)  18.8 us
    ppermute x3, starting transfers between devices, ring_gather(): above.append(lax.ppermute(above[-1], 'y', down))  17.4 us
    all_to_all x1, blocking collectives, local(): swapped = lax.all_to_all(sums, 'core', 0, 0, tiled=True)  7.89 us
    pallas_call x1, Pallas kernels, tile_sums(): pl.pallas_call(tiles_body, out_shape=jax.ShapeDtypeStruct((GRID, T, F), B...  5.87 us
  transfers between devices with their start and end apart: 8, of which 4 were waited for; matrix products, arithmetic and copies ran while one was open for 0% of the time, Pallas kernels for 0%

profile of v1, /device:TPU:1, one launch (start us, length us, event | category | flops | bytes accessed | tf_op | source)
XLA Modules:
  0.0 216.9 jit_solution(3429032196529352793)
XLA Ops:
  0.6 1.7 cluster.1
  2.3 29.0 %all_gather.3.refs_1_ = bf16[512,256]{1,0:T(8,128)(2,1)S(1)} all-gather(bf16[128,256]{1,0:T(8,128)(2,1)} %cluster.1), channel_id=1, replica_groups=mesh['y'=8,'zh'=4,'x'=4,'zl'=4,'core'=2] {'zh'}, dimensions={0}, use_global_device_ids=true | all-gather | bytes 327680 | tf_op jit(solution)/shard_map/all_gather | solution.py:151
  31.3 6.7 %collective-permute-start.4 = (bf16[512,256]{1,0:T(8,128)(2,1)S(1)}, bf16[512,256]{1,0:T(8,128)(2,1)S(1)}, u32[]{:S(2)}, u32[]{:S(2)}) collective-permute-start(bf16[512,256]{1,0:T(8,128)(2,1)S(1)} %all_gather.3.refs_1_), channel_id=1, source_target_pairs={{0,896},{128,0},{256,128},{384,256},{512,384},{640,512},{768,640},... | collective-permute-start | bytes 786440 | tf_op jit(solution)/shard_map/ppermute | solution.py:144
  38.0 1.9 collective-permute-start
  39.9 2.4 %collective-permute-done.4.refs_9_ = bf16[512,256]{1,0:T(8,128)(2,1)S(1)} collective-permute-done((bf16[512,256]{1,0:T(8,128)(2,1)S(1)}, bf16[512,256]{1,0:T(8,128)(2,1)S(1)}, u32[]{:S(2)}, u32[]{:S(2)}) %collective-permute-start.4) | collective-permute-done | bytes 262176 | tf_op jit(solution)/shard_map/ppermute | solution.py:144
  42.4 5.3 %collective-permute-start.5 = (bf16[512,256]{1,0:T(8,128)(2,1)S(1)}, bf16[512,256]{1,0:T(8,128)(2,1)S(1)}, u32[]{:S(2)}, u32[]{:S(2)}) collective-permute-start(bf16[512,256]{1,0:T(8,128)(2,1)S(1)} %collective-permute-done.4.refs_9_), channel_id=1, source_target_pairs={{0,896},{128,0},{256,128},{384,256},{512,384},{640,512},{768,640},... | collective-permute-start | bytes 786440 | tf_op jit(solution)/shard_map/ppermute | solution.py:144
  47.7 0.0 collective-permute-done.refs_2_
  47.7 1.9 collective-permute-start.1
  49.6 1.4 collective-permute-done.5.refs_8_
  51.0 5.5 %collective-permute-start.6 = (bf16[512,256]{1,0:T(8,128)(2,1)S(1)}, bf16[512,256]{1,0:T(8,128)(2,1)S(1)}, u32[]{:S(2)}, u32[]{:S(2)}) collective-permute-start(bf16[512,256]{1,0:T(8,128)(2,1)S(1)} %collective-permute-done.5.refs_8_), channel_id=1, source_target_pairs={{0,896},{128,0},{256,128},{384,256},{512,384},{640,512},{768,640},... | collective-permute-start | bytes 786440 | tf_op jit(solution)/shard_map/ppermute | solution.py:144
  56.4 0.0 collective-permute-done.1.refs_3_
  56.4 1.9 collective-permute-start.2
  58.4 1.4 collective-permute-done.6.refs_7_
  59.7 5.0 %collective-permute-start.7 = (bf16[256,256]{1,0:T(8,128)(2,1)S(1)}, bf16[256,256]{1,0:T(8,128)(2,1)S(1)}, u32[]{:S(2)}, u32[]{:S(2)}) collective-permute-start(bf16[256,256]{1,0:T(8,128)(2,1)S(1)} %slice.29), channel_id=1, source_target_pairs={{0,896},{128,0},{256,128},{384,256},{512,384},{640,512},{768,640},... | collective-permute-start | bytes 393224 | tf_op jit(solution)/shard_map/ppermute | solution.py:145
  64.8 0.0 collective-permute-done.2.refs_4_
  64.8 1.9 collective-permute-start.3
  67.4 0.0 collective-permute-done.7.refs_6_
  67.4 4.3 %collective-permute-done.3.refs_5_ = bf16[256,256]{1,0:T(8,128)(2,1)S(1)} collective-permute-done((bf16[256,256]{1,0:T(8,128)(2,1)S(1)}, bf16[256,256]{1,0:T(8,128)(2,1)S(1)}, u32[]{:S(2)}, u32[]{:S(2)}) %collective-permute-start.3) | collective-permute-done | bytes 131104 | tf_op jit(solution)/shard_map/ppermute | solution.py:145
  71.7 0.0 copy-start
  71.7 1.9 copy-done
  73.6 0.0 copy-start.5
  73.6 0.7 copy-done.5
  74.3 5.9 %tile_sums.1 = bf16[32,128,256]{2,1,0:T(8,128)(2,1)S(1)} custom-call(s32[1]{0:T(128)} %bitcast.me, s32[1,96]{1,0:T(1,128)S(1)} %copy-done.5, s32[1]{0:T(128)S(6)} %copy.11.count, bf16[96,128,128]{2,1,0:T(8,128)(2,1)S(1)} %bitcast.9, bf16[512,256]{1,0:T(8,128)(2,1)S(1)} %all_gather.3.refs_1_, bf16[512,256]{1,0:T(8,128)(2,1)S(1)} %collective-permute-done.refs_2_, ...), custom_call_target="tpu_custom_call" | custom-call | flops 805306368 | bytes 8388608 | tf_op jit(solution)/shard_map/tile_sums/pallas_call | solution.py:86
  80.1 7.9 %all_to_all.28 = bf16[32,128,256]{2,1,0:T(8,128)(2,1)S(1)} all-to-all(bf16[32,128,256]{2,1,0:T(8,128)(2,1)S(1)} %tile_sums.1), channel_id=1, replica_groups=mesh['y'=8,'zh'=4,'x'=4,'zl'=4,'core'=2] {'core'}, dimensions={0} | all-to-all | bytes 4194304 | tf_op jit(solution)/shard_map/all_to_all | solution.py:155
  88.0 0.0 copy-start.1
  88.0 0.0 copy-start.2
  88.0 0.0 copy-start.3
  88.0 0.0 copy-start.4
  88.0 0.3 add_convert_fusion
  88.4 38.8 %all_to_all.29.parts = bf16[16,128,256]{2,1,0:T(8,128)(2,1)S(1)} all-to-all(bf16[16,128,256]{2,1,0:T(8,128)(2,1)S(1)} %add_convert_fusion), channel_id=1, replica_groups=mesh['y'=8,'zh'=4,'x'=4,'zl'=4,'core'=2] {'x','zl'}, dimensions={0} | all-to-all | bytes 2097152 | tf_op jit(solution)/shard_map/all_to_all | solution.py:158
  127.1 0.0 copy-done.1
  127.1 0.0 copy-done.2
  127.1 0.0 copy-done.3
  127.1 0.0 copy-done.4
  127.2 1.1 finish.1
  128.2 18.8 %all_to_all.30 = f32[32,8,384]{2,1,0:T(8,128)S(1)} all-to-all(f32[32,8,384]{2,1,0:T(8,128)S(1)} %bitcast.10), channel_id=1, replica_groups=mesh['y'=8,'zh'=4,'x'=4,'zl'=4,'core'=2] {'x','zl','core'}, dimensions={0} | all-to-all | bytes 786432 | tf_op jit(solution)/shard_map/all_to_all | solution.py:160
  147.0 20.4 %psum.14 = f32[8,384]{1,0:T(8,128)S(1)} all-reduce(f32[8,384]{1,0:T(8,128)S(1)} %reduce_sum.9), channel_id=1, replica_groups=mesh['y'=8,'zh'=4,'x'=4,'zl'=4,'core'=2] {'y'}, use_global_device_ids=true, to_apply=%region_1.0 | all-reduce | flops 3072 | bytes 24576 | tf_op jit(solution)/shard_map/psum | solution.py:161
  167.4 20.3 %psum.15 = f32[8,384]{1,0:T(8,128)S(1)} all-reduce(f32[8,384]{1,0:T(8,128)S(1)} %psum.14), channel_id=1, replica_groups=mesh['y'=8,'zh'=4,'x'=4,'zl'=4,'core'=2] {'zh'}, use_global_device_ids=true, to_apply=%region_2.0 | all-reduce | flops 3072 | bytes 24576 | tf_op jit(solution)/shard_map/psum | solution.py:161
  187.8 27.8 %all_to_all.31 = f32[32,8,384]{2,1,0:T(8,128)S(1)} all-to-all(f32[32,8,384]{2,1,0:T(8,128)S(1)} %tile.2), channel_id=1, replica_groups=mesh['y'=8,'zh'=4,'x'=4,'zl'=4,'core'=2] {'x','zl','core'}, dimensions={0} | all-to-all | bytes 786432 | tf_op jit(solution)/shard_map/all_to_all | solution.py:162
  215.6 0.7 slice.32
  216.3 0.6 pad_maximum_fusion
  (5 shorter events, 0.1 us)
Async XLA Ops:
  31.3 11.0 %collective-permute-start.4 = (bf16[512,256]{1,0:T(8,128)(2,1)S(1)}, bf16[512,256]{1,0:T(8,128)(2,1)S(1)}, u32[]{:S(2)}, u32[]{:S(2)}) collective-permute-start(bf16[512,256]{1,0:T(8,128)(2,1)S(1)} %all_gather.3.refs_1_), channel_id=1, source_target_pairs={{0,896},{128,0},{256,128},{384,256},{512,384},{640,512},{768,640},... | collective-permute-start | bytes 786440 | tf_op jit(solution)/shard_map/ppermute | solution.py:144
  38.0 9.7 %collective-permute-start = (bf16[512,256]{1,0:T(8,128)(2,1)S(1)}, bf16[512,256]{1,0:T(8,128)(2,1)S(1)}, u32[]{:S(2)}, u32[]{:S(2)}) collective-permute-start(bf16[512,256]{1,0:T(8,128)(2,1)S(1)} %all_gather.3.refs_1_), channel_id=1, source_target_pairs={{0,128},{128,256},{256,384},{384,512},{512,640},{640,768},{768,896... | collective-permute-start | bytes 786440 | tf_op jit(solution)/shard_map/ppermute | solution.py:143
  42.4 8.6 %collective-permute-start.5 = (bf16[512,256]{1,0:T(8,128)(2,1)S(1)}, bf16[512,256]{1,0:T(8,128)(2,1)S(1)}, u32[]{:S(2)}, u32[]{:S(2)}) collective-permute-start(bf16[512,256]{1,0:T(8,128)(2,1)S(1)} %collective-permute-done.4.refs_9_), channel_id=1, source_target_pairs={{0,896},{128,0},{256,128},{384,256},{512,384},{640,512},{768,640},... | collective-permute-start | bytes 786440 | tf_op jit(solution)/shard_map/ppermute | solution.py:144
  47.7 8.7 %collective-permute-start.1 = (bf16[512,256]{1,0:T(8,128)(2,1)S(1)}, bf16[512,256]{1,0:T(8,128)(2,1)S(1)}, u32[]{:S(2)}, u32[]{:S(2)}) collective-permute-start(bf16[512,256]{1,0:T(8,128)(2,1)S(1)} %collective-permute-done.refs_2_), channel_id=1, source_target_pairs={{0,128},{128,256},{256,384},{384,512},{512,640},{640,768},{768,896... | collective-permute-start | bytes 786440 | tf_op jit(solution)/shard_map/ppermute | solution.py:143
  51.0 8.8 %collective-permute-start.6 = (bf16[512,256]{1,0:T(8,128)(2,1)S(1)}, bf16[512,256]{1,0:T(8,128)(2,1)S(1)}, u32[]{:S(2)}, u32[]{:S(2)}) collective-permute-start(bf16[512,256]{1,0:T(8,128)(2,1)S(1)} %collective-permute-done.5.refs_8_), channel_id=1, source_target_pairs={{0,896},{128,0},{256,128},{384,256},{512,384},{640,512},{768,640},... | collective-permute-start | bytes 786440 | tf_op jit(solution)/shard_map/ppermute | solution.py:144
  56.4 8.3 %collective-permute-start.2 = (bf16[512,256]{1,0:T(8,128)(2,1)S(1)}, bf16[512,256]{1,0:T(8,128)(2,1)S(1)}, u32[]{:S(2)}, u32[]{:S(2)}) collective-permute-start(bf16[512,256]{1,0:T(8,128)(2,1)S(1)} %collective-permute-done.1.refs_3_), channel_id=1, source_target_pairs={{0,128},{128,256},{256,384},{384,512},{512,640},{640,768},{768,896... | collective-permute-start | bytes 786440 | tf_op jit(solution)/shard_map/ppermute | solution.py:143
  59.7 7.6 %collective-permute-start.7 = (bf16[256,256]{1,0:T(8,128)(2,1)S(1)}, bf16[256,256]{1,0:T(8,128)(2,1)S(1)}, u32[]{:S(2)}, u32[]{:S(2)}) collective-permute-start(bf16[256,256]{1,0:T(8,128)(2,1)S(1)} %slice.29), channel_id=1, source_target_pairs={{0,896},{128,0},{256,128},{384,256},{512,384},{640,512},{768,640},... | collective-permute-start | bytes 393224 | tf_op jit(solution)/shard_map/ppermute | solution.py:145
  64.8 6.9 %collective-permute-start.3 = (bf16[256,256]{1,0:T(8,128)(2,1)S(1)}, bf16[256,256]{1,0:T(8,128)(2,1)S(1)}, u32[]{:S(2)}, u32[]{:S(2)}) collective-permute-start(bf16[256,256]{1,0:T(8,128)(2,1)S(1)} %slice.28), channel_id=1, source_target_pairs={{0,128},{128,256},{256,384},{384,512},{512,640},{640,768},{768,896... | collective-permute-start | bytes 393224 | tf_op jit(solution)/shard_map/ppermute | solution.py:145
  71.7 1.9 copy-start
  73.6 0.7 copy-start.5
  88.0 39.1 %copy-start.1 = (bf16[256,256]{1,0:T(8,128)(2,1)S(1)}, bf16[256,256]{1,0:T(8,128)(2,1)}, u32[]{:S(2)}) copy-start(bf16[256,256]{1,0:T(8,128)(2,1)} %weight.1) | copy-start | bytes 393220
  88.0 39.1 %copy-start.2 = (bf16[128,256]{1,0:T(8,128)(2,1)S(1)}, bf16[128,256]{1,0:T(8,128)(2,1)}, u32[]{:S(2)}) copy-start(bf16[128,256]{1,0:T(8,128)(2,1)} %out_grad.1) | copy-start | bytes 196612
  88.0 39.1 %copy-start.3 = (s32[1,128]{1,0:T(1,128)S(1)}, s32[1,128]{1,0:T(1,128)}, u32[]{:S(2)}) copy-start(s32[1,128]{1,0:T(1,128)} %order.3) | copy-start | bytes 1540
  88.0 39.1 %copy-start.4 = (f32[256]{0:T(256)S(1)}, f32[256]{0:T(256)}, u32[]{:S(2)}) copy-start(f32[256]{0:T(256)} %param.14) | copy-start | bytes 3076

commit v2 on v1

--- a/solution.py
+++ b/solution.py
@@ -6,7 +6,6 @@
 from jax.sharding import Mesh, PartitionSpec as P
 
 AXES = ("y", "zh", "x", "zl", "core")
-COL = ("x", "zl", "core")
 T = 128
 F = 256
 TILES = 96
@@ -33,9 +32,9 @@
     )(order, feats)
 
 
-def tiles_body(me, index, count, *refs):
-    tiles, pieces, out = refs[0], refs[1:10], refs[10]
-    src, vals, acc, piece_sem, tile_sem = refs[11:]
+def tiles_body(spot, index, count, *refs):
+    tiles, pieces, mine, other = refs[0], refs[1:10], refs[10], refs[11]
+    src, vals, acc, piece_sem, tile_sem = refs[12:]
     copies = []
     row = 0
     for i, piece in enumerate(pieces):
@@ -56,7 +55,7 @@
     for copy in copies:
         copy.wait()
     used = count[0]
-    here = me[0]
+    here, core = spot[0], spot[1]
     for c, load in enumerate(loads):
         load.wait()
 
@@ -75,19 +74,23 @@
                     start = pl.multiple_of(slot * T, T)
                     acc[to] += jnp.dot(vals[k], src[pl.ds(start, T), :], preferred_element_type=F32)
 
-    @pl.loop(0, GRID)
+    @pl.loop(0, GRID // 2)
     def _(r):
-        out[(r & 1) * (GRID // 2) + (r >> 1)] = acc[r].astype(out.dtype)
-
-
-def tile_sums(me, index, count, tiles, pieces):
+        other[r] = acc[2 * r + 1 - core].astype(other.dtype)
+        mine[r] = acc[2 * r + core]
+
+
+def tile_sums(spot, index, count, tiles, pieces):
     smem = pl.BlockSpec(memory_space=pltpu.SMEM)
     hbm = pl.BlockSpec(memory_space=pl.ANY)
     return pl.pallas_call(
         tiles_body,
-        out_shape=jax.ShapeDtypeStruct((GRID, T, F), BF),
-        in_specs=[smem] * 3 + [hbm] * (1 + len(pieces)),
-        out_specs=pl.BlockSpec(memory_space=pltpu.VMEM),
+        out_shape=(
+            jax.ShapeDtypeStruct((GRID // 2, T, F), F32),
+            jax.ShapeDtypeStruct((GRID // 2, T, F), BF),
+        ),
+        in_specs=[smem] * 3 + [pl.BlockSpec(memory_space=pltpu.HBM)] + [hbm] * len(pieces),
+        out_specs=[pl.BlockSpec(memory_space=pltpu.VMEM)] * 2,
         scratch_shapes=[
             pltpu.VMEM((GRID * T, F), BF),
             pltpu.VMEM((TILES, T, T), BF),
@@ -95,15 +98,15 @@
             pltpu.SemaphoreType.DMA((len(pieces),)),
             pltpu.SemaphoreType.DMA((TILES // CHUNK,)),
         ],
-        compiler_params=pltpu.CompilerParams(vmem_limit_bytes=40 * 2**20),
+        compiler_params=pltpu.CompilerParams(vmem_limit_bytes=50 * 2**20),
         cost_estimate=pl.CostEstimate(
             flops=2 * TILES * T * T * F, bytes_accessed=8 * 2**20, transcendentals=0
         ),
         name="tile_sums",
-    )(me, index, count, tiles, *pieces)
-
-
-def finish_body(parts, order, weight, bias, out_grad, act_out, grads):
+    )(spot, index, count, tiles, *pieces)
+
+
+def finish_body(core, parts, order, weight, bias, out_grad, act_out, mine, other):
     total = parts[0].astype(F32)
     for i in range(1, parts.shape[0]):
         total += parts[i].astype(F32)
@@ -116,22 +119,64 @@
     act_out[...] = jnp.dot(hot, act, preferred_element_type=F32).astype(BF)
     cot = lax.dot_general(hot, out_grad[...], (((0,), (0,)), ((), ())), preferred_element_type=F32)
     grad = cot * sig * (1.0 + pre * (1.0 - sig))
-    grads[:, :F] = lax.dot_general(
+    wgrad = lax.dot_general(
         agg, grad.astype(BF), (((0,), (0,)), ((), ())), preferred_element_type=F32
     )
     sums = jnp.sum(grad, axis=0, keepdims=True)
-    grads[:, F:] = jnp.zeros((F, T), F32)
-    grads[0:1, F:] = sums[:, :T]
-    grads[8:9, F:] = sums[:, T:]
-
-
-def finish(parts, order, weight, bias, out_grad):
+    first = core[0] == 0
+
+    def halves(lead, low, high):
+        return (jnp.where(lead, low, high), jnp.where(lead, high, low))
+
+    own, away = halves(first, wgrad[:T], wgrad[T:])
+    own_sum, away_sum = halves(first, sums[:, :T], sums[:, T:])
+    for out, half, tail in ((mine, own, own_sum), (other, away, away_sum)):
+        out[:, 8:, :] = jnp.zeros((GRID, 8, T), F32)
+        out[0, 8:9, :] = tail
+        for i in range(T // 8):
+            for h in range(2):
+                out[2 * i + h, :8, :] = half[8 * i : 8 * i + 8, T * h : T * h + T]
+
+
+def finish(core, parts, order, weight, bias, out_grad):
+    smem = pl.BlockSpec(memory_space=pltpu.SMEM)
+    vmem = pl.BlockSpec(memory_space=pltpu.VMEM)
     return pl.pallas_call(
         finish_body,
-        out_shape=(jax.ShapeDtypeStruct((T, F), BF), jax.ShapeDtypeStruct((F, F + T), F32)),
+        out_shape=(
+            jax.ShapeDtypeStruct((T, F), BF),
+            jax.ShapeDtypeStruct((GRID, 16, T), F32),
+            jax.ShapeDtypeStruct((GRID, 16, T), F32),
+        ),
+        in_specs=[smem] + [vmem] * 5,
+        out_specs=[vmem] * 3,
         compiler_params=pltpu.CompilerParams(vmem_limit_bytes=40 * 2**20),
         name="finish",
-    )(parts, order, weight, bias, out_grad)
+    )(core, parts, order, weight, bias, out_grad)
+
+
+def unpack_body(core, mine, other, wgrad, bgrad):
+    first = core[0] == 0
+    for c in range(2):
+        pick = first if c == 0 else jnp.logical_not(first)
+        for i in range(T // 8):
+            for h in range(2):
+                wgrad[T * c + 8 * i : T * c + 8 * i + 8, T * h : T * h + T] = jnp.where(
+                    pick, mine[2 * i + h, :8, :], other[2 * i + h, :8, :]
+                )
+        bgrad[:, T * c : T * c + T] = jnp.where(pick, mine[0, 8:9, :], other[0, 8:9, :])
+
+
+def unpack(core, mine, other):
+    smem = pl.BlockSpec(memory_space=pltpu.SMEM)
+    vmem = pl.BlockSpec(memory_space=pltpu.VMEM)
+    return pl.pallas_call(
+        unpack_body,
+        out_shape=(jax.ShapeDtypeStruct((F, F), F32), jax.ShapeDtypeStruct((1, F), F32)),
+        in_specs=[smem, vmem, vmem],
+        out_specs=[vmem] * 2,
+        name="unpack",
+    )(core, mine, other)
 
 
 def ring_gather(own):
@@ -146,22 +191,33 @@
     return below + far + above[:0:-1]
 
 
+def spread(block, axes, copies):
+    repeated = jnp.broadcast_to(block[None], (copies, *block.shape))
+    return lax.all_to_all(repeated, axes, 0, 0, tiled=True)
+
+
 def local(features, node_order, tile_index, tile_count, tile_values, weight, out_bias, out_grad):
+    swap = [(0, 1), (1, 0)]
+    row_at = lax.axis_index("y").astype(jnp.int32)
+    core = lax.axis_index("core").astype(jnp.int32)
     clustered = cluster(node_order, features)
     near = lax.all_gather(clustered, "zh", axis=0, tiled=True)
     pieces = ring_gather(near)
-    me = lax.axis_index("y").astype(jnp.int32).reshape(1)
-    sums = tile_sums(me, tile_index, tile_count, tile_values[0], pieces)
-    swapped = lax.all_to_all(sums, "core", 0, 0, tiled=True)
-    half = GRID // 2
-    paired = (swapped[:half].astype(F32) + swapped[half:].astype(F32)).astype(BF)
+    mine, other = tile_sums(
+        jnp.stack([row_at, core]), tile_index, tile_count, tile_values[0], pieces
+    )
+    paired = (mine + lax.ppermute(other, "core", swap).astype(F32)).astype(BF)
     parts = lax.all_to_all(paired, ("x", "zl"), 0, 0, tiled=True)
-    activated, grads = finish(parts, node_order, weight, out_bias.reshape(1, F), out_grad)
-    mine = lax.all_to_all(grads, COL, 0, 0, tiled=True).reshape(GRID, 8, F + T).sum(axis=0)
-    mine = lax.psum(lax.psum(mine, "y"), "zh")
-    whole = lax.all_to_all(jnp.tile(mine, (GRID, 1)), COL, 0, 0, tiled=True)
-    bias_grad = jnp.concatenate([whole[0, F:], whole[8, F:]])
-    return activated, whole[:, :F], bias_grad
+    core = core.reshape(1)
+    activated, mine, other = finish(
+        core, parts, node_order, weight, out_bias.reshape(1, F), out_grad
+    )
+    half = mine + lax.ppermute(other, "core", swap)
+    block = lax.all_to_all(half, ("y", "x"), 0, 0, tiled=True).sum(axis=0)
+    block = spread(block, ("zh", "zl"), 16).sum(axis=0)
+    half = spread(block, ("y", "x"), GRID)
+    weight_grad, bias_grad = unpack(core, half, lax.ppermute(half, "core", swap))
+    return activated, weight_grad, bias_grad.reshape(F)
 
 
 def solution(mesh):

time: 218 us -> 193 us (0.89)
  blocking collectives: 163 us -> 116 us
  starting transfers between devices: 30.1 us -> 46.9 us
  waiting for transfers between devices: 9.49 us -> 14 us
    psum x2 -> x0, blocking collectives: 40.7 us -> none  [local(): mine = lax.psum(lax.psum(mine, 'y'), 'zh')]
    ppermute x0 -> x3, starting transfers between devices: none -> 16.8 us  [the longest x1 6.89 us: local(): lax.ppermute(half, 'core', swap)]
    all_to_all x3, blocking collectives: 54.5 us -> 49.2 us  [the longest x2 33 us: spread(): return lax.all_to_all(repeated, axes, 0, 0, tiled=True)]
    ppermute x0 -> x3, waiting for transfers between devices: none -> 4.54 us  [the longest x1 2.26 us: local(): paired = (mine + lax.ppermute(other, 'core', swap).astype(F32)).astype(BF)]
    pallas_call x1 -> x2, Pallas kernels: 5.87 us -> 7.62 us  [the longest x1 5.87 us: tile_sums(): pl.pallas_call(tiles_body, out_shape=(jax.ShapeDtypeStruct((GRID // 2, T,...]
  transfers between devices with their start and end apart: 8 -> 11, of which waited for: 4 -> 7; matrix products, arithmetic and copies ran while one was open for 0% -> 0% of each run, Pallas kernels for 0% -> 0%
where the time goes in v2:
time: 193 us; the launch traced here: 192 us
  blocking collectives  116 us (60%)
  starting transfers between devices  46.9 us (24%)
  waiting for transfers between devices  14 us (7%)
  Pallas kernels  10.4 us (5%)
  other arithmetic  2.12 us (1%)
    all_to_all x1, blocking collectives, local(): parts = lax.all_to_all(paired, ('x', 'zl'), 0, 0, tiled=True)  37.4 us
    all_to_all x2, blocking collectives, spread(): return lax.all_to_all(repeated, axes, 0, 0, tiled=True)  33 us
    all_gather x1, blocking collectives, local(): near = lax.all_gather(clustered, 'zh', axis=0, tiled=True)  29 us
    ppermute x3, starting transfers between devices, ring_gather(): above.append(lax.ppermute(above[-1], 'y', down))  17.4 us
    all_to_all x1, blocking collectives, local(): block = lax.all_to_all(half, ('y', 'x'), 0, 0, tiled=True).sum(axis=0)  16.2 us
    ppermute x1, starting transfers between devices, local(): lax.ppermute(half, 'core', swap)  6.89 us
    ppermute x1, starting transfers between devices, local(): paired = (mine + lax.ppermute(other, 'core', swap).astype(F32)).astype(BF)  6.31 us
    pallas_call x1, Pallas kernels, tile_sums(): pl.pallas_call(tiles_body, out_shape=(jax.ShapeDtypeStruct((GRID // 2, T,...  5.87 us
  transfers between devices with their start and end apart: 11, of which 7 were waited for; matrix products, arithmetic and copies ran while one was open for 0% of the time, Pallas kernels for 0%

profile of v2, /device:TPU:1, one launch (start us, length us, event | category | flops | bytes accessed | tf_op | source)
XLA Modules:
  0.0 191.9 jit_solution(3520367419779223158)
XLA Ops:
  0.6 1.7 cluster.1
  2.3 29.0 %all_gather.3.refs_1_ = bf16[512,256]{1,0:T(8,128)(2,1)S(1)} all-gather(bf16[128,256]{1,0:T(8,128)(2,1)} %cluster.1), channel_id=1, replica_groups=mesh['y'=8,'zh'=4,'x'=4,'zl'=4,'core'=2] {'zh'}, dimensions={0}, use_global_device_ids=true | all-gather | bytes 327680 | tf_op jit(solution)/shard_map/all_gather | solution.py:204
  31.3 6.7 %collective-permute-start.4 = (bf16[512,256]{1,0:T(8,128)(2,1)S(1)}, bf16[512,256]{1,0:T(8,128)(2,1)S(1)}, u32[]{:S(2)}, u32[]{:S(2)}) collective-permute-start(bf16[512,256]{1,0:T(8,128)(2,1)S(1)} %all_gather.3.refs_1_), channel_id=1, source_target_pairs={{0,896},{128,0},{256,128},{384,256},{512,384},{640,512},{768,640},... | collective-permute-start | bytes 786440 | tf_op jit(solution)/shard_map/ppermute | solution.py:189
  38.0 1.9 %collective-permute-start = (bf16[512,256]{1,0:T(8,128)(2,1)S(1)}, bf16[512,256]{1,0:T(8,128)(2,1)S(1)}, u32[]{:S(2)}, u32[]{:S(2)}) collective-permute-start(bf16[512,256]{1,0:T(8,128)(2,1)S(1)} %all_gather.3.refs_1_), channel_id=1, source_target_pairs={{0,128},{128,256},{256,384},{384,512},{512,640},{640,768},{768,896... | collective-permute-start | bytes 786440 | tf_op jit(solution)/shard_map/ppermute | solution.py:188
  39.9 2.4 %collective-permute-done.4.refs_9_ = bf16[512,256]{1,0:T(8,128)(2,1)S(1)} collective-permute-done((bf16[512,256]{1,0:T(8,128)(2,1)S(1)}, bf16[512,256]{1,0:T(8,128)(2,1)S(1)}, u32[]{:S(2)}, u32[]{:S(2)}) %collective-permute-start.4) | collective-permute-done | bytes 262176 | tf_op jit(solution)/shard_map/ppermute | solution.py:189
  42.4 5.3 %collective-permute-start.5 = (bf16[512,256]{1,0:T(8,128)(2,1)S(1)}, bf16[512,256]{1,0:T(8,128)(2,1)S(1)}, u32[]{:S(2)}, u32[]{:S(2)}) collective-permute-start(bf16[512,256]{1,0:T(8,128)(2,1)S(1)} %collective-permute-done.4.refs_9_), channel_id=1, source_target_pairs={{0,896},{128,0},{256,128},{384,256},{512,384},{640,512},{768,640},... | collective-permute-start | bytes 786440 | tf_op jit(solution)/shard_map/ppermute | solution.py:189
  47.7 0.0 collective-permute-done.refs_2_
  47.7 1.9 %collective-permute-start.1 = (bf16[512,256]{1,0:T(8,128)(2,1)S(1)}, bf16[512,256]{1,0:T(8,128)(2,1)S(1)}, u32[]{:S(2)}, u32[]{:S(2)}) collective-permute-start(bf16[512,256]{1,0:T(8,128)(2,1)S(1)} %collective-permute-done.refs_2_), channel_id=1, source_target_pairs={{0,128},{128,256},{256,384},{384,512},{512,640},{640,768},{768,896... | collective-permute-start | bytes 786440 | tf_op jit(solution)/shard_map/ppermute | solution.py:188
  49.6 1.4 collective-permute-done.5.refs_8_
  51.0 5.5 %collective-permute-start.6 = (bf16[512,256]{1,0:T(8,128)(2,1)S(1)}, bf16[512,256]{1,0:T(8,128)(2,1)S(1)}, u32[]{:S(2)}, u32[]{:S(2)}) collective-permute-start(bf16[512,256]{1,0:T(8,128)(2,1)S(1)} %collective-permute-done.5.refs_8_), channel_id=1, source_target_pairs={{0,896},{128,0},{256,128},{384,256},{512,384},{640,512},{768,640},... | collective-permute-start | bytes 786440 | tf_op jit(solution)/shard_map/ppermute | solution.py:189
  56.4 0.0 collective-permute-done.1.refs_3_
  56.4 1.9 %collective-permute-start.2 = (bf16[512,256]{1,0:T(8,128)(2,1)S(1)}, bf16[512,256]{1,0:T(8,128)(2,1)S(1)}, u32[]{:S(2)}, u32[]{:S(2)}) collective-permute-start(bf16[512,256]{1,0:T(8,128)(2,1)S(1)} %collective-permute-done.1.refs_3_), channel_id=1, source_target_pairs={{0,128},{128,256},{256,384},{384,512},{512,640},{640,768},{768,896... | collective-permute-start | bytes 786440 | tf_op jit(solution)/shard_map/ppermute | solution.py:188
  58.4 1.4 collective-permute-done.6.refs_7_
  59.7 5.0 %collective-permute-start.7 = (bf16[256,256]{1,0:T(8,128)(2,1)S(1)}, bf16[256,256]{1,0:T(8,128)(2,1)S(1)}, u32[]{:S(2)}, u32[]{:S(2)}) collective-permute-start(bf16[256,256]{1,0:T(8,128)(2,1)S(1)} %slice.9), channel_id=1, source_target_pairs={{0,896},{128,0},{256,128},{384,256},{512,384},{640,512},{768,640},... | collective-permute-start | bytes 393224 | tf_op jit(solution)/shard_map/ppermute | solution.py:190
  64.8 0.0 collective-permute-done.2.refs_4_
  64.8 1.9 %collective-permute-start.3 = (bf16[256,256]{1,0:T(8,128)(2,1)S(1)}, bf16[256,256]{1,0:T(8,128)(2,1)S(1)}, u32[]{:S(2)}, u32[]{:S(2)}) collective-permute-start(bf16[256,256]{1,0:T(8,128)(2,1)S(1)} %slice.8), channel_id=1, source_target_pairs={{0,128},{128,256},{256,384},{384,512},{512,640},{640,768},{768,896... | collective-permute-start | bytes 393224 | tf_op jit(solution)/shard_map/ppermute | solution.py:190
  67.4 0.1 pad_add_fusion.spot
  67.5 0.0 collective-permute-done.7.refs_6_
  67.5 4.3 %collective-permute-done.3.refs_5_ = bf16[256,256]{1,0:T(8,128)(2,1)S(1)} collective-permute-done((bf16[256,256]{1,0:T(8,128)(2,1)S(1)}, bf16[256,256]{1,0:T(8,128)(2,1)S(1)}, u32[]{:S(2)}, u32[]{:S(2)}) %collective-permute-start.3) | collective-permute-done | bytes 131104 | tf_op jit(solution)/shard_map/ppermute | solution.py:190
  71.7 0.0 copy-start.4
  71.7 0.7 copy-done.4
  72.4 5.9 %tile_sums.1 = (f32[16,128,256]{2,1,0:T(8,128)}, bf16[16,128,256]{2,1,0:T(8,128)(2,1)S(1)}) custom-call(s32[2]{0:T(128)S(1)} %pad_add_fusion.spot, s32[1,96]{1,0:T(1,128)S(1)} %copy-done.4, s32[1]{0:T(128)S(6)} %copy.11.count, bf16[96,128,128]{2,1,0:T(8,128)(2,1)} %bitcast.6, bf16[512,256]{1,0:T(8,128)(2,1)S(1)} %all_gather.3.refs_1_, ...), custom_call_target="tpu_custom_call" | custom-call | flops 805306368 | bytes 8388608 | tf_op jit(solution)/shard_map/tile_sums/pallas_call | solution.py:86
  78.3 6.3 %collective-permute-start.8 = (bf16[16,128,256]{2,1,0:T(8,128)(2,1)S(1)}, bf16[16,128,256]{2,1,0:T(8,128)(2,1)S(1)}, u32[]{:S(2)}, u32[]{:S(2)}) collective-permute-start(bf16[16,128,256]{2,1,0:T(8,128)(2,1)S(1)} %get-tuple-element.11), channel_id=1, source_target_pairs={{0,1},{1,0},{2,3},{3,2},{4,5},{5,4},{6,7},{7,6},{8,9},{9,8},{10,11... | collective-permute-start | bytes 3145736 | tf_op jit(solution)/shard_map/ppermute | solution.py:209
  84.6 2.3 %collective-permute-done.8 = bf16[16,128,256]{2,1,0:T(8,128)(2,1)S(1)} collective-permute-done((bf16[16,128,256]{2,1,0:T(8,128)(2,1)S(1)}, bf16[16,128,256]{2,1,0:T(8,128)(2,1)S(1)}, u32[]{:S(2)}, u32[]{:S(2)}) %collective-permute-start.8) | collective-permute-done | bytes 1048608 | tf_op jit(solution)/shard_map/ppermute | solution.py:209
  86.8 2.0 %add_convert_fusion = bf16[16,128,256]{2,1,0:T(8,128)(2,1)S(1)} fusion(f32[16,128,256]{2,1,0:T(8,128)} %get-tuple-element.10, bf16[16,128,256]{2,1,0:T(8,128)(2,1)S(1)} %collective-permute-done.8), kind=kLoop, calls=%fused_computation | loop fusion | flops 1572864 | bytes 4194304 | tf_op jit(solution)/shard_map/convert_element_type | solution.py:209
  88.8 0.0 copy-start
  88.8 0.0 copy-start.1
  88.8 0.0 copy-start.2
  88.8 0.0 copy-start.3
  88.8 37.4 %all_to_all.20.parts = bf16[16,128,256]{2,1,0:T(8,128)(2,1)S(1)} all-to-all(bf16[16,128,256]{2,1,0:T(8,128)(2,1)S(1)} %add_convert_fusion), channel_id=1, replica_groups=mesh['y'=8,'zh'=4,'x'=4,'zl'=4,'core'=2] {'x','zl'}, dimensions={0} | all-to-all | bytes 2097152 | tf_op jit(solution)/shard_map/all_to_all | solution.py:210
  126.3 0.0 copy-done
  126.3 0.0 copy-done.1
  126.3 0.0 copy-done.2
  126.3 0.0 copy-done.3
  126.3 1.1 finish.1
  127.3 3.6 %collective-permute-start.9 = (f32[32,16,128]{2,1,0:T(8,128)S(1)}, f32[32,16,128]{2,1,0:T(8,128)S(1)}, u32[]{:S(2)}, u32[]{:S(2)}) collective-permute-start(f32[32,16,128]{2,1,0:T(8,128)S(1)} %get-tuple-element.14), channel_id=1, source_target_pairs={{0,1},{1,0},{2,3},{3,2},{4,5},{5,4},{6,7},{7,6},{8,9},{9,8},{10,11... | collective-permute-start | bytes 786440 | tf_op jit(solution)/shard_map/ppermute | solution.py:215
  130.9 1.1 collective-permute-done.9
  132.1 16.2 %all_to_all.21 = f32[32,16,128]{2,1,0:T(8,128)S(1)} all-to-all(f32[32,16,128]{2,1,0:T(8,128)S(1)} %add.7), channel_id=1, replica_groups=mesh['y'=8,'zh'=4,'x'=4,'zl'=4,'core'=2] {'y','x'}, dimensions={0} | all-to-all | bytes 524288 | tf_op jit(solution)/shard_map/all_to_all | solution.py:216
  148.4 18.2 %all_to_all.22 = f32[16,16,128]{2,1,0:T(8,128)S(1)} all-to-all(f32[16,16,128]{2,1,0:T(8,128)S(1)} %broadcast_in_dim.4), channel_id=1, replica_groups=mesh['y'=8,'zh'=4,'x'=4,'zl'=4,'core'=2] {'zh','zl'}, dimensions={0} | all-to-all | bytes 262144 | tf_op jit(solution)/shard_map/all_to_all | solution.py:196
  166.6 14.8 %all_to_all.23.mine = f32[32,16,128]{2,1,0:T(8,128)S(1)} all-to-all(f32[32,16,128]{2,1,0:T(8,128)S(1)} %broadcast_in_dim.5), channel_id=1, replica_groups=mesh['y'=8,'zh'=4,'x'=4,'zl'=4,'core'=2] {'y','x'}, dimensions={0} | all-to-all | bytes 524288 | tf_op jit(solution)/shard_map/all_to_all | solution.py:196
  181.4 0.0 copy-start.5
  181.4 6.9 %collective-permute-start.10 = (f32[32,16,128]{2,1,0:T(8,128)S(1)}, f32[32,16,128]{2,1,0:T(8,128)S(1)}, u32[]{:S(2)}, u32[]{:S(2)}) collective-permute-start(f32[32,16,128]{2,1,0:T(8,128)S(1)} %all_to_all.23.mine), channel_id=1, source_target_pairs={{0,1},{1,0},{2,3},{3,2},{4,5},{5,4},{6,7},{7,6},{8,9},{9,8},{10,11... | collective-permute-start | bytes 786440 | tf_op jit(solution)/shard_map/ppermute | solution.py:219
  188.3 1.1 collective-permute-done.10.other
  189.5 0.0 copy-done.5
  189.5 0.0 copy-start.6
  189.5 0.7 copy-done.6
  190.2 1.8 unpack.1
  (7 shorter events, 0.1 us)
Async XLA Ops:
  31.3 11.0 %collective-permute-start.4 = (bf16[512,256]{1,0:T(8,128)(2,1)S(1)}, bf16[512,256]{1,0:T(8,128)(2,1)S(1)}, u32[]{:S(2)}, u32[]{:S(2)}) collective-permute-start(bf16[512,256]{1,0:T(8,128)(2,1)S(1)} %all_gather.3.refs_1_), channel_id=1, source_target_pairs={{0,896},{128,0},{256,128},{384,256},{512,384},{640,512},{768,640},... | collective-permute-start | bytes 786440 | tf_op jit(solution)/shard_map/ppermute | solution.py:189
  38.0 9.7 %collective-permute-start = (bf16[512,256]{1,0:T(8,128)(2,1)S(1)}, bf16[512,256]{1,0:T(8,128)(2,1)S(1)}, u32[]{:S(2)}, u32[]{:S(2)}) collective-permute-start(bf16[512,256]{1,0:T(8,128)(2,1)S(1)} %all_gather.3.refs_1_), channel_id=1, source_target_pairs={{0,128},{128,256},{256,384},{384,512},{512,640},{640,768},{768,896... | collective-permute-start | bytes 786440 | tf_op jit(solution)/shard_map/ppermute | solution.py:188
  42.4 8.6 %collective-permute-start.5 = (bf16[512,256]{1,0:T(8,128)(2,1)S(1)}, bf16[512,256]{1,0:T(8,128)(2,1)S(1)}, u32[]{:S(2)}, u32[]{:S(2)}) collective-permute-start(bf16[512,256]{1,0:T(8,128)(2,1)S(1)} %collective-permute-done.4.refs_9_), channel_id=1, source_target_pairs={{0,896},{128,0},{256,128},{384,256},{512,384},{640,512},{768,640},... | collective-permute-start | bytes 786440 | tf_op jit(solution)/shard_map/ppermute | solution.py:189
  47.7 8.8 %collective-permute-start.1 = (bf16[512,256]{1,0:T(8,128)(2,1)S(1)}, bf16[512,256]{1,0:T(8,128)(2,1)S(1)}, u32[]{:S(2)}, u32[]{:S(2)}) collective-permute-start(bf16[512,256]{1,0:T(8,128)(2,1)S(1)} %collective-permute-done.refs_2_), channel_id=1, source_target_pairs={{0,128},{128,256},{256,384},{384,512},{512,640},{640,768},{768,896... | collective-permute-start | bytes 786440 | tf_op jit(solution)/shard_map/ppermute | solution.py:188
  51.0 8.8 %collective-permute-start.6 = (bf16[512,256]{1,0:T(8,128)(2,1)S(1)}, bf16[512,256]{1,0:T(8,128)(2,1)S(1)}, u32[]{:S(2)}, u32[]{:S(2)}) collective-permute-start(bf16[512,256]{1,0:T(8,128)(2,1)S(1)} %collective-permute-done.5.refs_8_), channel_id=1, source_target_pairs={{0,896},{128,0},{256,128},{384,256},{512,384},{640,512},{768,640},... | collective-permute-start | bytes 786440 | tf_op jit(solution)/shard_map/ppermute | solution.py:189
  56.4 8.3 %collective-permute-start.2 = (bf16[512,256]{1,0:T(8,128)(2,1)S(1)}, bf16[512,256]{1,0:T(8,128)(2,1)S(1)}, u32[]{:S(2)}, u32[]{:S(2)}) collective-permute-start(bf16[512,256]{1,0:T(8,128)(2,1)S(1)} %collective-permute-done.1.refs_3_), channel_id=1, source_target_pairs={{0,128},{128,256},{256,384},{384,512},{512,640},{640,768},{768,896... | collective-permute-start | bytes 786440 | tf_op jit(solution)/shard_map/ppermute | solution.py:188
  59.7 7.7 %collective-permute-start.7 = (bf16[256,256]{1,0:T(8,128)(2,1)S(1)}, bf16[256,256]{1,0:T(8,128)(2,1)S(1)}, u32[]{:S(2)}, u32[]{:S(2)}) collective-permute-start(bf16[256,256]{1,0:T(8,128)(2,1)S(1)} %slice.9), channel_id=1, source_target_pairs={{0,896},{128,0},{256,128},{384,256},{512,384},{640,512},{768,640},... | collective-permute-start | bytes 393224 | tf_op jit(solution)/shard_map/ppermute | solution.py:190
  64.8 6.9 %collective-permute-start.3 = (bf16[256,256]{1,0:T(8,128)(2,1)S(1)}, bf16[256,256]{1,0:T(8,128)(2,1)S(1)}, u32[]{:S(2)}, u32[]{:S(2)}) collective-permute-start(bf16[256,256]{1,0:T(8,128)(2,1)S(1)} %slice.8), channel_id=1, source_target_pairs={{0,128},{128,256},{256,384},{384,512},{512,640},{640,768},{768,896... | collective-permute-start | bytes 393224 | tf_op jit(solution)/shard_map/ppermute | solution.py:190
  71.7 0.7 copy-start.4
  78.3 8.6 %collective-permute-start.8 = (bf16[16,128,256]{2,1,0:T(8,128)(2,1)S(1)}, bf16[16,128,256]{2,1,0:T(8,128)(2,1)S(1)}, u32[]{:S(2)}, u32[]{:S(2)}) collective-permute-start(bf16[16,128,256]{2,1,0:T(8,128)(2,1)S(1)} %get-tuple-element.11), channel_id=1, source_target_pairs={{0,1},{1,0},{2,3},{3,2},{4,5},{5,4},{6,7},{7,6},{8,9},{9,8},{10,11... | collective-permute-start | bytes 3145736 | tf_op jit(solution)/shard_map/ppermute | solution.py:209
  88.8 37.5 %copy-start = (bf16[256,256]{1,0:T(8,128)(2,1)S(1)}, bf16[256,256]{1,0:T(8,128)(2,1)}, u32[]{:S(2)}) copy-start(bf16[256,256]{1,0:T(8,128)(2,1)} %weight.1) | copy-start | bytes 393220
  88.8 37.5 %copy-start.1 = (bf16[128,256]{1,0:T(8,128)(2,1)S(1)}, bf16[128,256]{1,0:T(8,128)(2,1)}, u32[]{:S(2)}) copy-start(bf16[128,256]{1,0:T(8,128)(2,1)} %out_grad.1) | copy-start | bytes 196612
  88.8 37.4 %copy-start.2 = (s32[1,128]{1,0:T(1,128)S(1)}, s32[1,128]{1,0:T(1,128)}, u32[]{:S(2)}) copy-start(s32[1,128]{1,0:T(1,128)} %order.3) | copy-start | bytes 1540
  88.8 37.4 %copy-start.3 = (f32[256]{0:T(256)S(1)}, f32[256]{0:T(256)}, u32[]{:S(2)}) copy-start(f32[256]{0:T(256)} %param.14) | copy-start | bytes 3076
  127.3 4.7 %collective-permute-start.9 = (f32[32,16,128]{2,1,0:T(8,128)S(1)}, f32[32,16,128]{2,1,0:T(8,128)S(1)}, u32[]{:S(2)}, u32[]{:S(2)}) collective-permute-start(f32[32,16,128]{2,1,0:T(8,128)S(1)} %get-tuple-element.14), channel_id=1, source_target_pairs={{0,1},{1,0},{2,3},{3,2},{4,5},{5,4},{6,7},{7,6},{8,9},{9,8},{10,11... | collective-permute-start | bytes 786440 | tf_op jit(solution)/shard_map/ppermute | solution.py:215
  181.4 8.0 %copy-start.5 = (f32[32,16,128]{2,1,0:T(8,128)}, f32[32,16,128]{2,1,0:T(8,128)S(1)}, u32[]{:S(2)}) copy-start(f32[32,16,128]{2,1,0:T(8,128)S(1)} %all_to_all.23.mine) | copy-start | bytes 786436
  181.4 8.0 %collective-permute-start.10 = (f32[32,16,128]{2,1,0:T(8,128)S(1)}, f32[32,16,128]{2,1,0:T(8,128)S(1)}, u32[]{:S(2)}, u32[]{:S(2)}) collective-permute-start(f32[32,16,128]{2,1,0:T(8,128)S(1)} %all_to_all.23.mine), channel_id=1, source_target_pairs={{0,1},{1,0},{2,3},{3,2},{4,5},{5,4},{6,7},{7,6},{8,9},{9,8},{10,11... | collective-permute-start | bytes 786440 | tf_op jit(solution)/shard_map/ppermute | solution.py:219
  189.5 0.7 copy-start.6

commit v3 on v2

--- a/solution.py
+++ b/solution.py
@@ -32,7 +32,7 @@
     )(order, feats)
 
 
-def tiles_body(spot, index, count, *refs):
+def tiles_body(ints, *refs):
     tiles, pieces, mine, other = refs[0], refs[1:10], refs[10], refs[11]
     src, vals, acc, piece_sem, tile_sem = refs[12:]
     copies = []
@@ -54,8 +54,7 @@
 
     for copy in copies:
         copy.wait()
-    used = count[0]
-    here, core = spot[0], spot[1]
+    used, here, core = ints[TILES], ints[TILES + 1], ints[TILES + 2]
     for c, load in enumerate(loads):
         load.wait()
 
@@ -67,7 +66,7 @@
             def _():
                 for u in range(UNROLL):
                     k = first + u
-                    at = index[0, k]
+                    at = ints[k]
                     to = jnp.where(k < used, at // GRID, GRID)
                     col = at % GRID
                     slot = ((here - col // 4) & 7) * 4 + (col & 3)
@@ -80,7 +79,7 @@
         mine[r] = acc[2 * r + core]
 
 
-def tile_sums(spot, index, count, tiles, pieces):
+def tile_sums(ints, tiles, pieces):
     smem = pl.BlockSpec(memory_space=pltpu.SMEM)
     hbm = pl.BlockSpec(memory_space=pl.ANY)
     return pl.pallas_call(
@@ -89,7 +88,7 @@
             jax.ShapeDtypeStruct((GRID // 2, T, F), F32),
             jax.ShapeDtypeStruct((GRID // 2, T, F), BF),
         ),
-        in_specs=[smem] * 3 + [pl.BlockSpec(memory_space=pltpu.HBM)] + [hbm] * len(pieces),
+        in_specs=[smem] + [hbm] * (1 + len(pieces)),
         out_specs=[pl.BlockSpec(memory_space=pltpu.VMEM)] * 2,
         scratch_shapes=[
             pltpu.VMEM((GRID * T, F), BF),
@@ -98,12 +97,12 @@
             pltpu.SemaphoreType.DMA((len(pieces),)),
             pltpu.SemaphoreType.DMA((TILES // CHUNK,)),
         ],
-        compiler_params=pltpu.CompilerParams(vmem_limit_bytes=50 * 2**20),
+        compiler_params=pltpu.CompilerParams(vmem_limit_bytes=47 * 2**20),
         cost_estimate=pl.CostEstimate(
             flops=2 * TILES * T * T * F, bytes_accessed=8 * 2**20, transcendentals=0
         ),
         name="tile_sums",
-    )(spot, index, count, tiles, *pieces)
+    )(ints, tiles, *pieces)
 
 
 def finish_body(core, parts, order, weight, bias, out_grad, act_out, mine, other):
@@ -131,11 +130,10 @@
     own, away = halves(first, wgrad[:T], wgrad[T:])
     own_sum, away_sum = halves(first, sums[:, :T], sums[:, T:])
     for out, half, tail in ((mine, own, own_sum), (other, away, away_sum)):
-        out[:, 8:, :] = jnp.zeros((GRID, 8, T), F32)
-        out[0, 8:9, :] = tail
-        for i in range(T // 8):
-            for h in range(2):
-                out[2 * i + h, :8, :] = half[8 * i : 8 * i + 8, T * h : T * h + T]
+        out[:, 0, 4 * F :] = jnp.zeros((GRID, T), F32)
+        out[0:1, 0, 4 * F :] = tail
+        for q in range(4):
+            out[:, 0, q * F : (q + 1) * F] = half[q * GRID : (q + 1) * GRID]
 
 
 def finish(core, parts, order, weight, bias, out_grad):
@@ -145,8 +143,8 @@
         finish_body,
         out_shape=(
             jax.ShapeDtypeStruct((T, F), BF),
-            jax.ShapeDtypeStruct((GRID, 16, T), F32),
-            jax.ShapeDtypeStruct((GRID, 16, T), F32),
+            jax.ShapeDtypeStruct((GRID, 1, 4 * F + T), F32),
+            jax.ShapeDtypeStruct((GRID, 1, 4 * F + T), F32),
         ),
         in_specs=[smem] + [vmem] * 5,
         out_specs=[vmem] * 3,
@@ -159,12 +157,11 @@
     first = core[0] == 0
     for c in range(2):
         pick = first if c == 0 else jnp.logical_not(first)
-        for i in range(T // 8):
-            for h in range(2):
-                wgrad[T * c + 8 * i : T * c + 8 * i + 8, T * h : T * h + T] = jnp.where(
-                    pick, mine[2 * i + h, :8, :], other[2 * i + h, :8, :]
-                )
-        bgrad[:, T * c : T * c + T] = jnp.where(pick, mine[0, 8:9, :], other[0, 8:9, :])
+        for q in range(4):
+            at = T * c + GRID * q
+            lanes = slice(q * F, (q + 1) * F)
+            wgrad[at : at + GRID, :] = jnp.where(pick, mine[:, 0, lanes], other[:, 0, lanes])
+        bgrad[:, T * c : T * c + T] = jnp.where(pick, mine[0:1, 0, 4 * F :], other[0:1, 0, 4 * F :])
 
 
 def unpack(core, mine, other):
@@ -175,6 +172,7 @@
         out_shape=(jax.ShapeDtypeStruct((F, F), F32), jax.ShapeDtypeStruct((1, F), F32)),
         in_specs=[smem, vmem, vmem],
         out_specs=[vmem] * 2,
+        compiler_params=pltpu.CompilerParams(vmem_limit_bytes=16 * 2**20),
         name="unpack",
     )(core, mine, other)
 
@@ -203,9 +201,8 @@
     clustered = cluster(node_order, features)
     near = lax.all_gather(clustered, "zh", axis=0, tiled=True)
     pieces = ring_gather(near)
-    mine, other = tile_sums(
-        jnp.stack([row_at, core]), tile_index, tile_count, tile_values[0], pieces
-    )
+    ints = jnp.concatenate([tile_index[0], tile_count, jnp.stack([row_at, core])])
+    mine, other = tile_sums(ints, tile_values[0], pieces)
     paired = (mine + lax.ppermute(other, "core", swap).astype(F32)).astype(BF)
     parts = lax.all_to_all(paired, ("x", "zl"), 0, 0, tiled=True)
     core = core.reshape(1)

time: 193 us -> 184 us (0.953)
  Pallas kernels: 10.4 us -> 6.86 us
  blocking collectives: 116 us -> 113 us
    pallas_call x1, Pallas kernels: 5.87 us -> 3.29 us  [tile_sums(): pl.pallas_call(tiles_body, out_shape=(jax.ShapeDtypeStruct((GRID // 2, T,...]
where the time goes in v3:
time: 184 us
  blocking collectives  113 us (61%)
  starting transfers between devices  47.3 us (26%)
  waiting for transfers between devices  13 us (7%)
  Pallas kernels  6.86 us (4%)
    all_to_all x1, blocking collectives, local(): parts = lax.all_to_all(paired, ('x', 'zl'), 0, 0, tiled=True)  36.2 us
    all_to_all x2, blocking collectives, spread(): return lax.all_to_all(repeated, axes, 0, 0, tiled=True)  31.4 us
    all_gather x1, blocking collectives, local(): near = lax.all_gather(clustered, 'zh', axis=0, tiled=True)  29 us
    ppermute x3, starting transfers between devices, ring_gather(): above.append(lax.ppermute(above[-1], 'y', down))  17.4 us
    all_to_all x1, blocking collectives, local(): block = lax.all_to_all(half, ('y', 'x'), 0, 0, tiled=True).sum(axis=0)  16.7 us
    ppermute x1, starting transfers between devices, local(): paired = (mine + lax.ppermute(other, 'core', swap).astype(F32)).astype(BF)  7.54 us
    ppermute x1, starting transfers between devices, local(): lax.ppermute(half, 'core', swap)  6 us
    ppermute x3, starting transfers between devices, ring_gather(): below.append(lax.ppermute(below[-1], 'y', up))  5.76 us
  transfers between devices with their start and end apart: 11, of which 7 were waited for; matrix products, arithmetic and copies ran while one was open for 0% of the time, Pallas kernels for 0%

profile of v3, /device:TPU:1, one launch (start us, length us, event | category | flops | bytes accessed | tf_op | source)
XLA Modules:
  0.0 183.5 jit_solution(10789137532758433741)
XLA Ops:
  0.6 1.7 cluster.1
  2.3 29.0 %all_gather.3.refs_1_ = bf16[512,256]{1,0:T(8,128)(2,1)S(1)} all-gather(bf16[128,256]{1,0:T(8,128)(2,1)} %cluster.1), channel_id=1, replica_groups=mesh['y'=8,'zh'=4,'x'=4,'zl'=4,'core'=2] {'zh'}, dimensions={0}, use_global_device_ids=true | all-gather | bytes 327680 | tf_op jit(solution)/shard_map/all_gather | solution.py:202
  31.3 6.7 %collective-permute-start.4 = (bf16[512,256]{1,0:T(8,128)(2,1)S(1)}, bf16[512,256]{1,0:T(8,128)(2,1)S(1)}, u32[]{:S(2)}, u32[]{:S(2)}) collective-permute-start(bf16[512,256]{1,0:T(8,128)(2,1)S(1)} %all_gather.3.refs_1_), channel_id=1, source_target_pairs={{0,896},{128,0},{256,128},{384,256},{512,384},{640,512},{768,640},... | collective-permute-start | bytes 786440 | tf_op jit(solution)/shard_map/ppermute | solution.py:187
  38.0 1.9 %collective-permute-start = (bf16[512,256]{1,0:T(8,128)(2,1)S(1)}, bf16[512,256]{1,0:T(8,128)(2,1)S(1)}, u32[]{:S(2)}, u32[]{:S(2)}) collective-permute-start(bf16[512,256]{1,0:T(8,128)(2,1)S(1)} %all_gather.3.refs_1_), channel_id=1, source_target_pairs={{0,128},{128,256},{256,384},{384,512},{512,640},{640,768},{768,896... | collective-permute-start | bytes 786440 | tf_op jit(solution)/shard_map/ppermute | solution.py:186
  39.9 2.4 %collective-permute-done.4.refs_9_ = bf16[512,256]{1,0:T(8,128)(2,1)S(1)} collective-permute-done((bf16[512,256]{1,0:T(8,128)(2,1)S(1)}, bf16[512,256]{1,0:T(8,128)(2,1)S(1)}, u32[]{:S(2)}, u32[]{:S(2)}) %collective-permute-start.4) | collective-permute-done | bytes 262176 | tf_op jit(solution)/shard_map/ppermute | solution.py:187
  42.4 5.3 %collective-permute-start.5 = (bf16[512,256]{1,0:T(8,128)(2,1)S(1)}, bf16[512,256]{1,0:T(8,128)(2,1)S(1)}, u32[]{:S(2)}, u32[]{:S(2)}) collective-permute-start(bf16[512,256]{1,0:T(8,128)(2,1)S(1)} %collective-permute-done.4.refs_9_), channel_id=1, source_target_pairs={{0,896},{128,0},{256,128},{384,256},{512,384},{640,512},{768,640},... | collective-permute-start | bytes 786440 | tf_op jit(solution)/shard_map/ppermute | solution.py:187
  47.7 0.0 collective-permute-done.refs_2_
  47.7 1.9 %collective-permute-start.1 = (bf16[512,256]{1,0:T(8,128)(2,1)S(1)}, bf16[512,256]{1,0:T(8,128)(2,1)S(1)}, u32[]{:S(2)}, u32[]{:S(2)}) collective-permute-start(bf16[512,256]{1,0:T(8,128)(2,1)S(1)} %collective-permute-done.refs_2_), channel_id=1, source_target_pairs={{0,128},{128,256},{256,384},{384,512},{512,640},{640,768},{768,896... | collective-permute-start | bytes 786440 | tf_op jit(solution)/shard_map/ppermute | solution.py:186
  49.6 1.4 collective-permute-done.5.refs_8_
  51.0 5.5 %collective-permute-start.6 = (bf16[512,256]{1,0:T(8,128)(2,1)S(1)}, bf16[512,256]{1,0:T(8,128)(2,1)S(1)}, u32[]{:S(2)}, u32[]{:S(2)}) collective-permute-start(bf16[512,256]{1,0:T(8,128)(2,1)S(1)} %collective-permute-done.5.refs_8_), channel_id=1, source_target_pairs={{0,896},{128,0},{256,128},{384,256},{512,384},{640,512},{768,640},... | collective-permute-start | bytes 786440 | tf_op jit(solution)/shard_map/ppermute | solution.py:187
  56.4 0.0 collective-permute-done.1.refs_3_
  56.4 1.9 %collective-permute-start.2 = (bf16[512,256]{1,0:T(8,128)(2,1)S(1)}, bf16[512,256]{1,0:T(8,128)(2,1)S(1)}, u32[]{:S(2)}, u32[]{:S(2)}) collective-permute-start(bf16[512,256]{1,0:T(8,128)(2,1)S(1)} %collective-permute-done.1.refs_3_), channel_id=1, source_target_pairs={{0,128},{128,256},{256,384},{384,512},{512,640},{640,768},{768,896... | collective-permute-start | bytes 786440 | tf_op jit(solution)/shard_map/ppermute | solution.py:186
  58.4 1.4 collective-permute-done.6.refs_7_
  59.7 5.0 %collective-permute-start.7 = (bf16[256,256]{1,0:T(8,128)(2,1)S(1)}, bf16[256,256]{1,0:T(8,128)(2,1)S(1)}, u32[]{:S(2)}, u32[]{:S(2)}) collective-permute-start(bf16[256,256]{1,0:T(8,128)(2,1)S(1)} %slice.9), channel_id=1, source_target_pairs={{0,896},{128,0},{256,128},{384,256},{512,384},{640,512},{768,640},... | collective-permute-start | bytes 393224 | tf_op jit(solution)/shard_map/ppermute | solution.py:188
  64.8 0.0 collective-permute-done.2.refs_4_
  64.8 1.9 %collective-permute-start.3 = (bf16[256,256]{1,0:T(8,128)(2,1)S(1)}, bf16[256,256]{1,0:T(8,128)(2,1)S(1)}, u32[]{:S(2)}, u32[]{:S(2)}) collective-permute-start(bf16[256,256]{1,0:T(8,128)(2,1)S(1)} %slice.8), channel_id=1, source_target_pairs={{0,128},{128,256},{256,384},{384,512},{512,640},{640,768},{768,896... | collective-permute-start | bytes 393224 | tf_op jit(solution)/shard_map/ppermute | solution.py:188
  67.4 0.7 pad_add_fusion.ints
  68.1 0.0 collective-permute-done.7.refs_6_
  68.1 3.6 %collective-permute-done.3.refs_5_ = bf16[256,256]{1,0:T(8,128)(2,1)S(1)} collective-permute-done((bf16[256,256]{1,0:T(8,128)(2,1)S(1)}, bf16[256,256]{1,0:T(8,128)(2,1)S(1)}, u32[]{:S(2)}, u32[]{:S(2)}) %collective-permute-start.3) | collective-permute-done | bytes 131104 | tf_op jit(solution)/shard_map/ppermute | solution.py:188
  71.7 3.3 %tile_sums.1 = (f32[16,128,256]{2,1,0:T(8,128)S(1)}, bf16[16,128,256]{2,1,0:T(8,128)(2,1)S(1)}) custom-call(s32[99]{0:T(128)S(1)} %pad_add_fusion.ints, bf16[96,128,128]{2,1,0:T(8,128)(2,1)} %bitcast.7, bf16[512,256]{1,0:T(8,128)(2,1)S(1)} %all_gather.3.refs_1_, bf16[512,256]{1,0:T(8,128)(2,1)S(1)} %collective-permute-done.refs_2_, ...), custom_call_target="tpu_custom_call" | custom-call | flops 805306368 | bytes 8388608 | tf_op jit(solution)/shard_map/tile_sums/pallas_call | solution.py:85
  75.0 7.5 %collective-permute-start.8 = (bf16[16,128,256]{2,1,0:T(8,128)(2,1)S(1)}, bf16[16,128,256]{2,1,0:T(8,128)(2,1)S(1)}, u32[]{:S(2)}, u32[]{:S(2)}) collective-permute-start(bf16[16,128,256]{2,1,0:T(8,128)(2,1)S(1)} %get-tuple-element.11), channel_id=1, source_target_pairs={{0,1},{1,0},{2,3},{3,2},{4,5},{5,4},{6,7},{7,6},{8,9},{9,8},{10,11... | collective-permute-start | bytes 3145736 | tf_op jit(solution)/shard_map/ppermute | solution.py:206
  82.6 2.3 %collective-permute-done.8 = bf16[16,128,256]{2,1,0:T(8,128)(2,1)S(1)} collective-permute-done((bf16[16,128,256]{2,1,0:T(8,128)(2,1)S(1)}, bf16[16,128,256]{2,1,0:T(8,128)(2,1)S(1)}, u32[]{:S(2)}, u32[]{:S(2)}) %collective-permute-start.8) | collective-permute-done | bytes 1048608 | tf_op jit(solution)/shard_map/ppermute | solution.py:206
  84.8 0.4 add_convert_fusion
  85.2 0.0 copy-start
  85.2 0.0 copy-start.1
  85.2 0.0 copy-start.2
  85.2 0.0 copy-start.3
  85.3 36.2 %all_to_all.20.parts = bf16[16,128,256]{2,1,0:T(8,128)(2,1)S(1)} all-to-all(bf16[16,128,256]{2,1,0:T(8,128)(2,1)S(1)} %add_convert_fusion), channel_id=1, replica_groups=mesh['y'=8,'zh'=4,'x'=4,'zl'=4,'core'=2] {'x','zl'}, dimensions={0} | all-to-all | bytes 2097152 | tf_op jit(solution)/shard_map/all_to_all | solution.py:207
  121.4 0.0 copy-done
  121.4 0.0 copy-done.1
  121.4 0.0 copy-done.2
  121.4 0.0 copy-done.3
  121.4 1.1 finish.1
  122.5 3.6 %collective-permute-start.9 = (f32[32,1,1152]{2,1,0:T(1,128)S(1)}, f32[32,1,1152]{2,1,0:T(1,128)S(1)}, u32[]{:S(2)}, u32[]{:S(2)}) collective-permute-start(f32[32,1,1152]{2,1,0:T(1,128)S(1)} %get-tuple-element.14), channel_id=1, source_target_pairs={{0,1},{1,0},{2,3},{3,2},{4,5},{5,4},{6,7},{7,6},{8,9},{9,8},{10,11... | collective-permute-start | bytes 442376 | tf_op jit(solution)/shard_map/ppermute | solution.py:212
  126.1 1.0 collective-permute-done.9
  127.1 0.2 add.7
  127.3 16.7 %all_to_all.21 = f32[32,1,1152]{2,1,0:T(1,128)S(1)} all-to-all(f32[32,1,1152]{2,1,0:T(1,128)S(1)} %add.7), channel_id=1, replica_groups=mesh['y'=8,'zh'=4,'x'=4,'zl'=4,'core'=2] {'y','x'}, dimensions={0} | all-to-all | bytes 294912 | tf_op jit(solution)/shard_map/all_to_all | solution.py:213
  144.0 0.1 reduce_sum.18
  144.1 18.1 %all_to_all.22 = f32[16,1,1152]{2,1,0:T(1,128)S(1)} all-to-all(f32[16,1,1152]{2,1,0:T(1,128)S(1)} %broadcast_in_dim.4), channel_id=1, replica_groups=mesh['y'=8,'zh'=4,'x'=4,'zl'=4,'core'=2] {'zh','zl'}, dimensions={0} | all-to-all | bytes 147456 | tf_op jit(solution)/shard_map/all_to_all | solution.py:194
  162.2 0.1 reduce_sum.19
  162.3 0.1 broadcast_in_dim.5
  162.3 13.4 %all_to_all.23.mine = f32[32,1,1152]{2,1,0:T(1,128)S(1)} all-to-all(f32[32,1,1152]{2,1,0:T(1,128)S(1)} %broadcast_in_dim.5), channel_id=1, replica_groups=mesh['y'=8,'zh'=4,'x'=4,'zl'=4,'core'=2] {'y','x'}, dimensions={0} | all-to-all | bytes 294912 | tf_op jit(solution)/shard_map/all_to_all | solution.py:194
  175.7 6.0 %collective-permute-start.10 = (f32[32,1,1152]{2,1,0:T(1,128)S(1)}, f32[32,1,1152]{2,1,0:T(1,128)S(1)}, u32[]{:S(2)}, u32[]{:S(2)}) collective-permute-start(f32[32,1,1152]{2,1,0:T(1,128)S(1)} %all_to_all.23.mine), channel_id=1, source_target_pairs={{0,1},{1,0},{2,3},{3,2},{4,5},{5,4},{6,7},{7,6},{8,9},{9,8},{10,11... | collective-permute-start | bytes 442376 | tf_op jit(solution)/shard_map/ppermute | solution.py:216
  181.7 1.0 collective-permute-done.10.other
  182.7 0.8 unpack.1
  (3 shorter events, 0.1 us)
Async XLA Ops:
  31.3 11.0 %collective-permute-start.4 = (bf16[512,256]{1,0:T(8,128)(2,1)S(1)}, bf16[512,256]{1,0:T(8,128)(2,1)S(1)}, u32[]{:S(2)}, u32[]{:S(2)}) collective-permute-start(bf16[512,256]{1,0:T(8,128)(2,1)S(1)} %all_gather.3.refs_1_), channel_id=1, source_target_pairs={{0,896},{128,0},{256,128},{384,256},{512,384},{640,512},{768,640},... | collective-permute-start | bytes 786440 | tf_op jit(solution)/shard_map/ppermute | solution.py:187
  38.0 9.7 %collective-permute-start = (bf16[512,256]{1,0:T(8,128)(2,1)S(1)}, bf16[512,256]{1,0:T(8,128)(2,1)S(1)}, u32[]{:S(2)}, u32[]{:S(2)}) collective-permute-start(bf16[512,256]{1,0:T(8,128)(2,1)S(1)} %all_gather.3.refs_1_), channel_id=1, source_target_pairs={{0,128},{128,256},{256,384},{384,512},{512,640},{640,768},{768,896... | collective-permute-start | bytes 786440 | tf_op jit(solution)/shard_map/ppermute | solution.py:186
  42.4 8.6 %collective-permute-start.5 = (bf16[512,256]{1,0:T(8,128)(2,1)S(1)}, bf16[512,256]{1,0:T(8,128)(2,1)S(1)}, u32[]{:S(2)}, u32[]{:S(2)}) collective-permute-start(bf16[512,256]{1,0:T(8,128)(2,1)S(1)} %collective-permute-done.4.refs_9_), channel_id=1, source_target_pairs={{0,896},{128,0},{256,128},{384,256},{512,384},{640,512},{768,640},... | collective-permute-start | bytes 786440 | tf_op jit(solution)/shard_map/ppermute | solution.py:187
  47.7 8.8 %collective-permute-start.1 = (bf16[512,256]{1,0:T(8,128)(2,1)S(1)}, bf16[512,256]{1,0:T(8,128)(2,1)S(1)}, u32[]{:S(2)}, u32[]{:S(2)}) collective-permute-start(bf16[512,256]{1,0:T(8,128)(2,1)S(1)} %collective-permute-done.refs_2_), channel_id=1, source_target_pairs={{0,128},{128,256},{256,384},{384,512},{512,640},{640,768},{768,896... | collective-permute-start | bytes 786440 | tf_op jit(solution)/shard_map/ppermute | solution.py:186
  51.0 8.8 %collective-permute-start.6 = (bf16[512,256]{1,0:T(8,128)(2,1)S(1)}, bf16[512,256]{1,0:T(8,128)(2,1)S(1)}, u32[]{:S(2)}, u32[]{:S(2)}) collective-permute-start(bf16[512,256]{1,0:T(8,128)(2,1)S(1)} %collective-permute-done.5.refs_8_), channel_id=1, source_target_pairs={{0,896},{128,0},{256,128},{384,256},{512,384},{640,512},{768,640},... | collective-permute-start | bytes 786440 | tf_op jit(solution)/shard_map/ppermute | solution.py:187
  56.4 8.3 %collective-permute-start.2 = (bf16[512,256]{1,0:T(8,128)(2,1)S(1)}, bf16[512,256]{1,0:T(8,128)(2,1)S(1)}, u32[]{:S(2)}, u32[]{:S(2)}) collective-permute-start(bf16[512,256]{1,0:T(8,128)(2,1)S(1)} %collective-permute-done.1.refs_3_), channel_id=1, source_target_pairs={{0,128},{128,256},{256,384},{384,512},{512,640},{640,768},{768,896... | collective-permute-start | bytes 786440 | tf_op jit(solution)/shard_map/ppermute | solution.py:186
  59.7 8.4 %collective-permute-start.7 = (bf16[256,256]{1,0:T(8,128)(2,1)S(1)}, bf16[256,256]{1,0:T(8,128)(2,1)S(1)}, u32[]{:S(2)}, u32[]{:S(2)}) collective-permute-start(bf16[256,256]{1,0:T(8,128)(2,1)S(1)} %slice.9), channel_id=1, source_target_pairs={{0,896},{128,0},{256,128},{384,256},{512,384},{640,512},{768,640},... | collective-permute-start | bytes 393224 | tf_op jit(solution)/shard_map/ppermute | solution.py:188
  64.8 6.9 %collective-permute-start.3 = (bf16[256,256]{1,0:T(8,128)(2,1)S(1)}, bf16[256,256]{1,0:T(8,128)(2,1)S(1)}, u32[]{:S(2)}, u32[]{:S(2)}) collective-permute-start(bf16[256,256]{1,0:T(8,128)(2,1)S(1)} %slice.8), channel_id=1, source_target_pairs={{0,128},{128,256},{256,384},{384,512},{512,640},{640,768},{768,896... | collective-permute-start | bytes 393224 | tf_op jit(solution)/shard_map/ppermute | solution.py:188
  75.0 9.8 %collective-permute-start.8 = (bf16[16,128,256]{2,1,0:T(8,128)(2,1)S(1)}, bf16[16,128,256]{2,1,0:T(8,128)(2,1)S(1)}, u32[]{:S(2)}, u32[]{:S(2)}) collective-permute-start(bf16[16,128,256]{2,1,0:T(8,128)(2,1)S(1)} %get-tuple-element.11), channel_id=1, source_target_pairs={{0,1},{1,0},{2,3},{3,2},{4,5},{5,4},{6,7},{7,6},{8,9},{9,8},{10,11... | collective-permute-start | bytes 3145736 | tf_op jit(solution)/shard_map/ppermute | solution.py:206
  85.2 36.2 %copy-start = (bf16[256,256]{1,0:T(8,128)(2,1)S(1)}, bf16[256,256]{1,0:T(8,128)(2,1)}, u32[]{:S(2)}) copy-start(bf16[256,256]{1,0:T(8,128)(2,1)} %weight.1) | copy-start | bytes 393220
  85.2 36.2 %copy-start.1 = (bf16[128,256]{1,0:T(8,128)(2,1)S(1)}, bf16[128,256]{1,0:T(8,128)(2,1)}, u32[]{:S(2)}) copy-start(bf16[128,256]{1,0:T(8,128)(2,1)} %out_grad.1) | copy-start | bytes 196612
  85.2 36.2 %copy-start.2 = (s32[1,128]{1,0:T(1,128)S(1)}, s32[1,128]{1,0:T(1,128)}, u32[]{:S(2)}) copy-start(s32[1,128]{1,0:T(1,128)} %order.3) | copy-start | bytes 1540
  85.2 36.2 %copy-start.3 = (f32[256]{0:T(256)S(1)}, f32[256]{0:T(256)}, u32[]{:S(2)}) copy-start(f32[256]{0:T(256)} %param.14) | copy-start | bytes 3076
  122.5 4.6 %collective-permute-start.9 = (f32[32,1,1152]{2,1,0:T(1,128)S(1)}, f32[32,1,1152]{2,1,0:T(1,128)S(1)}, u32[]{:S(2)}, u32[]{:S(2)}) collective-permute-start(f32[32,1,1152]{2,1,0:T(1,128)S(1)} %get-tuple-element.14), channel_id=1, source_target_pairs={{0,1},{1,0},{2,3},{3,2},{4,5},{5,4},{6,7},{7,6},{8,9},{9,8},{10,11... | collective-permute-start | bytes 442376 | tf_op jit(solution)/shard_map/ppermute | solution.py:212
  175.7 7.0 %collective-permute-start.10 = (f32[32,1,1152]{2,1,0:T(1,128)S(1)}, f32[32,1,1152]{2,1,0:T(1,128)S(1)}, u32[]{:S(2)}, u32[]{:S(2)}) collective-permute-start(f32[32,1,1152]{2,1,0:T(1,128)S(1)} %all_to_all.23.mine), channel_id=1, source_target_pairs={{0,1},{1,0},{2,3},{3,2},{4,5},{5,4},{6,7},{7,6},{8,9},{9,8},{10,11... | collective-permute-start | bytes 442376 | tf_op jit(solution)/shard_map/ppermute | solution.py:216

commit v4 on v3

--- a/solution.py
+++ b/solution.py
@@ -10,8 +10,10 @@
 F = 256
 TILES = 96
 GRID = 32
-CHUNK = 16
 UNROLL = 8
+FAR_FROM, FAR_TO = 3, 6
+NEAR_ROWS = (0, 512, 1024, 3072, 3584)
+FAR_ROWS = (1536, 2048, 2304, 2560)
 BF = jnp.bfloat16
 F32 = jnp.float32
 
@@ -32,77 +34,125 @@
     )(order, feats)
 
 
-def tiles_body(ints, *refs):
-    tiles, pieces, mine, other = refs[0], refs[1:10], refs[10], refs[11]
-    src, vals, acc, piece_sem, tile_sem = refs[12:]
+def near_block(ints, k):
+    at = ints[k]
+    row, col = at // GRID, at % GRID
+    back = (ints[TILES + 1] - col // 4) & 7
+    start = pl.multiple_of((back * 4 + (col & 3)) * T, T)
+    to = ((row & 1) ^ ints[TILES + 2]) * (GRID // 2) + (row >> 1)
+    return jnp.logical_or(back < FAR_FROM, back >= FAR_TO), start, to
+
+
+def add_tiles(ints, listed, used, vals, src, acc):
+    @pl.loop(0, (used + UNROLL - 1) // UNROLL)
+    def _(g):
+        for u in range(UNROLL):
+            i = g * UNROLL + u
+            k = jnp.where(i < used, listed[i], 0)
+            _, start, to = near_block(ints, k)
+            to = jnp.where(i < used, to, GRID)
+            acc[to] += jnp.dot(vals[k], src[pl.ds(start, T), :], preferred_element_type=F32)
+
+
+def first_body(ints, *refs):
+    vals, pieces, acc, later = refs[0], refs[1:-5], refs[-5], refs[-4]
+    src, now, piece_sem = refs[-3:]
     copies = []
-    row = 0
-    for i, piece in enumerate(pieces):
-        rows = piece.shape[0]
-        copies.append(pltpu.make_async_copy(piece, src.at[pl.ds(row, rows)], piece_sem.at[i]))
-        row += rows
-    loads = [
-        pltpu.make_async_copy(tiles.at[pl.ds(c * CHUNK, CHUNK)], vals.at[pl.ds(c * CHUNK, CHUNK)], tile_sem.at[c])
-        for c in range(TILES // CHUNK)
-    ]
-    for copy in copies + loads:
+    for i, (piece, row) in enumerate(zip(pieces, NEAR_ROWS)):
+        copies.append(pltpu.make_async_copy(piece, src.at[pl.ds(row, piece.shape[0])], piece_sem.at[i]))
+    for copy in copies:
         copy.start()
 
     @pl.loop(0, GRID + 1)
     def _(r):
         acc[r] = jnp.zeros((T, F), F32)
 
+    def sort(k, counts):
+        near, _, _ = near_block(ints, k)
+        early, late = counts
+        now[early] = k
+        later[late] = k
+        step = near.astype(jnp.int32)
+        return early + step, late + 1 - step
+
+    early, late = lax.fori_loop(0, ints[TILES], sort, (jnp.int32(0), jnp.int32(0)))
+    later[TILES + 1] = late
     for copy in copies:
         copy.wait()
-    used, here, core = ints[TILES], ints[TILES + 1], ints[TILES + 2]
-    for c, load in enumerate(loads):
-        load.wait()
-
-        @pl.loop(0, CHUNK // UNROLL)
-        def _(g):
-            first = c * CHUNK + g * UNROLL
-
-            @pl.when(first < used)
-            def _():
-                for u in range(UNROLL):
-                    k = first + u
-                    at = ints[k]
-                    to = jnp.where(k < used, at // GRID, GRID)
-                    col = at % GRID
-                    slot = ((here - col // 4) & 7) * 4 + (col & 3)
-                    start = pl.multiple_of(slot * T, T)
-                    acc[to] += jnp.dot(vals[k], src[pl.ds(start, T), :], preferred_element_type=F32)
+    add_tiles(ints, now, early, vals, src, acc)
+
+
+def first_sums(ints, tiles, pieces):
+    smem = pl.BlockSpec(memory_space=pltpu.SMEM)
+    vmem = pl.BlockSpec(memory_space=pltpu.VMEM)
+    hbm = pl.BlockSpec(memory_space=pl.ANY)
+    return pl.pallas_call(
+        first_body,
+        out_shape=(
+            jax.ShapeDtypeStruct((GRID + 1, T, F), F32),
+            jax.ShapeDtypeStruct((T,), jnp.int32),
+        ),
+        in_specs=[smem, vmem] + [hbm] * len(pieces),
+        out_specs=[vmem, smem],
+        scratch_shapes=[
+            pltpu.VMEM((GRID * T, F), BF),
+            pltpu.SMEM((T,), jnp.int32),
+            pltpu.SemaphoreType.DMA((len(pieces),)),
+        ],
+        compiler_params=pltpu.CompilerParams(vmem_limit_bytes=24 * 2**20),
+        cost_estimate=pl.CostEstimate(
+            flops=2 * TILES * T * T * F, bytes_accessed=8 * 2**20, transcendentals=0
+        ),
+        name="first_sums",
+    )(ints, tiles, *pieces)
+
+
+def last_body(ints, listed, begun, vals, *refs):
+    pieces, mine, other = refs[:-5], refs[-5], refs[-4]
+    src, acc, piece_sem = refs[-3:]
+    copies = []
+    for i, (piece, row) in enumerate(zip(pieces, FAR_ROWS)):
+        copies.append(pltpu.make_async_copy(piece, src.at[pl.ds(row, piece.shape[0])], piece_sem.at[i]))
+    for copy in copies:
+        copy.start()
+
+    @pl.loop(0, GRID + 1)
+    def _(r):
+        acc[r] = begun[r]
+
+    for copy in copies:
+        copy.wait()
+    add_tiles(ints, listed, listed[TILES + 1], vals, src, acc)
 
     @pl.loop(0, GRID // 2)
     def _(r):
-        other[r] = acc[2 * r + 1 - core].astype(other.dtype)
-        mine[r] = acc[2 * r + core]
-
-
-def tile_sums(ints, tiles, pieces):
-    smem = pl.BlockSpec(memory_space=pltpu.SMEM)
+        mine[r] = acc[r]
+        other[r] = acc[GRID // 2 + r].astype(other.dtype)
+
+
+def last_sums(ints, listed, begun, vals, pieces):
+    smem = pl.BlockSpec(memory_space=pltpu.SMEM)
+    vmem = pl.BlockSpec(memory_space=pltpu.VMEM)
     hbm = pl.BlockSpec(memory_space=pl.ANY)
     return pl.pallas_call(
-        tiles_body,
+        last_body,
         out_shape=(
             jax.ShapeDtypeStruct((GRID // 2, T, F), F32),
             jax.ShapeDtypeStruct((GRID // 2, T, F), BF),
         ),
-        in_specs=[smem] + [hbm] * (1 + len(pieces)),
-        out_specs=[pl.BlockSpec(memory_space=pltpu.VMEM)] * 2,
+        in_specs=[smem, smem, vmem, vmem] + [hbm] * len(pieces),
+        out_specs=[vmem] * 2,
         scratch_shapes=[
             pltpu.VMEM((GRID * T, F), BF),
-            pltpu.VMEM((TILES, T, T), BF),
             pltpu.VMEM((GRID + 1, T, F), F32),
             pltpu.SemaphoreType.DMA((len(pieces),)),
-            pltpu.SemaphoreType.DMA((TILES // CHUNK,)),
         ],
-        compiler_params=pltpu.CompilerParams(vmem_limit_bytes=47 * 2**20),
+        compiler_params=pltpu.CompilerParams(vmem_limit_bytes=24 * 2**20),
         cost_estimate=pl.CostEstimate(
-            flops=2 * TILES * T * T * F, bytes_accessed=8 * 2**20, transcendentals=0
-        ),
-        name="tile_sums",
-    )(ints, tiles, *pieces)
+            flops=TILES * T * T * F, bytes_accessed=8 * 2**20, transcendentals=0
+        ),
+        name="last_sums",
+    )(ints, listed, begun, vals, *pieces)
 
 
 def finish_body(core, parts, order, weight, bias, out_grad, act_out, mine, other):
@@ -178,15 +228,14 @@
 
 
 def ring_gather(own):
-    up = [(i, (i + 1) % 8) for i in range(8)]
-    down = [(i, (i - 1) % 8) for i in range(8)]
+    def shift(block, by):
+        return lax.ppermute(block, "y", [(i, (i + by) % 8) for i in range(8)])
+
     half = own.shape[0] // 2
-    below, above = [own], [own]
-    for _ in range(3):
-        below.append(lax.ppermute(below[-1], "y", up))
-        above.append(lax.ppermute(above[-1], "y", down))
-    far = [lax.ppermute(below[-1][:half], "y", up), lax.ppermute(above[-1][half:], "y", down)]
-    return below + far + above[:0:-1]
+    back1, ahead1, back2, ahead2 = (shift(own, by) for by in (1, -1, 2, -2))
+    back3, ahead3 = shift(back2, 1), shift(ahead2, -1)
+    far_low, far_high = shift(back2[:half], 2), shift(ahead2[half:], -2)
+    return (own, back1, back2, ahead2, ahead1), (back3, far_low, far_high, ahead3)
 
 
 def spread(block, axes, copies):
@@ -200,9 +249,10 @@
     core = lax.axis_index("core").astype(jnp.int32)
     clustered = cluster(node_order, features)
     near = lax.all_gather(clustered, "zh", axis=0, tiled=True)
-    pieces = ring_gather(near)
+    early, late = ring_gather(near)
     ints = jnp.concatenate([tile_index[0], tile_count, jnp.stack([row_at, core])])
-    mine, other = tile_sums(ints, tile_values[0], pieces)
+    begun, listed = first_sums(ints, tile_values[0], early)
+    mine, other = last_sums(ints, listed, begun, tile_values[0], late)
     paired = (mine + lax.ppermute(other, "core", swap).astype(F32)).astype(BF)
     parts = lax.all_to_all(paired, ("x", "zl"), 0, 0, tiled=True)
     core = core.reshape(1)

time: 184 us -> 180 us (0.978)
  waiting for transfers between devices: 13 us -> 6.88 us
  Pallas kernels: 6.86 us -> 9.75 us
  starting transfers between devices: 47.3 us -> 44.9 us
  local copies, waits for them, and re-layouts: 0.16 us -> 2.06 us
    ppermute x8, waiting for transfers between devices: 8.76 us -> 2.64 us  [shift(): return lax.ppermute(block, 'y', [(i, (i + by) % 8) for i in range(8)])]
    all_to_all x1, blocking collectives: 16.7 us -> 13.5 us  [local(): block = lax.all_to_all(half, ('y', 'x'), 0, 0, tiled=True).sum(axis=0)]
    pallas_call x1 -> x2, Pallas kernels: 3.29 us -> 6.17 us  [the longest x1 3.64 us: first_sums(): pl.pallas_call(first_body, out_shape=(jax.ShapeDtypeStruct((GRID + 1, T,...]
    all_to_all x1, blocking collectives: 36.2 us -> 38.3 us  [local(): parts = lax.all_to_all(paired, ('x', 'zl'), 0, 0, tiled=True)]
    unnamed x8 -> x10, local copies, waits for them, and re-layouts: 0.03 us -> 1.92 us
  transfers between devices with their start and end apart: 11 -> 11, of which waited for: 7 -> 5; matrix products, arithmetic and copies ran while one was open for 0% -> 0% of each run, Pallas kernels for 0% -> 2%
where the time goes in v4:
time: 180 us
  blocking collectives  113 us (63%)
  starting transfers between devices  44.9 us (25%)
  Pallas kernels  9.75 us (5%)
  waiting for transfers between devices  6.88 us (4%)
  local copies, waits for them, and re-layouts  2.06 us (1%)
    all_to_all x1, blocking collectives, local(): parts = lax.all_to_all(paired, ('x', 'zl'), 0, 0, tiled=True)  38.3 us
    all_to_all x2, blocking collectives, spread(): return lax.all_to_all(repeated, axes, 0, 0, tiled=True)  32.5 us
    ppermute x8, starting transfers between devices, shift(): return lax.ppermute(block, 'y', [(i, (i + by) % 8) for i in range(8)])  29.2 us
    all_gather x1, blocking collectives, local(): near = lax.all_gather(clustered, 'zh', axis=0, tiled=True)  29 us
    all_to_all x1, blocking collectives, local(): block = lax.all_to_all(half, ('y', 'x'), 0, 0, tiled=True).sum(axis=0)  13.5 us
    ppermute x1, starting transfers between devices, local(): paired = (mine + lax.ppermute(other, 'core', swap).astype(F32)).astype(BF)  6.16 us
    ppermute x1, starting transfers between devices, local(): lax.ppermute(half, 'core', swap)  6 us
    pallas_call x1, Pallas kernels, first_sums(): pl.pallas_call(first_body, out_shape=(jax.ShapeDtypeStruct((GRID + 1, T,...  3.64 us
  transfers between devices with their start and end apart: 11, of which 5 were waited for; matrix products, arithmetic and copies ran while one was open for 0% of the time, Pallas kernels for 2%

profile of v4, /device:TPU:1, one launch (start us, length us, event | category | flops | bytes accessed | tf_op | source)
XLA Modules:
  0.0 179.8 jit_solution(61886302044404461)
XLA Ops:
  0.6 1.7 cluster.1
  2.3 29.0 %all_gather.3.refs_1_ = bf16[512,256]{1,0:T(8,128)(2,1)S(1)} all-gather(bf16[128,256]{1,0:T(8,128)(2,1)} %cluster.1), channel_id=1, replica_groups=mesh['y'=8,'zh'=4,'x'=4,'zl'=4,'core'=2] {'zh'}, dimensions={0}, use_global_device_ids=true | all-gather | bytes 327680 | tf_op jit(solution)/shard_map/all_gather | solution.py:251
  31.3 7.4 %collective-permute-start.2 = (bf16[512,256]{1,0:T(8,128)(2,1)S(1)}, bf16[512,256]{1,0:T(8,128)(2,1)S(1)}, u32[]{:S(2)}, u32[]{:S(2)}) collective-permute-start(bf16[512,256]{1,0:T(8,128)(2,1)S(1)} %all_gather.3.refs_1_), channel_id=1, source_target_pairs={{0,768},{128,896},{256,0},{384,128},{512,256},{640,384},{768,512},... | collective-permute-start | bytes 786440 | tf_op jit(solution)/shard_map/ppermute | solution.py:232
  38.8 1.9 %collective-permute-start.1 = (bf16[512,256]{1,0:T(8,128)(2,1)S(1)}, bf16[512,256]{1,0:T(8,128)(2,1)S(1)}, u32[]{:S(2)}, u32[]{:S(2)}) collective-permute-start(bf16[512,256]{1,0:T(8,128)(2,1)S(1)} %all_gather.3.refs_1_), channel_id=1, source_target_pairs={{0,256},{128,384},{256,512},{384,640},{512,768},{640,896},{768,0},... | collective-permute-start | bytes 786440 | tf_op jit(solution)/shard_map/ppermute | solution.py:232
  40.7 4.7 %collective-permute-start.3 = (bf16[512,256]{1,0:T(8,128)(2,1)S(1)}, bf16[512,256]{1,0:T(8,128)(2,1)S(1)}, u32[]{:S(2)}, u32[]{:S(2)}) collective-permute-start(bf16[512,256]{1,0:T(8,128)(2,1)S(1)} %all_gather.3.refs_1_), channel_id=1, source_target_pairs={{0,896},{128,0},{256,128},{384,256},{512,384},{640,512},{768,640},... | collective-permute-start | bytes 786440 | tf_op jit(solution)/shard_map/ppermute | solution.py:232
  45.4 1.9 %collective-permute-start = (bf16[512,256]{1,0:T(8,128)(2,1)S(1)}, bf16[512,256]{1,0:T(8,128)(2,1)S(1)}, u32[]{:S(2)}, u32[]{:S(2)}) collective-permute-start(bf16[512,256]{1,0:T(8,128)(2,1)S(1)} %all_gather.3.refs_1_), channel_id=1, source_target_pairs={{0,128},{128,256},{256,384},{384,512},{512,640},{640,768},{768,896... | collective-permute-start | bytes 786440 | tf_op jit(solution)/shard_map/ppermute | solution.py:232
  47.3 2.1 %collective-permute-done.2.refs_4_ = bf16[512,256]{1,0:T(8,128)(2,1)S(1)} collective-permute-done((bf16[512,256]{1,0:T(8,128)(2,1)S(1)}, bf16[512,256]{1,0:T(8,128)(2,1)S(1)}, u32[]{:S(2)}, u32[]{:S(2)}) %collective-permute-start.2) | collective-permute-done | bytes 262176 | tf_op jit(solution)/shard_map/ppermute | solution.py:232
  49.5 2.4 %collective-permute-start.7 = (bf16[512,256]{1,0:T(8,128)(2,1)S(1)}, bf16[512,256]{1,0:T(8,128)(2,1)S(1)}, u32[]{:S(2)}, u32[]{:S(2)}) collective-permute-start(bf16[512,256]{1,0:T(8,128)(2,1)S(1)} %collective-permute-done.2.refs_4_), channel_id=1, source_target_pairs={{0,896},{128,0},{256,128},{384,256},{512,384},{640,512},{768,640},... | collective-permute-start | bytes 786440 | tf_op jit(solution)/shard_map/ppermute | solution.py:232
  51.9 0.5 collective-permute-done.1.refs_3_
  52.4 4.0 %collective-permute-start.4 = (bf16[512,256]{1,0:T(8,128)(2,1)S(1)}, bf16[512,256]{1,0:T(8,128)(2,1)S(1)}, u32[]{:S(2)}, u32[]{:S(2)}) collective-permute-start(bf16[512,256]{1,0:T(8,128)(2,1)S(1)} %collective-permute-done.1.refs_3_), channel_id=1, source_target_pairs={{0,128},{128,256},{256,384},{384,512},{512,640},{640,768},{768,896... | collective-permute-start | bytes 786440 | tf_op jit(solution)/shard_map/ppermute | solution.py:232
  57.1 4.8 %collective-permute-start.6 = (bf16[256,256]{1,0:T(8,128)(2,1)S(1)}, bf16[256,256]{1,0:T(8,128)(2,1)S(1)}, u32[]{:S(2)}, u32[]{:S(2)}) collective-permute-start(bf16[256,256]{1,0:T(8,128)(2,1)S(1)} %slice.9), channel_id=1, source_target_pairs={{0,768},{128,896},{256,0},{384,128},{512,256},{640,384},{768,512},... | collective-permute-start | bytes 393224 | tf_op jit(solution)/shard_map/ppermute | solution.py:232
  61.9 0.0 collective-permute-done.3.refs_5_
  61.9 1.9 %collective-permute-start.5 = (bf16[256,256]{1,0:T(8,128)(2,1)S(1)}, bf16[256,256]{1,0:T(8,128)(2,1)S(1)}, u32[]{:S(2)}, u32[]{:S(2)}) collective-permute-start(bf16[256,256]{1,0:T(8,128)(2,1)S(1)} %slice.8), channel_id=1, source_target_pairs={{0,256},{128,384},{256,512},{384,640},{512,768},{640,896},{768,0},... | collective-permute-start | bytes 393224 | tf_op jit(solution)/shard_map/ppermute | solution.py:232
  63.9 0.7 pad_add_fusion.ints
  64.6 0.0 collective-permute-done.refs_2_
  64.6 0.0 copy-start
  64.6 1.9 %copy-done = bf16[1,96,128,128]{3,2,1,0:T(8,128)(2,1)S(1)} copy-done((bf16[1,96,128,128]{3,2,1,0:T(8,128)(2,1)S(1)}, bf16[1,96,128,128]{3,2,1,0:T(8,128)(2,1)}, u32[]{:S(2)}) %copy-start) | copy-done | bytes 3145752
  66.5 3.6 %first_sums.1 = (f32[33,128,256]{2,1,0:T(8,128)S(1)}, s32[128]{0:T(128)S(1)}) custom-call(s32[99]{0:T(128)S(1)} %pad_add_fusion.ints, bf16[96,128,128]{2,1,0:T(8,128)(2,1)S(1)} %bitcast.6, bf16[512,256]{1,0:T(8,128)(2,1)S(1)} %all_gather.3.refs_1_, bf16[512,256]{1,0:T(8,128)(2,1)S(1)} %collective-permute-done.refs_2_, ...), custom_call_target="tpu_custom_call" | custom-call | flops 805306368 | bytes 8388608 | tf_op jit(solution)/shard_map/first_sums/pallas_call | solution.py:89
  70.2 0.0 collective-permute-done.6.refs_2_
  70.2 0.0 collective-permute-done.5.refs_1_
  70.2 0.0 collective-permute-done.7.refs_3_
  70.2 0.0 collective-permute-done.4.refs_0_
  70.2 2.5 %last_sums.1 = (f32[16,128,256]{2,1,0:T(8,128)S(1)}, bf16[16,128,256]{2,1,0:T(8,128)(2,1)S(1)}) custom-call(s32[99]{0:T(128)S(1)} %pad_add_fusion.ints, s32[128]{0:T(128)S(1)} %get-tuple-element.12.listed, f32[33,128,256]{2,1,0:T(8,128)S(1)} %get-tuple-element.13.begun, bf16[96,128,128]{2,1,0:T(8,128)(2,1)S(1)} %bitcast.7, ...), custom_call_target="tpu_custom_call" | custom-call | flops 402653184 | bytes 8388608 | tf_op jit(solution)/shard_map/last_sums/pallas_call | solution.py:137
  72.7 6.2 %collective-permute-start.8 = (bf16[16,128,256]{2,1,0:T(8,128)(2,1)S(1)}, bf16[16,128,256]{2,1,0:T(8,128)(2,1)S(1)}, u32[]{:S(2)}, u32[]{:S(2)}) collective-permute-start(bf16[16,128,256]{2,1,0:T(8,128)(2,1)S(1)} %get-tuple-element.15), channel_id=1, source_target_pairs={{0,1},{1,0},{2,3},{3,2},{4,5},{5,4},{6,7},{7,6},{8,9},{9,8},{10,11... | collective-permute-start | bytes 3145736 | tf_op jit(solution)/shard_map/ppermute | solution.py:256
  78.9 2.3 %collective-permute-done.8 = bf16[16,128,256]{2,1,0:T(8,128)(2,1)S(1)} collective-permute-done((bf16[16,128,256]{2,1,0:T(8,128)(2,1)S(1)}, bf16[16,128,256]{2,1,0:T(8,128)(2,1)S(1)}, u32[]{:S(2)}, u32[]{:S(2)}) %collective-permute-start.8) | collective-permute-done | bytes 1048608 | tf_op jit(solution)/shard_map/ppermute | solution.py:256
  81.2 0.3 add_convert_fusion
  81.5 0.0 copy-start.1
  81.5 0.0 copy-start.2
  81.5 0.0 copy-start.3
  81.5 0.0 copy-start.4
  81.5 38.3 %all_to_all.20.parts = bf16[16,128,256]{2,1,0:T(8,128)(2,1)S(1)} all-to-all(bf16[16,128,256]{2,1,0:T(8,128)(2,1)S(1)} %add_convert_fusion), channel_id=1, replica_groups=mesh['y'=8,'zh'=4,'x'=4,'zl'=4,'core'=2] {'x','zl'}, dimensions={0} | all-to-all | bytes 2097152 | tf_op jit(solution)/shard_map/all_to_all | solution.py:257
  119.8 0.0 copy-done.1
  119.8 0.0 copy-done.2
  119.8 0.0 copy-done.3
  119.8 0.0 copy-done.4
  119.8 1.1 finish.1
  120.9 3.6 %collective-permute-start.9 = (f32[32,1,1152]{2,1,0:T(1,128)S(1)}, f32[32,1,1152]{2,1,0:T(1,128)S(1)}, u32[]{:S(2)}, u32[]{:S(2)}) collective-permute-start(f32[32,1,1152]{2,1,0:T(1,128)S(1)} %get-tuple-element.18), channel_id=1, source_target_pairs={{0,1},{1,0},{2,3},{3,2},{4,5},{5,4},{6,7},{7,6},{8,9},{9,8},{10,11... | collective-permute-start | bytes 442376 | tf_op jit(solution)/shard_map/ppermute | solution.py:262
  124.5 1.0 collective-permute-done.9
  125.5 0.2 add.7
  125.7 13.5 %all_to_all.21 = f32[32,1,1152]{2,1,0:T(1,128)S(1)} all-to-all(f32[32,1,1152]{2,1,0:T(1,128)S(1)} %add.7), channel_id=1, replica_groups=mesh['y'=8,'zh'=4,'x'=4,'zl'=4,'core'=2] {'y','x'}, dimensions={0} | all-to-all | bytes 294912 | tf_op jit(solution)/shard_map/all_to_all | solution.py:263
  139.1 0.1 reduce_sum.18
  139.3 19.2 %all_to_all.22 = f32[16,1,1152]{2,1,0:T(1,128)S(1)} all-to-all(f32[16,1,1152]{2,1,0:T(1,128)S(1)} %broadcast_in_dim.4), channel_id=1, replica_groups=mesh['y'=8,'zh'=4,'x'=4,'zl'=4,'core'=2] {'zh','zl'}, dimensions={0} | all-to-all | bytes 147456 | tf_op jit(solution)/shard_map/all_to_all | solution.py:243
  158.5 0.1 reduce_sum.19
  158.5 0.1 broadcast_in_dim.5
  158.6 13.4 %all_to_all.23.mine = f32[32,1,1152]{2,1,0:T(1,128)S(1)} all-to-all(f32[32,1,1152]{2,1,0:T(1,128)S(1)} %broadcast_in_dim.5), channel_id=1, replica_groups=mesh['y'=8,'zh'=4,'x'=4,'zl'=4,'core'=2] {'y','x'}, dimensions={0} | all-to-all | bytes 294912 | tf_op jit(solution)/shard_map/all_to_all | solution.py:243
  172.0 6.0 %collective-permute-start.10 = (f32[32,1,1152]{2,1,0:T(1,128)S(1)}, f32[32,1,1152]{2,1,0:T(1,128)S(1)}, u32[]{:S(2)}, u32[]{:S(2)}) collective-permute-start(f32[32,1,1152]{2,1,0:T(1,128)S(1)} %all_to_all.23.mine), channel_id=1, source_target_pairs={{0,1},{1,0},{2,3},{3,2},{4,5},{5,4},{6,7},{7,6},{8,9},{9,8},{10,11... | collective-permute-start | bytes 442376 | tf_op jit(solution)/shard_map/ppermute | solution.py:266
  178.0 1.0 collective-permute-done.10.other
  178.9 0.8 unpack.1
  (3 shorter events, 0.1 us)
Async XLA Ops:
  31.3 18.1 %collective-permute-start.2 = (bf16[512,256]{1,0:T(8,128)(2,1)S(1)}, bf16[512,256]{1,0:T(8,128)(2,1)S(1)}, u32[]{:S(2)}, u32[]{:S(2)}) collective-permute-start(bf16[512,256]{1,0:T(8,128)(2,1)S(1)} %all_gather.3.refs_1_), channel_id=1, source_target_pairs={{0,768},{128,896},{256,0},{384,128},{512,256},{640,384},{768,512},... | collective-permute-start | bytes 786440 | tf_op jit(solution)/shard_map/ppermute | solution.py:232
  38.8 13.6 %collective-permute-start.1 = (bf16[512,256]{1,0:T(8,128)(2,1)S(1)}, bf16[512,256]{1,0:T(8,128)(2,1)S(1)}, u32[]{:S(2)}, u32[]{:S(2)}) collective-permute-start(bf16[512,256]{1,0:T(8,128)(2,1)S(1)} %all_gather.3.refs_1_), channel_id=1, source_target_pairs={{0,256},{128,384},{256,512},{384,640},{512,768},{640,896},{768,0},... | collective-permute-start | bytes 786440 | tf_op jit(solution)/shard_map/ppermute | solution.py:232
  40.7 21.2 %collective-permute-start.3 = (bf16[512,256]{1,0:T(8,128)(2,1)S(1)}, bf16[512,256]{1,0:T(8,128)(2,1)S(1)}, u32[]{:S(2)}, u32[]{:S(2)}) collective-permute-start(bf16[512,256]{1,0:T(8,128)(2,1)S(1)} %all_gather.3.refs_1_), channel_id=1, source_target_pairs={{0,896},{128,0},{256,128},{384,256},{512,384},{640,512},{768,640},... | collective-permute-start | bytes 786440 | tf_op jit(solution)/shard_map/ppermute | solution.py:232
  45.4 19.2 %collective-permute-start = (bf16[512,256]{1,0:T(8,128)(2,1)S(1)}, bf16[512,256]{1,0:T(8,128)(2,1)S(1)}, u32[]{:S(2)}, u32[]{:S(2)}) collective-permute-start(bf16[512,256]{1,0:T(8,128)(2,1)S(1)} %all_gather.3.refs_1_), channel_id=1, source_target_pairs={{0,128},{128,256},{256,384},{384,512},{512,640},{640,768},{768,896... | collective-permute-start | bytes 786440 | tf_op jit(solution)/shard_map/ppermute | solution.py:232
  49.5 20.7 %collective-permute-start.7 = (bf16[512,256]{1,0:T(8,128)(2,1)S(1)}, bf16[512,256]{1,0:T(8,128)(2,1)S(1)}, u32[]{:S(2)}, u32[]{:S(2)}) collective-permute-start(bf16[512,256]{1,0:T(8,128)(2,1)S(1)} %collective-permute-done.2.refs_4_), channel_id=1, source_target_pairs={{0,896},{128,0},{256,128},{384,256},{512,384},{640,512},{768,640},... | collective-permute-start | bytes 786440 | tf_op jit(solution)/shard_map/ppermute | solution.py:232
  52.4 17.8 %collective-permute-start.4 = (bf16[512,256]{1,0:T(8,128)(2,1)S(1)}, bf16[512,256]{1,0:T(8,128)(2,1)S(1)}, u32[]{:S(2)}, u32[]{:S(2)}) collective-permute-start(bf16[512,256]{1,0:T(8,128)(2,1)S(1)} %collective-permute-done.1.refs_3_), channel_id=1, source_target_pairs={{0,128},{128,256},{256,384},{384,512},{512,640},{640,768},{768,896... | collective-permute-start | bytes 786440 | tf_op jit(solution)/shard_map/ppermute | solution.py:232
  57.1 13.0 %collective-permute-start.6 = (bf16[256,256]{1,0:T(8,128)(2,1)S(1)}, bf16[256,256]{1,0:T(8,128)(2,1)S(1)}, u32[]{:S(2)}, u32[]{:S(2)}) collective-permute-start(bf16[256,256]{1,0:T(8,128)(2,1)S(1)} %slice.9), channel_id=1, source_target_pairs={{0,768},{128,896},{256,0},{384,128},{512,256},{640,384},{768,512},... | collective-permute-start | bytes 393224 | tf_op jit(solution)/shard_map/ppermute | solution.py:232
  61.9 8.2 %collective-permute-start.5 = (bf16[256,256]{1,0:T(8,128)(2,1)S(1)}, bf16[256,256]{1,0:T(8,128)(2,1)S(1)}, u32[]{:S(2)}, u32[]{:S(2)}) collective-permute-start(bf16[256,256]{1,0:T(8,128)(2,1)S(1)} %slice.8), channel_id=1, source_target_pairs={{0,256},{128,384},{256,512},{384,640},{512,768},{640,896},{768,0},... | collective-permute-start | bytes 393224 | tf_op jit(solution)/shard_map/ppermute | solution.py:232
  64.6 1.9 %copy-start = (bf16[1,96,128,128]{3,2,1,0:T(8,128)(2,1)S(1)}, bf16[1,96,128,128]{3,2,1,0:T(8,128)(2,1)}, u32[]{:S(2)}) copy-start(bf16[1,96,128,128]{3,2,1,0:T(8,128)(2,1)} %param.12) | copy-start | bytes 9437188
  72.7 8.4 %collective-permute-start.8 = (bf16[16,128,256]{2,1,0:T(8,128)(2,1)S(1)}, bf16[16,128,256]{2,1,0:T(8,128)(2,1)S(1)}, u32[]{:S(2)}, u32[]{:S(2)}) collective-permute-start(bf16[16,128,256]{2,1,0:T(8,128)(2,1)S(1)} %get-tuple-element.15), channel_id=1, source_target_pairs={{0,1},{1,0},{2,3},{3,2},{4,5},{5,4},{6,7},{7,6},{8,9},{9,8},{10,11... | collective-permute-start | bytes 3145736 | tf_op jit(solution)/shard_map/ppermute | solution.py:256
  81.5 38.3 %copy-start.1 = (bf16[256,256]{1,0:T(8,128)(2,1)S(1)}, bf16[256,256]{1,0:T(8,128)(2,1)}, u32[]{:S(2)}) copy-start(bf16[256,256]{1,0:T(8,128)(2,1)} %weight.1) | copy-start | bytes 393220
  81.5 38.3 %copy-start.2 = (bf16[128,256]{1,0:T(8,128)(2,1)S(1)}, bf16[128,256]{1,0:T(8,128)(2,1)}, u32[]{:S(2)}) copy-start(bf16[128,256]{1,0:T(8,128)(2,1)} %out_grad.1) | copy-start | bytes 196612
  81.5 38.3 %copy-start.3 = (s32[1,128]{1,0:T(1,128)S(1)}, s32[1,128]{1,0:T(1,128)}, u32[]{:S(2)}) copy-start(s32[1,128]{1,0:T(1,128)} %order.3) | copy-start | bytes 1540
  81.5 38.3 %copy-start.4 = (f32[256]{0:T(256)S(1)}, f32[256]{0:T(256)}, u32[]{:S(2)}) copy-start(f32[256]{0:T(256)} %param.14) | copy-start | bytes 3076
  120.9 4.6 %collective-permute-start.9 = (f32[32,1,1152]{2,1,0:T(1,128)S(1)}, f32[32,1,1152]{2,1,0:T(1,128)S(1)}, u32[]{:S(2)}, u32[]{:S(2)}) collective-permute-start(f32[32,1,1152]{2,1,0:T(1,128)S(1)} %get-tuple-element.18), channel_id=1, source_target_pairs={{0,1},{1,0},{2,3},{3,2},{4,5},{5,4},{6,7},{7,6},{8,9},{9,8},{10,11... | collective-permute-start | bytes 442376 | tf_op jit(solution)/shard_map/ppermute | solution.py:262
  172.0 7.0 %collective-permute-start.10 = (f32[32,1,1152]{2,1,0:T(1,128)S(1)}, f32[32,1,1152]{2,1,0:T(1,128)S(1)}, u32[]{:S(2)}, u32[]{:S(2)}) collective-permute-start(f32[32,1,1152]{2,1,0:T(1,128)S(1)} %all_to_all.23.mine), channel_id=1, source_target_pairs={{0,1},{1,0},{2,3},{3,2},{4,5},{5,4},{6,7},{7,6},{8,9},{9,8},{10,11... | collective-permute-start | bytes 442376 | tf_op jit(solution)/shard_map/ppermute | solution.py:266

commit v5 on v4

--- a/solution.py
+++ b/solution.py
@@ -1,3 +1,5 @@
+import functools
+
 import jax
 import jax.numpy as jnp
 from jax import lax
@@ -34,28 +36,22 @@
     )(order, feats)
 
 
-def near_block(ints, k):
-    at = ints[k]
-    row, col = at // GRID, at % GRID
-    back = (ints[TILES + 1] - col // 4) & 7
-    start = pl.multiple_of((back * 4 + (col & 3)) * T, T)
-    to = ((row & 1) ^ ints[TILES + 2]) * (GRID // 2) + (row >> 1)
-    return jnp.logical_or(back < FAR_FROM, back >= FAR_TO), start, to
-
-
-def add_tiles(ints, listed, used, vals, src, acc):
+def add_tiles(listed, vals, src, acc, base):
+    used, spare = listed[TILES + 1], acc.shape[0] - 1
+
     @pl.loop(0, (used + UNROLL - 1) // UNROLL)
     def _(g):
         for u in range(UNROLL):
             i = g * UNROLL + u
-            k = jnp.where(i < used, listed[i], 0)
-            _, start, to = near_block(ints, k)
-            to = jnp.where(i < used, to, GRID)
+            entry = listed[i]
+            to = jnp.where(i < used, (entry >> 12) - base, spare)
+            k = jnp.where(i < used, entry & 127, 0)
+            start = pl.multiple_of(jnp.where(i < used, (entry >> 7) & 31, 0) * T, T)
             acc[to] += jnp.dot(vals[k], src[pl.ds(start, T), :], preferred_element_type=F32)
 
 
 def first_body(ints, *refs):
-    vals, pieces, acc, later = refs[0], refs[1:-5], refs[-5], refs[-4]
+    vals, pieces, acc, own_later, away_later = refs[0], refs[1:-6], refs[-6], refs[-5], refs[-4]
     src, now, piece_sem = refs[-3:]
     copies = []
     for i, (piece, row) in enumerate(zip(pieces, NEAR_ROWS)):
@@ -67,19 +63,33 @@
     def _(r):
         acc[r] = jnp.zeros((T, F), F32)
 
-    def sort(k, counts):
-        near, _, _ = near_block(ints, k)
-        early, late = counts
-        now[early] = k
-        later[late] = k
-        step = near.astype(jnp.int32)
-        return early + step, late + 1 - step
-
-    early, late = lax.fori_loop(0, ints[TILES], sort, (jnp.int32(0), jnp.int32(0)))
-    later[TILES + 1] = late
+    used, here, core = ints[TILES], ints[TILES + 1], ints[TILES + 2]
+
+    lists = (now, own_later, away_later)
+
+    def sort(g, counts):
+        for u in range(UNROLL):
+            k = g * UNROLL + u
+            at = ints[k]
+            row, col = at >> 5, at & 31
+            back = (here - (col >> 2)) & 7
+            away = (row & 1) ^ core
+            to = away * (GRID // 2) + (row >> 1)
+            entry = k + (back * 4 + (col & 3)) * 128 + to * 4096
+            for held, n in zip(lists, counts):
+                held[n] = entry
+            far = jnp.logical_and(back >= FAR_FROM, back < FAR_TO).astype(jnp.int32)
+            live = (k < used).astype(jnp.int32)
+            steps = (live * (1 - far), live * far * (1 - away), live * far * away)
+            counts = tuple(n + step for n, step in zip(counts, steps))
+        return counts
+
+    counts = lax.fori_loop(0, (used + UNROLL - 1) // UNROLL, sort, (jnp.int32(0),) * 3)
+    for held, n in zip(lists, counts):
+        held[TILES + 1] = n
     for copy in copies:
         copy.wait()
-    add_tiles(ints, now, early, vals, src, acc)
+    add_tiles(now, vals, src, acc, 0)
 
 
 def first_sums(ints, tiles, pieces):
@@ -91,9 +101,10 @@
         out_shape=(
             jax.ShapeDtypeStruct((GRID + 1, T, F), F32),
             jax.ShapeDtypeStruct((T,), jnp.int32),
+            jax.ShapeDtypeStruct((T,), jnp.int32),
         ),
         in_specs=[smem, vmem] + [hbm] * len(pieces),
-        out_specs=[vmem, smem],
+        out_specs=[vmem, smem, smem],
         scratch_shapes=[
             pltpu.VMEM((GRID * T, F), BF),
             pltpu.SMEM((T,), jnp.int32),
@@ -107,52 +118,47 @@
     )(ints, tiles, *pieces)
 
 
-def last_body(ints, listed, begun, vals, *refs):
-    pieces, mine, other = refs[:-5], refs[-5], refs[-4]
-    src, acc, piece_sem = refs[-3:]
+def last_body(base, listed, begun, vals, *refs):
+    pieces, out, src, acc, piece_sem = refs[:-4], refs[-4], refs[-3], refs[-2], refs[-1]
     copies = []
     for i, (piece, row) in enumerate(zip(pieces, FAR_ROWS)):
         copies.append(pltpu.make_async_copy(piece, src.at[pl.ds(row, piece.shape[0])], piece_sem.at[i]))
     for copy in copies:
         copy.start()
 
-    @pl.loop(0, GRID + 1)
-    def _(r):
-        acc[r] = begun[r]
-
-    for copy in copies:
-        copy.wait()
-    add_tiles(ints, listed, listed[TILES + 1], vals, src, acc)
-
     @pl.loop(0, GRID // 2)
     def _(r):
-        mine[r] = acc[r]
-        other[r] = acc[GRID // 2 + r].astype(other.dtype)
-
-
-def last_sums(ints, listed, begun, vals, pieces):
+        acc[r] = begun[base + r]
+
+    for copy in copies:
+        copy.wait()
+    add_tiles(listed, vals, src, acc, base)
+
+    @pl.loop(0, GRID // 2)
+    def _(r):
+        out[r] = acc[r].astype(out.dtype)
+
+
+def last_sums(base, kind, listed, begun, vals, pieces):
     smem = pl.BlockSpec(memory_space=pltpu.SMEM)
     vmem = pl.BlockSpec(memory_space=pltpu.VMEM)
     hbm = pl.BlockSpec(memory_space=pl.ANY)
     return pl.pallas_call(
-        last_body,
-        out_shape=(
-            jax.ShapeDtypeStruct((GRID // 2, T, F), F32),
-            jax.ShapeDtypeStruct((GRID // 2, T, F), BF),
-        ),
-        in_specs=[smem, smem, vmem, vmem] + [hbm] * len(pieces),
-        out_specs=[vmem] * 2,
+        functools.partial(last_body, base),
+        out_shape=jax.ShapeDtypeStruct((GRID // 2, T, F), kind),
+        in_specs=[smem, vmem, vmem] + [hbm] * len(pieces),
+        out_specs=vmem,
         scratch_shapes=[
             pltpu.VMEM((GRID * T, F), BF),
-            pltpu.VMEM((GRID + 1, T, F), F32),
+            pltpu.VMEM((GRID // 2 + 1, T, F), F32),
             pltpu.SemaphoreType.DMA((len(pieces),)),
         ],
         compiler_params=pltpu.CompilerParams(vmem_limit_bytes=24 * 2**20),
         cost_estimate=pl.CostEstimate(
             flops=TILES * T * T * F, bytes_accessed=8 * 2**20, transcendentals=0
         ),
-        name="last_sums",
-    )(ints, listed, begun, vals, *pieces)
+        name="last_away" if base else "last_own",
+    )(listed, begun, vals, *pieces)
 
 
 def finish_body(core, parts, order, weight, bias, out_grad, act_out, mine, other):
@@ -251,9 +257,11 @@
     near = lax.all_gather(clustered, "zh", axis=0, tiled=True)
     early, late = ring_gather(near)
     ints = jnp.concatenate([tile_index[0], tile_count, jnp.stack([row_at, core])])
-    begun, listed = first_sums(ints, tile_values[0], early)
-    mine, other = last_sums(ints, listed, begun, tile_values[0], late)
-    paired = (mine + lax.ppermute(other, "core", swap).astype(F32)).astype(BF)
+    vals = tile_values[0]
+    begun, own_later, away_later = first_sums(ints, vals, early)
+    away = lax.ppermute(last_sums(GRID // 2, BF, away_later, begun, vals, late), "core", swap)
+    own = last_sums(0, F32, own_later, begun, vals, late)
+    paired = (own + away.astype(F32)).astype(BF)
     parts = lax.all_to_all(paired, ("x", "zl"), 0, 0, tiled=True)
     core = core.reshape(1)
     activated, mine, other = finish(

time: 180 us -> 179 us (level)
  starting transfers between devices: 44.9 us -> 47.7 us
  blocking collectives: 113 us -> 111 us
    all_to_all x1, blocking collectives: 38.3 us -> 34.2 us  [local(): parts = lax.all_to_all(paired, ('x', 'zl'), 0, 0, tiled=True)]
    ppermute x1, starting transfers between devices: 6.16 us -> 8.99 us  [local(): lax.ppermute(last_sums(GRID // 2, BF, away_later, begun, vals, late), 'co...]
    all_to_all x1, blocking collectives: 13.5 us -> 15.8 us  [local(): block = lax.all_to_all(half, ('y', 'x'), 0, 0, tiled=True).sum(axis=0)]
  transfers between devices with their start and end apart: 11 -> 11, of which waited for: 5 -> 6; matrix products, arithmetic and copies ran while one was open for 0% -> 0% of each run, Pallas kernels for 2% -> 2%
where the time goes in v5:
time: 179 us
  blocking collectives  111 us (62%)
  starting transfers between devices  47.7 us (27%)
  Pallas kernels  8.63 us (5%)
  waiting for transfers between devices  6.59 us (4%)
  local copies, waits for them, and re-layouts  2.06 us (1%)
    all_to_all x1, blocking collectives, local(): parts = lax.all_to_all(paired, ('x', 'zl'), 0, 0, tiled=True)  34.2 us
    all_to_all x2, blocking collectives, spread(): return lax.all_to_all(repeated, axes, 0, 0, tiled=True)  31.8 us
    ppermute x8, starting transfers between devices, shift(): return lax.ppermute(block, 'y', [(i, (i + by) % 8) for i in range(8)])  29.2 us
    all_gather x1, blocking collectives, local(): near = lax.all_gather(clustered, 'zh', axis=0, tiled=True)  29 us
    all_to_all x1, blocking collectives, local(): block = lax.all_to_all(half, ('y', 'x'), 0, 0, tiled=True).sum(axis=0)  15.8 us
    ppermute x1, starting transfers between devices, local(): lax.ppermute(last_sums(GRID // 2, BF, away_later, begun, vals, late), 'co...  8.99 us
    ppermute x1, starting transfers between devices, local(): lax.ppermute(half, 'core', swap)  6 us
    ppermute x8, waiting for transfers between devices, shift(): return lax.ppermute(block, 'y', [(i, (i + by) % 8) for i in range(8)])  3.98 us
  transfers between devices with their start and end apart: 11, of which 6 were waited for; matrix products, arithmetic and copies ran while one was open for 0% of the time, Pallas kernels for 2%

profile of v5, /device:TPU:1, one launch (start us, length us, event | category | flops | bytes accessed | tf_op | source)
XLA Modules:
  0.0 178.6 jit_solution(3468869875561371817)
XLA Ops:
  0.6 1.7 cluster.1
  2.3 29.0 %all_gather.3.refs_1_ = bf16[512,256]{1,0:T(8,128)(2,1)S(1)} all-gather(bf16[128,256]{1,0:T(8,128)(2,1)} %cluster.1), channel_id=1, replica_groups=mesh['y'=8,'zh'=4,'x'=4,'zl'=4,'core'=2] {'zh'}, dimensions={0}, use_global_device_ids=true | all-gather | bytes 327680 | tf_op jit(solution)/shard_map/all_gather | solution.py:257
  31.3 7.4 %collective-permute-start.2 = (bf16[512,256]{1,0:T(8,128)(2,1)S(1)}, bf16[512,256]{1,0:T(8,128)(2,1)S(1)}, u32[]{:S(2)}, u32[]{:S(2)}) collective-permute-start(bf16[512,256]{1,0:T(8,128)(2,1)S(1)} %all_gather.3.refs_1_), channel_id=1, source_target_pairs={{0,768},{128,896},{256,0},{384,128},{512,256},{640,384},{768,512},... | collective-permute-start | bytes 786440 | tf_op jit(solution)/shard_map/ppermute | solution.py:238
  38.8 1.9 %collective-permute-start.1 = (bf16[512,256]{1,0:T(8,128)(2,1)S(1)}, bf16[512,256]{1,0:T(8,128)(2,1)S(1)}, u32[]{:S(2)}, u32[]{:S(2)}) collective-permute-start(bf16[512,256]{1,0:T(8,128)(2,1)S(1)} %all_gather.3.refs_1_), channel_id=1, source_target_pairs={{0,256},{128,384},{256,512},{384,640},{512,768},{640,896},{768,0},... | collective-permute-start | bytes 786440 | tf_op jit(solution)/shard_map/ppermute | solution.py:238
  40.7 4.7 %collective-permute-start.3 = (bf16[512,256]{1,0:T(8,128)(2,1)S(1)}, bf16[512,256]{1,0:T(8,128)(2,1)S(1)}, u32[]{:S(2)}, u32[]{:S(2)}) collective-permute-start(bf16[512,256]{1,0:T(8,128)(2,1)S(1)} %all_gather.3.refs_1_), channel_id=1, source_target_pairs={{0,896},{128,0},{256,128},{384,256},{512,384},{640,512},{768,640},... | collective-permute-start | bytes 786440 | tf_op jit(solution)/shard_map/ppermute | solution.py:238
  45.4 1.9 %collective-permute-start = (bf16[512,256]{1,0:T(8,128)(2,1)S(1)}, bf16[512,256]{1,0:T(8,128)(2,1)S(1)}, u32[]{:S(2)}, u32[]{:S(2)}) collective-permute-start(bf16[512,256]{1,0:T(8,128)(2,1)S(1)} %all_gather.3.refs_1_), channel_id=1, source_target_pairs={{0,128},{128,256},{256,384},{384,512},{512,640},{640,768},{768,896... | collective-permute-start | bytes 786440 | tf_op jit(solution)/shard_map/ppermute | solution.py:238
  47.3 2.1 %collective-permute-done.2.refs_4_ = bf16[512,256]{1,0:T(8,128)(2,1)S(1)} collective-permute-done((bf16[512,256]{1,0:T(8,128)(2,1)S(1)}, bf16[512,256]{1,0:T(8,128)(2,1)S(1)}, u32[]{:S(2)}, u32[]{:S(2)}) %collective-permute-start.2) | collective-permute-done | bytes 262176 | tf_op jit(solution)/shard_map/ppermute | solution.py:238
  49.5 2.4 %collective-permute-start.7 = (bf16[512,256]{1,0:T(8,128)(2,1)S(1)}, bf16[512,256]{1,0:T(8,128)(2,1)S(1)}, u32[]{:S(2)}, u32[]{:S(2)}) collective-permute-start(bf16[512,256]{1,0:T(8,128)(2,1)S(1)} %collective-permute-done.2.refs_4_), channel_id=1, source_target_pairs={{0,896},{128,0},{256,128},{384,256},{512,384},{640,512},{768,640},... | collective-permute-start | bytes 786440 | tf_op jit(solution)/shard_map/ppermute | solution.py:238
  51.9 0.5 collective-permute-done.1.refs_3_
  52.4 4.0 %collective-permute-start.4 = (bf16[512,256]{1,0:T(8,128)(2,1)S(1)}, bf16[512,256]{1,0:T(8,128)(2,1)S(1)}, u32[]{:S(2)}, u32[]{:S(2)}) collective-permute-start(bf16[512,256]{1,0:T(8,128)(2,1)S(1)} %collective-permute-done.1.refs_3_), channel_id=1, source_target_pairs={{0,128},{128,256},{256,384},{384,512},{512,640},{640,768},{768,896... | collective-permute-start | bytes 786440 | tf_op jit(solution)/shard_map/ppermute | solution.py:238
  57.1 4.8 %collective-permute-start.6 = (bf16[256,256]{1,0:T(8,128)(2,1)S(1)}, bf16[256,256]{1,0:T(8,128)(2,1)S(1)}, u32[]{:S(2)}, u32[]{:S(2)}) collective-permute-start(bf16[256,256]{1,0:T(8,128)(2,1)S(1)} %slice.9), channel_id=1, source_target_pairs={{0,768},{128,896},{256,0},{384,128},{512,256},{640,384},{768,512},... | collective-permute-start | bytes 393224 | tf_op jit(solution)/shard_map/ppermute | solution.py:238
  61.9 0.0 collective-permute-done.3.refs_5_
  61.9 1.9 %collective-permute-start.5 = (bf16[256,256]{1,0:T(8,128)(2,1)S(1)}, bf16[256,256]{1,0:T(8,128)(2,1)S(1)}, u32[]{:S(2)}, u32[]{:S(2)}) collective-permute-start(bf16[256,256]{1,0:T(8,128)(2,1)S(1)} %slice.8), channel_id=1, source_target_pairs={{0,256},{128,384},{256,512},{384,640},{512,768},{640,896},{768,0},... | collective-permute-start | bytes 393224 | tf_op jit(solution)/shard_map/ppermute | solution.py:238
  63.9 0.7 pad_add_fusion.ints
  64.6 0.0 collective-permute-done.refs_2_
  64.6 0.0 copy-start
  64.6 1.9 %copy-done = bf16[1,96,128,128]{3,2,1,0:T(8,128)(2,1)S(1)} copy-done((bf16[1,96,128,128]{3,2,1,0:T(8,128)(2,1)S(1)}, bf16[1,96,128,128]{3,2,1,0:T(8,128)(2,1)}, u32[]{:S(2)}) %copy-start) | copy-done | bytes 3145752
  66.5 0.0 copy-start.1
  66.5 2.1 %first_sums.1 = (f32[33,128,256]{2,1,0:T(8,128)S(1)}, s32[128]{0:T(128)S(1)}, s32[128]{0:T(128)S(1)}) custom-call(s32[99]{0:T(128)S(1)} %pad_add_fusion.ints, bf16[96,128,128]{2,1,0:T(8,128)(2,1)S(1)} %bitcast.6, bf16[512,256]{1,0:T(8,128)(2,1)S(1)} %all_gather.3.refs_1_, bf16[512,256]{1,0:T(8,128)(2,1)S(1)} %collective-permute-done.refs_2_, ...), custom_call_target="tpu_custom_call" | custom-call | flops 805306368 | bytes 8388608 | tf_op jit(solution)/shard_map/first_sums/pallas_call | solution.py:99
  68.6 0.0 collective-permute-done.6.refs_2_
  68.7 1.3 collective-permute-done.5.refs_1_
  70.0 0.0 collective-permute-done.7.refs_3_
  70.0 0.0 collective-permute-done.4.refs_0_
  70.0 0.0 copy-done.1
  70.0 1.3 last_away.1
  71.3 9.0 %collective-permute-start.8 = (bf16[16,128,256]{2,1,0:T(8,128)(2,1)S(1)}, bf16[16,128,256]{2,1,0:T(8,128)(2,1)S(1)}, u32[]{:S(2)}, u32[]{:S(2)}) collective-permute-start(bf16[16,128,256]{2,1,0:T(8,128)(2,1)S(1)} %last_away.1), channel_id=1, source_target_pairs={{0,1},{1,0},{2,3},{3,2},{4,5},{5,4},{6,7},{7,6},{8,9},{9,8},{10,11... | collective-permute-start | bytes 3145736 | tf_op jit(solution)/shard_map/ppermute | solution.py:262
  80.3 1.6 last_own.1
  81.9 0.6 collective-permute-done.8
  82.6 0.3 add_convert_fusion
  82.9 0.0 copy-start.2
  82.9 0.0 copy-start.3
  82.9 0.0 copy-start.4
  82.9 0.0 copy-start.5
  83.0 34.2 %all_to_all.20.parts = bf16[16,128,256]{2,1,0:T(8,128)(2,1)S(1)} all-to-all(bf16[16,128,256]{2,1,0:T(8,128)(2,1)S(1)} %add_convert_fusion), channel_id=1, replica_groups=mesh['y'=8,'zh'=4,'x'=4,'zl'=4,'core'=2] {'x','zl'}, dimensions={0} | all-to-all | bytes 2097152 | tf_op jit(solution)/shard_map/all_to_all | solution.py:265
  117.1 0.0 copy-done.2
  117.1 0.0 copy-done.3
  117.1 0.0 copy-done.4
  117.1 0.0 copy-done.5
  117.1 1.1 finish.1
  118.2 3.6 %collective-permute-start.9 = (f32[32,1,1152]{2,1,0:T(1,128)S(1)}, f32[32,1,1152]{2,1,0:T(1,128)S(1)}, u32[]{:S(2)}, u32[]{:S(2)}) collective-permute-start(f32[32,1,1152]{2,1,0:T(1,128)S(1)} %get-tuple-element.16), channel_id=1, source_target_pairs={{0,1},{1,0},{2,3},{3,2},{4,5},{5,4},{6,7},{7,6},{8,9},{9,8},{10,11... | collective-permute-start | bytes 442376 | tf_op jit(solution)/shard_map/ppermute | solution.py:270
  121.8 1.0 collective-permute-done.9
  122.8 0.2 add.7
  122.9 15.8 %all_to_all.21 = f32[32,1,1152]{2,1,0:T(1,128)S(1)} all-to-all(f32[32,1,1152]{2,1,0:T(1,128)S(1)} %add.7), channel_id=1, replica_groups=mesh['y'=8,'zh'=4,'x'=4,'zl'=4,'core'=2] {'y','x'}, dimensions={0} | all-to-all | bytes 294912 | tf_op jit(solution)/shard_map/all_to_all | solution.py:271
  138.7 0.1 reduce_sum.18
  138.8 18.4 %all_to_all.22 = f32[16,1,1152]{2,1,0:T(1,128)S(1)} all-to-all(f32[16,1,1152]{2,1,0:T(1,128)S(1)} %broadcast_in_dim.4), channel_id=1, replica_groups=mesh['y'=8,'zh'=4,'x'=4,'zl'=4,'core'=2] {'zh','zl'}, dimensions={0} | all-to-all | bytes 147456 | tf_op jit(solution)/shard_map/all_to_all | solution.py:249
  157.3 0.1 reduce_sum.19
  157.3 0.1 broadcast_in_dim.5
  157.4 13.4 %all_to_all.23.mine = f32[32,1,1152]{2,1,0:T(1,128)S(1)} all-to-all(f32[32,1,1152]{2,1,0:T(1,128)S(1)} %broadcast_in_dim.5), channel_id=1, replica_groups=mesh['y'=8,'zh'=4,'x'=4,'zl'=4,'core'=2] {'y','x'}, dimensions={0} | all-to-all | bytes 294912 | tf_op jit(solution)/shard_map/all_to_all | solution.py:249
  170.8 6.0 %collective-permute-start.10 = (f32[32,1,1152]{2,1,0:T(1,128)S(1)}, f32[32,1,1152]{2,1,0:T(1,128)S(1)}, u32[]{:S(2)}, u32[]{:S(2)}) collective-permute-start(f32[32,1,1152]{2,1,0:T(1,128)S(1)} %all_to_all.23.mine), channel_id=1, source_target_pairs={{0,1},{1,0},{2,3},{3,2},{4,5},{5,4},{6,7},{7,6},{8,9},{9,8},{10,11... | collective-permute-start | bytes 442376 | tf_op jit(solution)/shard_map/ppermute | solution.py:274
  176.8 1.0 collective-permute-done.10.other
  177.8 0.8 unpack.1
  (3 shorter events, 0.1 us)
Async XLA Ops:
  31.3 18.1 %collective-permute-start.2 = (bf16[512,256]{1,0:T(8,128)(2,1)S(1)}, bf16[512,256]{1,0:T(8,128)(2,1)S(1)}, u32[]{:S(2)}, u32[]{:S(2)}) collective-permute-start(bf16[512,256]{1,0:T(8,128)(2,1)S(1)} %all_gather.3.refs_1_), channel_id=1, source_target_pairs={{0,768},{128,896},{256,0},{384,128},{512,256},{640,384},{768,512},... | collective-permute-start | bytes 786440 | tf_op jit(solution)/shard_map/ppermute | solution.py:238
  38.8 13.6 %collective-permute-start.1 = (bf16[512,256]{1,0:T(8,128)(2,1)S(1)}, bf16[512,256]{1,0:T(8,128)(2,1)S(1)}, u32[]{:S(2)}, u32[]{:S(2)}) collective-permute-start(bf16[512,256]{1,0:T(8,128)(2,1)S(1)} %all_gather.3.refs_1_), channel_id=1, source_target_pairs={{0,256},{128,384},{256,512},{384,640},{512,768},{640,896},{768,0},... | collective-permute-start | bytes 786440 | tf_op jit(solution)/shard_map/ppermute | solution.py:238
  40.7 21.2 %collective-permute-start.3 = (bf16[512,256]{1,0:T(8,128)(2,1)S(1)}, bf16[512,256]{1,0:T(8,128)(2,1)S(1)}, u32[]{:S(2)}, u32[]{:S(2)}) collective-permute-start(bf16[512,256]{1,0:T(8,128)(2,1)S(1)} %all_gather.3.refs_1_), channel_id=1, source_target_pairs={{0,896},{128,0},{256,128},{384,256},{512,384},{640,512},{768,640},... | collective-permute-start | bytes 786440 | tf_op jit(solution)/shard_map/ppermute | solution.py:238
  45.4 19.2 %collective-permute-start = (bf16[512,256]{1,0:T(8,128)(2,1)S(1)}, bf16[512,256]{1,0:T(8,128)(2,1)S(1)}, u32[]{:S(2)}, u32[]{:S(2)}) collective-permute-start(bf16[512,256]{1,0:T(8,128)(2,1)S(1)} %all_gather.3.refs_1_), channel_id=1, source_target_pairs={{0,128},{128,256},{256,384},{384,512},{512,640},{640,768},{768,896... | collective-permute-start | bytes 786440 | tf_op jit(solution)/shard_map/ppermute | solution.py:238
  49.5 20.5 %collective-permute-start.7 = (bf16[512,256]{1,0:T(8,128)(2,1)S(1)}, bf16[512,256]{1,0:T(8,128)(2,1)S(1)}, u32[]{:S(2)}, u32[]{:S(2)}) collective-permute-start(bf16[512,256]{1,0:T(8,128)(2,1)S(1)} %collective-permute-done.2.refs_4_), channel_id=1, source_target_pairs={{0,896},{128,0},{256,128},{384,256},{512,384},{640,512},{768,640},... | collective-permute-start | bytes 786440 | tf_op jit(solution)/shard_map/ppermute | solution.py:238
  52.4 17.6 %collective-permute-start.4 = (bf16[512,256]{1,0:T(8,128)(2,1)S(1)}, bf16[512,256]{1,0:T(8,128)(2,1)S(1)}, u32[]{:S(2)}, u32[]{:S(2)}) collective-permute-start(bf16[512,256]{1,0:T(8,128)(2,1)S(1)} %collective-permute-done.1.refs_3_), channel_id=1, source_target_pairs={{0,128},{128,256},{256,384},{384,512},{512,640},{640,768},{768,896... | collective-permute-start | bytes 786440 | tf_op jit(solution)/shard_map/ppermute | solution.py:238
  57.1 11.5 %collective-permute-start.6 = (bf16[256,256]{1,0:T(8,128)(2,1)S(1)}, bf16[256,256]{1,0:T(8,128)(2,1)S(1)}, u32[]{:S(2)}, u32[]{:S(2)}) collective-permute-start(bf16[256,256]{1,0:T(8,128)(2,1)S(1)} %slice.9), channel_id=1, source_target_pairs={{0,768},{128,896},{256,0},{384,128},{512,256},{640,384},{768,512},... | collective-permute-start | bytes 393224 | tf_op jit(solution)/shard_map/ppermute | solution.py:238
  61.9 8.1 %collective-permute-start.5 = (bf16[256,256]{1,0:T(8,128)(2,1)S(1)}, bf16[256,256]{1,0:T(8,128)(2,1)S(1)}, u32[]{:S(2)}, u32[]{:S(2)}) collective-permute-start(bf16[256,256]{1,0:T(8,128)(2,1)S(1)} %slice.8), channel_id=1, source_target_pairs={{0,256},{128,384},{256,512},{384,640},{512,768},{640,896},{768,0},... | collective-permute-start | bytes 393224 | tf_op jit(solution)/shard_map/ppermute | solution.py:238
  64.6 1.9 %copy-start = (bf16[1,96,128,128]{3,2,1,0:T(8,128)(2,1)S(1)}, bf16[1,96,128,128]{3,2,1,0:T(8,128)(2,1)}, u32[]{:S(2)}) copy-start(bf16[1,96,128,128]{3,2,1,0:T(8,128)(2,1)} %param.12) | copy-start | bytes 9437188
  66.5 3.5 %copy-start.1 = (bf16[1,96,128,128]{3,2,1,0:T(8,128)(2,1)S(1)}, bf16[1,96,128,128]{3,2,1,0:T(8,128)(2,1)}, u32[]{:S(2)}) copy-start(bf16[1,96,128,128]{3,2,1,0:T(8,128)(2,1)} %param.12) | copy-start | bytes 9437188
  71.3 11.3 %collective-permute-start.8 = (bf16[16,128,256]{2,1,0:T(8,128)(2,1)S(1)}, bf16[16,128,256]{2,1,0:T(8,128)(2,1)S(1)}, u32[]{:S(2)}, u32[]{:S(2)}) collective-permute-start(bf16[16,128,256]{2,1,0:T(8,128)(2,1)S(1)} %last_away.1), channel_id=1, source_target_pairs={{0,1},{1,0},{2,3},{3,2},{4,5},{5,4},{6,7},{7,6},{8,9},{9,8},{10,11... | collective-permute-start | bytes 3145736 | tf_op jit(solution)/shard_map/ppermute | solution.py:262
  82.9 34.2 %copy-start.2 = (bf16[256,256]{1,0:T(8,128)(2,1)S(1)}, bf16[256,256]{1,0:T(8,128)(2,1)}, u32[]{:S(2)}) copy-start(bf16[256,256]{1,0:T(8,128)(2,1)} %weight.1) | copy-start | bytes 393220
  82.9 34.2 %copy-start.3 = (bf16[128,256]{1,0:T(8,128)(2,1)S(1)}, bf16[128,256]{1,0:T(8,128)(2,1)}, u32[]{:S(2)}) copy-start(bf16[128,256]{1,0:T(8,128)(2,1)} %out_grad.1) | copy-start | bytes 196612
  82.9 34.2 %copy-start.4 = (s32[1,128]{1,0:T(1,128)S(1)}, s32[1,128]{1,0:T(1,128)}, u32[]{:S(2)}) copy-start(s32[1,128]{1,0:T(1,128)} %order.3) | copy-start | bytes 1540
  82.9 34.2 %copy-start.5 = (f32[256]{0:T(256)S(1)}, f32[256]{0:T(256)}, u32[]{:S(2)}) copy-start(f32[256]{0:T(256)} %param.14) | copy-start | bytes 3076
  118.2 4.6 %collective-permute-start.9 = (f32[32,1,1152]{2,1,0:T(1,128)S(1)}, f32[32,1,1152]{2,1,0:T(1,128)S(1)}, u32[]{:S(2)}, u32[]{:S(2)}) collective-permute-start(f32[32,1,1152]{2,1,0:T(1,128)S(1)} %get-tuple-element.16), channel_id=1, source_target_pairs={{0,1},{1,0},{2,3},{3,2},{4,5},{5,4},{6,7},{7,6},{8,9},{9,8},{10,11... | collective-permute-start | bytes 442376 | tf_op jit(solution)/shard_map/ppermute | solution.py:270
  170.8 7.0 %collective-permute-start.10 = (f32[32,1,1152]{2,1,0:T(1,128)S(1)}, f32[32,1,1152]{2,1,0:T(1,128)S(1)}, u32[]{:S(2)}, u32[]{:S(2)}) collective-permute-start(f32[32,1,1152]{2,1,0:T(1,128)S(1)} %all_to_all.23.mine), channel_id=1, source_target_pairs={{0,1},{1,0},{2,3},{3,2},{4,5},{5,4},{6,7},{7,6},{8,9},{9,8},{10,11... | collective-permute-start | bytes 442376 | tf_op jit(solution)/shard_map/ppermute | solution.py:274

commit v6 on v5

--- a/solution.py
+++ b/solution.py
@@ -15,7 +15,7 @@
 UNROLL = 8
 FAR_FROM, FAR_TO = 3, 6
 NEAR_ROWS = (0, 512, 1024, 3072, 3584)
-FAR_ROWS = (1536, 2048, 2304, 2560)
+FAR_ROWS = (1536, 2048, 2560)
 BF = jnp.bfloat16
 F32 = jnp.float32
 
@@ -233,15 +233,15 @@
     )(core, mine, other)
 
 
-def ring_gather(own):
+def ring_gather(own, core):
     def shift(block, by):
         return lax.ppermute(block, "y", [(i, (i + by) % 8) for i in range(8)])
 
-    half = own.shape[0] // 2
     back1, ahead1, back2, ahead2 = (shift(own, by) for by in (1, -1, 2, -2))
     back3, ahead3 = shift(back2, 1), shift(ahead2, -1)
-    far_low, far_high = shift(back2[:half], 2), shift(ahead2[half:], -2)
-    return (own, back1, back2, ahead2, ahead1), (back3, far_low, far_high, ahead3)
+    hops = [(2 * i + c, 2 * ((i + (2, -2)[c]) % 8) + c) for i in range(8) for c in range(2)]
+    far = lax.ppermute(jnp.where(core == 0, back2, ahead2), ("y", "core"), hops)
+    return (own, back1, back2, ahead2, ahead1), (back3, far, ahead3)
 
 
 def spread(block, axes, copies):
@@ -255,7 +255,7 @@
     core = lax.axis_index("core").astype(jnp.int32)
     clustered = cluster(node_order, features)
     near = lax.all_gather(clustered, "zh", axis=0, tiled=True)
-    early, late = ring_gather(near)
+    early, late = ring_gather(near, core)
     ints = jnp.concatenate([tile_index[0], tile_count, jnp.stack([row_at, core])])
     vals = tile_values[0]
     begun, own_later, away_later = first_sums(ints, vals, early)

time: 179 us -> 176 us (0.983)
  starting transfers between devices: 47.7 us -> 44.1 us
  blocking collectives: 111 us -> 109 us
    ppermute x8 -> x6, starting transfers between devices: 29.2 us -> 21.8 us  [shift(): return lax.ppermute(block, 'y', [(i, (i + by) % 8) for i in range(8)])]
    ppermute x0 -> x1, starting transfers between devices: none -> 5.46 us  [ring_gather(): far = lax.ppermute(jnp.where(core == 0, back2, ahead2), ('y', 'core'), hops)]
    all_to_all x1, blocking collectives: 15.8 us -> 12.5 us  [local(): block = lax.all_to_all(half, ('y', 'x'), 0, 0, tiled=True).sum(axis=0)]
    ppermute x8 -> x6, waiting for transfers between devices: 3.98 us -> 5.25 us  [shift(): return lax.ppermute(block, 'y', [(i, (i + by) % 8) for i in range(8)])]
  transfers between devices with their start and end apart: 11 -> 10, of which waited for: 6 -> 6; matrix products, arithmetic and copies ran while one was open for 0% -> 0% of each run, Pallas kernels for 2% -> 2%
where the time goes in v6:
time: 176 us; the launch traced here: 175 us
  blocking collectives  109 us (62%)
  starting transfers between devices  44.1 us (25%)
  Pallas kernels  8.97 us (5%)
  waiting for transfers between devices  8.18 us (5%)
  local copies, waits for them, and re-layouts  2.03 us (1%)
    all_to_all x1, blocking collectives, local(): parts = lax.all_to_all(paired, ('x', 'zl'), 0, 0, tiled=True)  35.8 us
    all_to_all x2, blocking collectives, spread(): return lax.all_to_all(repeated, axes, 0, 0, tiled=True)  31.9 us
    all_gather x1, blocking collectives, local(): near = lax.all_gather(clustered, 'zh', axis=0, tiled=True)  29 us
    ppermute x6, starting transfers between devices, shift(): return lax.ppermute(block, 'y', [(i, (i + by) % 8) for i in range(8)])  21.8 us
    all_to_all x1, blocking collectives, local(): block = lax.all_to_all(half, ('y', 'x'), 0, 0, tiled=True).sum(axis=0)  12.5 us
    ppermute x1, starting transfers between devices, local(): lax.ppermute(last_sums(GRID // 2, BF, away_later, begun, vals, late), 'co...  7.2 us
    ppermute x1, starting transfers between devices, local(): lax.ppermute(half, 'core', swap)  6 us
    ppermute x1, starting transfers between devices, ring_gather(): far = lax.ppermute(jnp.where(core == 0, back2, ahead2), ('y', 'core'), hops)  5.46 us
  transfers between devices with their start and end apart: 10, of which 6 were waited for; matrix products, arithmetic and copies ran while one was open for 0% of the time, Pallas kernels for 2%

profile of v6, /device:TPU:1, one launch (start us, length us, event | category | flops | bytes accessed | tf_op | source)
XLA Modules:
  0.0 175.3 jit_solution(10388083258967669440)
XLA Ops:
  0.6 1.7 cluster.1
  2.3 29.0 %all_gather.3.refs_1_ = bf16[512,256]{1,0:T(8,128)(2,1)S(1)} all-gather(bf16[128,256]{1,0:T(8,128)(2,1)} %cluster.1), channel_id=1, replica_groups=mesh['y'=8,'zh'=4,'x'=4,'zl'=4,'core'=2] {'zh'}, dimensions={0}, use_global_device_ids=true | all-gather | bytes 327680 | tf_op jit(solution)/shard_map/all_gather | solution.py:257
  31.3 7.4 %collective-permute-start.2 = (bf16[512,256]{1,0:T(8,128)(2,1)S(1)}, bf16[512,256]{1,0:T(8,128)(2,1)S(1)}, u32[]{:S(2)}, u32[]{:S(2)}) collective-permute-start(bf16[512,256]{1,0:T(8,128)(2,1)S(1)} %all_gather.3.refs_1_), channel_id=1, source_target_pairs={{0,768},{128,896},{256,0},{384,128},{512,256},{640,384},{768,512},... | collective-permute-start | bytes 786440 | tf_op jit(solution)/shard_map/ppermute | solution.py:238
  38.8 1.9 %collective-permute-start.1 = (bf16[512,256]{1,0:T(8,128)(2,1)S(1)}, bf16[512,256]{1,0:T(8,128)(2,1)S(1)}, u32[]{:S(2)}, u32[]{:S(2)}) collective-permute-start(bf16[512,256]{1,0:T(8,128)(2,1)S(1)} %all_gather.3.refs_1_), channel_id=1, source_target_pairs={{0,256},{128,384},{256,512},{384,640},{512,768},{640,896},{768,0},... | collective-permute-start | bytes 786440 | tf_op jit(solution)/shard_map/ppermute | solution.py:238
  40.7 4.7 %collective-permute-start.3 = (bf16[512,256]{1,0:T(8,128)(2,1)S(1)}, bf16[512,256]{1,0:T(8,128)(2,1)S(1)}, u32[]{:S(2)}, u32[]{:S(2)}) collective-permute-start(bf16[512,256]{1,0:T(8,128)(2,1)S(1)} %all_gather.3.refs_1_), channel_id=1, source_target_pairs={{0,896},{128,0},{256,128},{384,256},{512,384},{640,512},{768,640},... | collective-permute-start | bytes 786440 | tf_op jit(solution)/shard_map/ppermute | solution.py:238
  45.4 1.9 %collective-permute-start = (bf16[512,256]{1,0:T(8,128)(2,1)S(1)}, bf16[512,256]{1,0:T(8,128)(2,1)S(1)}, u32[]{:S(2)}, u32[]{:S(2)}) collective-permute-start(bf16[512,256]{1,0:T(8,128)(2,1)S(1)} %all_gather.3.refs_1_), channel_id=1, source_target_pairs={{0,128},{128,256},{256,384},{384,512},{512,640},{640,768},{768,896... | collective-permute-start | bytes 786440 | tf_op jit(solution)/shard_map/ppermute | solution.py:238
  47.3 2.1 %collective-permute-done.2.refs_4_ = bf16[512,256]{1,0:T(8,128)(2,1)S(1)} collective-permute-done((bf16[512,256]{1,0:T(8,128)(2,1)S(1)}, bf16[512,256]{1,0:T(8,128)(2,1)S(1)}, u32[]{:S(2)}, u32[]{:S(2)}) %collective-permute-start.2) | collective-permute-done | bytes 262176 | tf_op jit(solution)/shard_map/ppermute | solution.py:238
  49.5 2.5 %collective-permute-start.6 = (bf16[512,256]{1,0:T(8,128)(2,1)S(1)}, bf16[512,256]{1,0:T(8,128)(2,1)S(1)}, u32[]{:S(2)}, u32[]{:S(2)}) collective-permute-start(bf16[512,256]{1,0:T(8,128)(2,1)S(1)} %collective-permute-done.2.refs_4_), channel_id=1, source_target_pairs={{0,896},{128,0},{256,128},{384,256},{512,384},{640,512},{768,640},... | collective-permute-start | bytes 786440 | tf_op jit(solution)/shard_map/ppermute | solution.py:238
  51.9 0.5 collective-permute-done.1.refs_3_
  52.4 5.5 %collective-permute-start.5 = (bf16[512,256]{1,0:T(8,128)(2,1)S(1)}, bf16[512,256]{1,0:T(8,128)(2,1)S(1)}, u32[]{:S(2)}, u32[]{:S(2)}) collective-permute-start(bf16[512,256]{1,0:T(8,128)(2,1)S(1)} %broadcast_select_fusion), channel_id=1, source_target_pairs={{0,256},{1,769},{128,384},{129,897},{256,512},{257,1},{384,640},{3... | collective-permute-start | bytes 786440 | tf_op jit(solution)/shard_map/ppermute | solution.py:243
  57.9 3.4 %collective-permute-start.4 = (bf16[512,256]{1,0:T(8,128)(2,1)S(1)}, bf16[512,256]{1,0:T(8,128)(2,1)S(1)}, u32[]{:S(2)}, u32[]{:S(2)}) collective-permute-start(bf16[512,256]{1,0:T(8,128)(2,1)S(1)} %collective-permute-done.1.refs_3_), channel_id=1, source_target_pairs={{0,128},{128,256},{256,384},{384,512},{512,640},{640,768},{768,896... | collective-permute-start | bytes 786440 | tf_op jit(solution)/shard_map/ppermute | solution.py:238
  61.9 0.7 pad_add_fusion.ints
  62.7 0.0 collective-permute-done.3.refs_5_
  62.7 0.0 collective-permute-done.refs_2_
  62.7 0.0 copy-start
  62.7 1.9 %copy-done = bf16[1,96,128,128]{3,2,1,0:T(8,128)(2,1)S(1)} copy-done((bf16[1,96,128,128]{3,2,1,0:T(8,128)(2,1)S(1)}, bf16[1,96,128,128]{3,2,1,0:T(8,128)(2,1)}, u32[]{:S(2)}) %copy-start) | copy-done | bytes 3145752
  64.6 0.0 copy-start.1
  64.6 2.8 %first_sums.1 = (f32[33,128,256]{2,1,0:T(8,128)S(1)}, s32[128]{0:T(128)S(1)}, s32[128]{0:T(128)S(1)}) custom-call(s32[99]{0:T(128)S(1)} %pad_add_fusion.ints, bf16[96,128,128]{2,1,0:T(8,128)(2,1)S(1)} %bitcast.6, bf16[512,256]{1,0:T(8,128)(2,1)S(1)} %all_gather.3.refs_1_, bf16[512,256]{1,0:T(8,128)(2,1)S(1)} %collective-permute-done.refs_2_, ...), custom_call_target="tpu_custom_call" | custom-call | flops 805306368 | bytes 8388608 | tf_op jit(solution)/shard_map/first_sums/pallas_call | solution.py:99
  67.4 0.0 collective-permute-done.6.refs_2_
  67.4 0.0 collective-permute-done.5.refs_1_
  67.4 2.6 %collective-permute-done.4.refs_0_ = bf16[512,256]{1,0:T(8,128)(2,1)S(1)} collective-permute-done((bf16[512,256]{1,0:T(8,128)(2,1)S(1)}, bf16[512,256]{1,0:T(8,128)(2,1)S(1)}, u32[]{:S(2)}, u32[]{:S(2)}) %collective-permute-start.4) | collective-permute-done | bytes 262176 | tf_op jit(solution)/shard_map/ppermute | solution.py:238
  70.1 0.0 copy-done.1
  70.1 1.3 last_away.1
  71.3 7.2 %collective-permute-start.7 = (bf16[16,128,256]{2,1,0:T(8,128)(2,1)S(1)}, bf16[16,128,256]{2,1,0:T(8,128)(2,1)S(1)}, u32[]{:S(2)}, u32[]{:S(2)}) collective-permute-start(bf16[16,128,256]{2,1,0:T(8,128)(2,1)S(1)} %last_away.1), channel_id=1, source_target_pairs={{0,1},{1,0},{2,3},{3,2},{4,5},{5,4},{6,7},{7,6},{8,9},{9,8},{10,11... | collective-permute-start | bytes 3145736 | tf_op jit(solution)/shard_map/ppermute | solution.py:262
  78.5 1.3 last_own.1
  79.8 1.0 collective-permute-done.7
  80.8 0.3 add_convert_fusion
  81.1 0.0 copy-start.2
  81.1 0.0 copy-start.3
  81.2 0.0 copy-start.4
  81.2 0.0 copy-start.5
  81.2 35.8 %all_to_all.20.parts = bf16[16,128,256]{2,1,0:T(8,128)(2,1)S(1)} all-to-all(bf16[16,128,256]{2,1,0:T(8,128)(2,1)S(1)} %add_convert_fusion), channel_id=1, replica_groups=mesh['y'=8,'zh'=4,'x'=4,'zl'=4,'core'=2] {'x','zl'}, dimensions={0} | all-to-all | bytes 2097152 | tf_op jit(solution)/shard_map/all_to_all | solution.py:265
  117.0 0.0 copy-done.2
  117.0 0.0 copy-done.3
  117.0 0.0 copy-done.4
  117.0 0.0 copy-done.5
  117.0 1.1 finish.1
  118.0 3.6 %collective-permute-start.8 = (f32[32,1,1152]{2,1,0:T(1,128)S(1)}, f32[32,1,1152]{2,1,0:T(1,128)S(1)}, u32[]{:S(2)}, u32[]{:S(2)}) collective-permute-start(f32[32,1,1152]{2,1,0:T(1,128)S(1)} %get-tuple-element.16), channel_id=1, source_target_pairs={{0,1},{1,0},{2,3},{3,2},{4,5},{5,4},{6,7},{7,6},{8,9},{9,8},{10,11... | collective-permute-start | bytes 442376 | tf_op jit(solution)/shard_map/ppermute | solution.py:270
  121.6 1.0 collective-permute-done.8
  122.6 0.2 add.7
  122.8 12.5 %all_to_all.21 = f32[32,1,1152]{2,1,0:T(1,128)S(1)} all-to-all(f32[32,1,1152]{2,1,0:T(1,128)S(1)} %add.7), channel_id=1, replica_groups=mesh['y'=8,'zh'=4,'x'=4,'zl'=4,'core'=2] {'y','x'}, dimensions={0} | all-to-all | bytes 294912 | tf_op jit(solution)/shard_map/all_to_all | solution.py:271
  135.3 0.1 reduce_sum.18
  135.5 18.5 %all_to_all.22 = f32[16,1,1152]{2,1,0:T(1,128)S(1)} all-to-all(f32[16,1,1152]{2,1,0:T(1,128)S(1)} %broadcast_in_dim.4), channel_id=1, replica_groups=mesh['y'=8,'zh'=4,'x'=4,'zl'=4,'core'=2] {'zh','zl'}, dimensions={0} | all-to-all | bytes 147456 | tf_op jit(solution)/shard_map/all_to_all | solution.py:249
  154.0 0.1 reduce_sum.19
  154.1 0.1 broadcast_in_dim.5
  154.1 13.4 %all_to_all.23.mine = f32[32,1,1152]{2,1,0:T(1,128)S(1)} all-to-all(f32[32,1,1152]{2,1,0:T(1,128)S(1)} %broadcast_in_dim.5), channel_id=1, replica_groups=mesh['y'=8,'zh'=4,'x'=4,'zl'=4,'core'=2] {'y','x'}, dimensions={0} | all-to-all | bytes 294912 | tf_op jit(solution)/shard_map/all_to_all | solution.py:249
  167.5 6.0 %collective-permute-start.9 = (f32[32,1,1152]{2,1,0:T(1,128)S(1)}, f32[32,1,1152]{2,1,0:T(1,128)S(1)}, u32[]{:S(2)}, u32[]{:S(2)}) collective-permute-start(f32[32,1,1152]{2,1,0:T(1,128)S(1)} %all_to_all.23.mine), channel_id=1, source_target_pairs={{0,1},{1,0},{2,3},{3,2},{4,5},{5,4},{6,7},{7,6},{8,9},{9,8},{10,11... | collective-permute-start | bytes 442376 | tf_op jit(solution)/shard_map/ppermute | solution.py:274
  173.5 1.0 collective-permute-done.9.other
  174.5 0.8 unpack.1
  (2 shorter events, 0.1 us)
Async XLA Ops:
  31.3 18.1 %collective-permute-start.2 = (bf16[512,256]{1,0:T(8,128)(2,1)S(1)}, bf16[512,256]{1,0:T(8,128)(2,1)S(1)}, u32[]{:S(2)}, u32[]{:S(2)}) collective-permute-start(bf16[512,256]{1,0:T(8,128)(2,1)S(1)} %all_gather.3.refs_1_), channel_id=1, source_target_pairs={{0,768},{128,896},{256,0},{384,128},{512,256},{640,384},{768,512},... | collective-permute-start | bytes 786440 | tf_op jit(solution)/shard_map/ppermute | solution.py:238
  38.8 13.6 %collective-permute-start.1 = (bf16[512,256]{1,0:T(8,128)(2,1)S(1)}, bf16[512,256]{1,0:T(8,128)(2,1)S(1)}, u32[]{:S(2)}, u32[]{:S(2)}) collective-permute-start(bf16[512,256]{1,0:T(8,128)(2,1)S(1)} %all_gather.3.refs_1_), channel_id=1, source_target_pairs={{0,256},{128,384},{256,512},{384,640},{512,768},{640,896},{768,0},... | collective-permute-start | bytes 786440 | tf_op jit(solution)/shard_map/ppermute | solution.py:238
  40.7 22.0 %collective-permute-start.3 = (bf16[512,256]{1,0:T(8,128)(2,1)S(1)}, bf16[512,256]{1,0:T(8,128)(2,1)S(1)}, u32[]{:S(2)}, u32[]{:S(2)}) collective-permute-start(bf16[512,256]{1,0:T(8,128)(2,1)S(1)} %all_gather.3.refs_1_), channel_id=1, source_target_pairs={{0,896},{128,0},{256,128},{384,256},{512,384},{640,512},{768,640},... | collective-permute-start | bytes 786440 | tf_op jit(solution)/shard_map/ppermute | solution.py:238
  45.4 17.3 %collective-permute-start = (bf16[512,256]{1,0:T(8,128)(2,1)S(1)}, bf16[512,256]{1,0:T(8,128)(2,1)S(1)}, u32[]{:S(2)}, u32[]{:S(2)}) collective-permute-start(bf16[512,256]{1,0:T(8,128)(2,1)S(1)} %all_gather.3.refs_1_), channel_id=1, source_target_pairs={{0,128},{128,256},{256,384},{384,512},{512,640},{640,768},{768,896... | collective-permute-start | bytes 786440 | tf_op jit(solution)/shard_map/ppermute | solution.py:238
  49.5 18.0 %collective-permute-start.6 = (bf16[512,256]{1,0:T(8,128)(2,1)S(1)}, bf16[512,256]{1,0:T(8,128)(2,1)S(1)}, u32[]{:S(2)}, u32[]{:S(2)}) collective-permute-start(bf16[512,256]{1,0:T(8,128)(2,1)S(1)} %collective-permute-done.2.refs_4_), channel_id=1, source_target_pairs={{0,896},{128,0},{256,128},{384,256},{512,384},{640,512},{768,640},... | collective-permute-start | bytes 786440 | tf_op jit(solution)/shard_map/ppermute | solution.py:238
  52.4 15.0 %collective-permute-start.5 = (bf16[512,256]{1,0:T(8,128)(2,1)S(1)}, bf16[512,256]{1,0:T(8,128)(2,1)S(1)}, u32[]{:S(2)}, u32[]{:S(2)}) collective-permute-start(bf16[512,256]{1,0:T(8,128)(2,1)S(1)} %broadcast_select_fusion), channel_id=1, source_target_pairs={{0,256},{1,769},{128,384},{129,897},{256,512},{257,1},{384,640},{3... | collective-permute-start | bytes 786440 | tf_op jit(solution)/shard_map/ppermute | solution.py:243
  57.9 12.1 %collective-permute-start.4 = (bf16[512,256]{1,0:T(8,128)(2,1)S(1)}, bf16[512,256]{1,0:T(8,128)(2,1)S(1)}, u32[]{:S(2)}, u32[]{:S(2)}) collective-permute-start(bf16[512,256]{1,0:T(8,128)(2,1)S(1)} %collective-permute-done.1.refs_3_), channel_id=1, source_target_pairs={{0,128},{128,256},{256,384},{384,512},{512,640},{640,768},{768,896... | collective-permute-start | bytes 786440 | tf_op jit(solution)/shard_map/ppermute | solution.py:238
  62.7 1.9 %copy-start = (bf16[1,96,128,128]{3,2,1,0:T(8,128)(2,1)S(1)}, bf16[1,96,128,128]{3,2,1,0:T(8,128)(2,1)}, u32[]{:S(2)}) copy-start(bf16[1,96,128,128]{3,2,1,0:T(8,128)(2,1)} %param.12) | copy-start | bytes 9437188
  64.6 5.5 %copy-start.1 = (bf16[1,96,128,128]{3,2,1,0:T(8,128)(2,1)S(1)}, bf16[1,96,128,128]{3,2,1,0:T(8,128)(2,1)}, u32[]{:S(2)}) copy-start(bf16[1,96,128,128]{3,2,1,0:T(8,128)(2,1)} %param.12) | copy-start | bytes 9437188
  71.3 9.5 %collective-permute-start.7 = (bf16[16,128,256]{2,1,0:T(8,128)(2,1)S(1)}, bf16[16,128,256]{2,1,0:T(8,128)(2,1)S(1)}, u32[]{:S(2)}, u32[]{:S(2)}) collective-permute-start(bf16[16,128,256]{2,1,0:T(8,128)(2,1)S(1)} %last_away.1), channel_id=1, source_target_pairs={{0,1},{1,0},{2,3},{3,2},{4,5},{5,4},{6,7},{7,6},{8,9},{9,8},{10,11... | collective-permute-start | bytes 3145736 | tf_op jit(solution)/shard_map/ppermute | solution.py:262
  81.1 35.8 %copy-start.2 = (bf16[256,256]{1,0:T(8,128)(2,1)S(1)}, bf16[256,256]{1,0:T(8,128)(2,1)}, u32[]{:S(2)}) copy-start(bf16[256,256]{1,0:T(8,128)(2,1)} %weight.1) | copy-start | bytes 393220
  81.1 35.8 %copy-start.3 = (bf16[128,256]{1,0:T(8,128)(2,1)S(1)}, bf16[128,256]{1,0:T(8,128)(2,1)}, u32[]{:S(2)}) copy-start(bf16[128,256]{1,0:T(8,128)(2,1)} %out_grad.1) | copy-start | bytes 196612
  81.2 35.8 %copy-start.4 = (s32[1,128]{1,0:T(1,128)S(1)}, s32[1,128]{1,0:T(1,128)}, u32[]{:S(2)}) copy-start(s32[1,128]{1,0:T(1,128)} %order.3) | copy-start | bytes 1540
  81.2 35.8 %copy-start.5 = (f32[256]{0:T(256)S(1)}, f32[256]{0:T(256)}, u32[]{:S(2)}) copy-start(f32[256]{0:T(256)} %param.14) | copy-start | bytes 3076
  118.0 4.6 %collective-permute-start.8 = (f32[32,1,1152]{2,1,0:T(1,128)S(1)}, f32[32,1,1152]{2,1,0:T(1,128)S(1)}, u32[]{:S(2)}, u32[]{:S(2)}) collective-permute-start(f32[32,1,1152]{2,1,0:T(1,128)S(1)} %get-tuple-element.16), channel_id=1, source_target_pairs={{0,1},{1,0},{2,3},{3,2},{4,5},{5,4},{6,7},{7,6},{8,9},{9,8},{10,11... | collective-permute-start | bytes 442376 | tf_op jit(solution)/shard_map/ppermute | solution.py:270
  167.5 7.0 %collective-permute-start.9 = (f32[32,1,1152]{2,1,0:T(1,128)S(1)}, f32[32,1,1152]{2,1,0:T(1,128)S(1)}, u32[]{:S(2)}, u32[]{:S(2)}) collective-permute-start(f32[32,1,1152]{2,1,0:T(1,128)S(1)} %all_to_all.23.mine), channel_id=1, source_target_pairs={{0,1},{1,0},{2,3},{3,2},{4,5},{5,4},{6,7},{7,6},{8,9},{9,8},{10,11... | collective-permute-start | bytes 442376 | tf_op jit(solution)/shard_map/ppermute | solution.py:274

commit v7 on v6

--- a/solution.py
+++ b/solution.py
@@ -239,8 +239,8 @@
 
     back1, ahead1, back2, ahead2 = (shift(own, by) for by in (1, -1, 2, -2))
     back3, ahead3 = shift(back2, 1), shift(ahead2, -1)
-    hops = [(2 * i + c, 2 * ((i + (2, -2)[c]) % 8) + c) for i in range(8) for c in range(2)]
-    far = lax.ppermute(jnp.where(core == 0, back2, ahead2), ("y", "core"), hops)
+    hops = [(2 * i + c, 2 * ((i + (-2, 2)[c]) % 8) + c) for i in range(8) for c in range(2)]
+    far = lax.ppermute(jnp.where(core == 0, ahead2, back2), ("y", "core"), hops)
     return (own, back1, back2, ahead2, ahead1), (back3, far, ahead3)
 
 

time: 176 us -> 174 us (0.989)
  starting transfers between devices: 44.1 us -> 38.2 us
  waiting for transfers between devices: 8.18 us -> 12.5 us
    ppermute x1, starting transfers between devices: 7.2 us -> 3.51 us  [local(): lax.ppermute(last_sums(GRID // 2, BF, away_later, begun, vals, late), 'co...]
    ppermute x1, waiting for transfers between devices: 0.01 us -> 2.54 us  [ring_gather(): far = lax.ppermute(jnp.where(core == 0, ahead2, back2), ('y', 'core'), hops)]
    ppermute x1, starting transfers between devices: 5.46 us -> 3.31 us  [ring_gather(): far = lax.ppermute(jnp.where(core == 0, ahead2, back2), ('y', 'core'), hops)]
  transfers between devices with their start and end apart: 10 -> 10, of which waited for: 6 -> 7; matrix products, arithmetic and copies ran while one was open for 0% -> 0% of each run, Pallas kernels for 2% -> 2%
where the time goes in v7:
time: 174 us
  blocking collectives  110 us (63%)
  starting transfers between devices  38.2 us (22%)
  waiting for transfers between devices  12.5 us (7%)
  Pallas kernels  8.66 us (5%)
  local copies, waits for them, and re-layouts  2.03 us (1%)
    all_to_all x1, blocking collectives, local(): parts = lax.all_to_all(paired, ('x', 'zl'), 0, 0, tiled=True)  35.4 us
    all_to_all x2, blocking collectives, spread(): return lax.all_to_all(repeated, axes, 0, 0, tiled=True)  31.6 us
    all_gather x1, blocking collectives, local(): near = lax.all_gather(clustered, 'zh', axis=0, tiled=True)  29 us
    ppermute x6, starting transfers between devices, shift(): return lax.ppermute(block, 'y', [(i, (i + by) % 8) for i in range(8)])  21.8 us
    all_to_all x1, blocking collectives, local(): block = lax.all_to_all(half, ('y', 'x'), 0, 0, tiled=True).sum(axis=0)  13.6 us
    ppermute x6, waiting for transfers between devices, shift(): return lax.ppermute(block, 'y', [(i, (i + by) % 8) for i in range(8)])  7.01 us
    ppermute x1, starting transfers between devices, local(): lax.ppermute(half, 'core', swap)  6 us
    ppermute x1, starting transfers between devices, local(): half = mine + lax.ppermute(other, 'core', swap)  3.59 us
  transfers between devices with their start and end apart: 10, of which 7 were waited for; matrix products, arithmetic and copies ran while one was open for 0% of the time, Pallas kernels for 2%

profile of v7, /device:TPU:1, one launch (start us, length us, event | category | flops | bytes accessed | tf_op | source)
XLA Modules:
  0.0 173.9 jit_solution(18047543589439348991)
XLA Ops:
  0.6 1.7 cluster.1
  2.3 29.0 %all_gather.3.refs_1_ = bf16[512,256]{1,0:T(8,128)(2,1)S(1)} all-gather(bf16[128,256]{1,0:T(8,128)(2,1)} %cluster.1), channel_id=1, replica_groups=mesh['y'=8,'zh'=4,'x'=4,'zl'=4,'core'=2] {'zh'}, dimensions={0}, use_global_device_ids=true | all-gather | bytes 327680 | tf_op jit(solution)/shard_map/all_gather | solution.py:257
  31.3 7.4 %collective-permute-start.2 = (bf16[512,256]{1,0:T(8,128)(2,1)S(1)}, bf16[512,256]{1,0:T(8,128)(2,1)S(1)}, u32[]{:S(2)}, u32[]{:S(2)}) collective-permute-start(bf16[512,256]{1,0:T(8,128)(2,1)S(1)} %all_gather.3.refs_1_), channel_id=1, source_target_pairs={{0,768},{128,896},{256,0},{384,128},{512,256},{640,384},{768,512},... | collective-permute-start | bytes 786440 | tf_op jit(solution)/shard_map/ppermute | solution.py:238
  38.8 1.9 %collective-permute-start.1 = (bf16[512,256]{1,0:T(8,128)(2,1)S(1)}, bf16[512,256]{1,0:T(8,128)(2,1)S(1)}, u32[]{:S(2)}, u32[]{:S(2)}) collective-permute-start(bf16[512,256]{1,0:T(8,128)(2,1)S(1)} %all_gather.3.refs_1_), channel_id=1, source_target_pairs={{0,256},{128,384},{256,512},{384,640},{512,768},{640,896},{768,0},... | collective-permute-start | bytes 786440 | tf_op jit(solution)/shard_map/ppermute | solution.py:238
  40.7 4.7 %collective-permute-start.3 = (bf16[512,256]{1,0:T(8,128)(2,1)S(1)}, bf16[512,256]{1,0:T(8,128)(2,1)S(1)}, u32[]{:S(2)}, u32[]{:S(2)}) collective-permute-start(bf16[512,256]{1,0:T(8,128)(2,1)S(1)} %all_gather.3.refs_1_), channel_id=1, source_target_pairs={{0,896},{128,0},{256,128},{384,256},{512,384},{640,512},{768,640},... | collective-permute-start | bytes 786440 | tf_op jit(solution)/shard_map/ppermute | solution.py:238
  45.4 1.9 %collective-permute-start = (bf16[512,256]{1,0:T(8,128)(2,1)S(1)}, bf16[512,256]{1,0:T(8,128)(2,1)S(1)}, u32[]{:S(2)}, u32[]{:S(2)}) collective-permute-start(bf16[512,256]{1,0:T(8,128)(2,1)S(1)} %all_gather.3.refs_1_), channel_id=1, source_target_pairs={{0,128},{128,256},{256,384},{384,512},{512,640},{640,768},{768,896... | collective-permute-start | bytes 786440 | tf_op jit(solution)/shard_map/ppermute | solution.py:238
  47.3 2.1 %collective-permute-done.2.refs_4_ = bf16[512,256]{1,0:T(8,128)(2,1)S(1)} collective-permute-done((bf16[512,256]{1,0:T(8,128)(2,1)S(1)}, bf16[512,256]{1,0:T(8,128)(2,1)S(1)}, u32[]{:S(2)}, u32[]{:S(2)}) %collective-permute-start.2) | collective-permute-done | bytes 262176 | tf_op jit(solution)/shard_map/ppermute | solution.py:238
  49.5 2.5 %collective-permute-start.6 = (bf16[512,256]{1,0:T(8,128)(2,1)S(1)}, bf16[512,256]{1,0:T(8,128)(2,1)S(1)}, u32[]{:S(2)}, u32[]{:S(2)}) collective-permute-start(bf16[512,256]{1,0:T(8,128)(2,1)S(1)} %collective-permute-done.2.refs_4_), channel_id=1, source_target_pairs={{0,896},{128,0},{256,128},{384,256},{512,384},{640,512},{768,640},... | collective-permute-start | bytes 786440 | tf_op jit(solution)/shard_map/ppermute | solution.py:238
  51.9 0.5 collective-permute-done.1.refs_3_
  52.4 3.3 %collective-permute-start.5 = (bf16[512,256]{1,0:T(8,128)(2,1)S(1)}, bf16[512,256]{1,0:T(8,128)(2,1)S(1)}, u32[]{:S(2)}, u32[]{:S(2)}) collective-permute-start(bf16[512,256]{1,0:T(8,128)(2,1)S(1)} %broadcast_select_fusion), channel_id=1, source_target_pairs={{0,768},{1,257},{128,896},{129,385},{256,0},{257,513},{384,128},{3... | collective-permute-start | bytes 786440 | tf_op jit(solution)/shard_map/ppermute | solution.py:243
  55.8 3.4 %collective-permute-start.4 = (bf16[512,256]{1,0:T(8,128)(2,1)S(1)}, bf16[512,256]{1,0:T(8,128)(2,1)S(1)}, u32[]{:S(2)}, u32[]{:S(2)}) collective-permute-start(bf16[512,256]{1,0:T(8,128)(2,1)S(1)} %collective-permute-done.1.refs_3_), channel_id=1, source_target_pairs={{0,128},{128,256},{256,384},{384,512},{512,640},{640,768},{768,896... | collective-permute-start | bytes 786440 | tf_op jit(solution)/shard_map/ppermute | solution.py:238
  59.8 0.7 pad_add_fusion.ints
  60.5 0.0 collective-permute-done.3.refs_5_
  60.5 0.0 collective-permute-done.refs_2_
  60.5 0.0 copy-start
  60.5 1.9 %copy-done = bf16[1,96,128,128]{3,2,1,0:T(8,128)(2,1)S(1)} copy-done((bf16[1,96,128,128]{3,2,1,0:T(8,128)(2,1)S(1)}, bf16[1,96,128,128]{3,2,1,0:T(8,128)(2,1)}, u32[]{:S(2)}) %copy-start) | copy-done | bytes 3145752
  62.4 0.0 copy-start.1
  62.4 2.5 %first_sums.1 = (f32[33,128,256]{2,1,0:T(8,128)S(1)}, s32[128]{0:T(128)S(1)}, s32[128]{0:T(128)S(1)}) custom-call(s32[99]{0:T(128)S(1)} %pad_add_fusion.ints, bf16[96,128,128]{2,1,0:T(8,128)(2,1)S(1)} %bitcast.6, bf16[512,256]{1,0:T(8,128)(2,1)S(1)} %all_gather.3.refs_1_, bf16[512,256]{1,0:T(8,128)(2,1)S(1)} %collective-permute-done.refs_2_, ...), custom_call_target="tpu_custom_call" | custom-call | flops 805306368 | bytes 8388608 | tf_op jit(solution)/shard_map/first_sums/pallas_call | solution.py:99
  65.0 0.0 collective-permute-done.6.refs_2_
  65.0 2.5 %collective-permute-done.5.refs_1_ = bf16[512,256]{1,0:T(8,128)(2,1)S(1)} collective-permute-done((bf16[512,256]{1,0:T(8,128)(2,1)S(1)}, bf16[512,256]{1,0:T(8,128)(2,1)S(1)}, u32[]{:S(2)}, u32[]{:S(2)}) %collective-permute-start.5) | collective-permute-done | bytes 262176 | tf_op jit(solution)/shard_map/ppermute | solution.py:243
  67.5 4.4 %collective-permute-done.4.refs_0_ = bf16[512,256]{1,0:T(8,128)(2,1)S(1)} collective-permute-done((bf16[512,256]{1,0:T(8,128)(2,1)S(1)}, bf16[512,256]{1,0:T(8,128)(2,1)S(1)}, u32[]{:S(2)}, u32[]{:S(2)}) %collective-permute-start.4) | collective-permute-done | bytes 262176 | tf_op jit(solution)/shard_map/ppermute | solution.py:238
  71.9 0.0 copy-done.1
  71.9 1.3 last_away.1
  73.2 3.5 %collective-permute-start.7 = (bf16[16,128,256]{2,1,0:T(8,128)(2,1)S(1)}, bf16[16,128,256]{2,1,0:T(8,128)(2,1)S(1)}, u32[]{:S(2)}, u32[]{:S(2)}) collective-permute-start(bf16[16,128,256]{2,1,0:T(8,128)(2,1)S(1)} %last_away.1), channel_id=1, source_target_pairs={{0,1},{1,0},{2,3},{3,2},{4,5},{5,4},{6,7},{7,6},{8,9},{9,8},{10,11... | collective-permute-start | bytes 3145736 | tf_op jit(solution)/shard_map/ppermute | solution.py:262
  76.7 1.3 last_own.1
  78.0 1.0 collective-permute-done.7
  79.0 0.3 add_convert_fusion
  79.3 0.0 copy-start.2
  79.3 0.0 copy-start.3
  79.3 0.0 copy-start.4
  79.3 0.0 copy-start.5
  79.3 35.4 %all_to_all.20.parts = bf16[16,128,256]{2,1,0:T(8,128)(2,1)S(1)} all-to-all(bf16[16,128,256]{2,1,0:T(8,128)(2,1)S(1)} %add_convert_fusion), channel_id=1, replica_groups=mesh['y'=8,'zh'=4,'x'=4,'zl'=4,'core'=2] {'x','zl'}, dimensions={0} | all-to-all | bytes 2097152 | tf_op jit(solution)/shard_map/all_to_all | solution.py:265
  114.8 0.0 copy-done.2
  114.8 0.0 copy-done.3
  114.8 0.0 copy-done.4
  114.8 0.0 copy-done.5
  114.8 1.1 finish.1
  115.8 3.6 %collective-permute-start.8 = (f32[32,1,1152]{2,1,0:T(1,128)S(1)}, f32[32,1,1152]{2,1,0:T(1,128)S(1)}, u32[]{:S(2)}, u32[]{:S(2)}) collective-permute-start(f32[32,1,1152]{2,1,0:T(1,128)S(1)} %get-tuple-element.16), channel_id=1, source_target_pairs={{0,1},{1,0},{2,3},{3,2},{4,5},{5,4},{6,7},{7,6},{8,9},{9,8},{10,11... | collective-permute-start | bytes 442376 | tf_op jit(solution)/shard_map/ppermute | solution.py:270
  119.4 1.0 collective-permute-done.8
  120.4 0.2 add.7
  120.6 13.6 %all_to_all.21 = f32[32,1,1152]{2,1,0:T(1,128)S(1)} all-to-all(f32[32,1,1152]{2,1,0:T(1,128)S(1)} %add.7), channel_id=1, replica_groups=mesh['y'=8,'zh'=4,'x'=4,'zl'=4,'core'=2] {'y','x'}, dimensions={0} | all-to-all | bytes 294912 | tf_op jit(solution)/shard_map/all_to_all | solution.py:271
  134.2 0.1 reduce_sum.18
  134.3 18.3 %all_to_all.22 = f32[16,1,1152]{2,1,0:T(1,128)S(1)} all-to-all(f32[16,1,1152]{2,1,0:T(1,128)S(1)} %broadcast_in_dim.4), channel_id=1, replica_groups=mesh['y'=8,'zh'=4,'x'=4,'zl'=4,'core'=2] {'zh','zl'}, dimensions={0} | all-to-all | bytes 147456 | tf_op jit(solution)/shard_map/all_to_all | solution.py:249
  152.6 0.1 reduce_sum.19
  152.7 0.1 broadcast_in_dim.5
  152.8 13.4 %all_to_all.23.mine = f32[32,1,1152]{2,1,0:T(1,128)S(1)} all-to-all(f32[32,1,1152]{2,1,0:T(1,128)S(1)} %broadcast_in_dim.5), channel_id=1, replica_groups=mesh['y'=8,'zh'=4,'x'=4,'zl'=4,'core'=2] {'y','x'}, dimensions={0} | all-to-all | bytes 294912 | tf_op jit(solution)/shard_map/all_to_all | solution.py:249
  166.1 6.0 %collective-permute-start.9 = (f32[32,1,1152]{2,1,0:T(1,128)S(1)}, f32[32,1,1152]{2,1,0:T(1,128)S(1)}, u32[]{:S(2)}, u32[]{:S(2)}) collective-permute-start(f32[32,1,1152]{2,1,0:T(1,128)S(1)} %all_to_all.23.mine), channel_id=1, source_target_pairs={{0,1},{1,0},{2,3},{3,2},{4,5},{5,4},{6,7},{7,6},{8,9},{9,8},{10,11... | collective-permute-start | bytes 442376 | tf_op jit(solution)/shard_map/ppermute | solution.py:274
  172.1 1.0 collective-permute-done.9.other
  173.1 0.8 unpack.1
  (2 shorter events, 0.1 us)
Async XLA Ops:
  31.3 18.1 %collective-permute-start.2 = (bf16[512,256]{1,0:T(8,128)(2,1)S(1)}, bf16[512,256]{1,0:T(8,128)(2,1)S(1)}, u32[]{:S(2)}, u32[]{:S(2)}) collective-permute-start(bf16[512,256]{1,0:T(8,128)(2,1)S(1)} %all_gather.3.refs_1_), channel_id=1, source_target_pairs={{0,768},{128,896},{256,0},{384,128},{512,256},{640,384},{768,512},... | collective-permute-start | bytes 786440 | tf_op jit(solution)/shard_map/ppermute | solution.py:238
  38.8 13.6 %collective-permute-start.1 = (bf16[512,256]{1,0:T(8,128)(2,1)S(1)}, bf16[512,256]{1,0:T(8,128)(2,1)S(1)}, u32[]{:S(2)}, u32[]{:S(2)}) collective-permute-start(bf16[512,256]{1,0:T(8,128)(2,1)S(1)} %all_gather.3.refs_1_), channel_id=1, source_target_pairs={{0,256},{128,384},{256,512},{384,640},{512,768},{640,896},{768,0},... | collective-permute-start | bytes 786440 | tf_op jit(solution)/shard_map/ppermute | solution.py:238
  40.7 19.8 %collective-permute-start.3 = (bf16[512,256]{1,0:T(8,128)(2,1)S(1)}, bf16[512,256]{1,0:T(8,128)(2,1)S(1)}, u32[]{:S(2)}, u32[]{:S(2)}) collective-permute-start(bf16[512,256]{1,0:T(8,128)(2,1)S(1)} %all_gather.3.refs_1_), channel_id=1, source_target_pairs={{0,896},{128,0},{256,128},{384,256},{512,384},{640,512},{768,640},... | collective-permute-start | bytes 786440 | tf_op jit(solution)/shard_map/ppermute | solution.py:238
  45.4 15.1 %collective-permute-start = (bf16[512,256]{1,0:T(8,128)(2,1)S(1)}, bf16[512,256]{1,0:T(8,128)(2,1)S(1)}, u32[]{:S(2)}, u32[]{:S(2)}) collective-permute-start(bf16[512,256]{1,0:T(8,128)(2,1)S(1)} %all_gather.3.refs_1_), channel_id=1, source_target_pairs={{0,128},{128,256},{256,384},{384,512},{512,640},{640,768},{768,896... | collective-permute-start | bytes 786440 | tf_op jit(solution)/shard_map/ppermute | solution.py:238
  49.5 15.5 %collective-permute-start.6 = (bf16[512,256]{1,0:T(8,128)(2,1)S(1)}, bf16[512,256]{1,0:T(8,128)(2,1)S(1)}, u32[]{:S(2)}, u32[]{:S(2)}) collective-permute-start(bf16[512,256]{1,0:T(8,128)(2,1)S(1)} %collective-permute-done.2.refs_4_), channel_id=1, source_target_pairs={{0,896},{128,0},{256,128},{384,256},{512,384},{640,512},{768,640},... | collective-permute-start | bytes 786440 | tf_op jit(solution)/shard_map/ppermute | solution.py:238
  52.4 15.1 %collective-permute-start.5 = (bf16[512,256]{1,0:T(8,128)(2,1)S(1)}, bf16[512,256]{1,0:T(8,128)(2,1)S(1)}, u32[]{:S(2)}, u32[]{:S(2)}) collective-permute-start(bf16[512,256]{1,0:T(8,128)(2,1)S(1)} %broadcast_select_fusion), channel_id=1, source_target_pairs={{0,768},{1,257},{128,896},{129,385},{256,0},{257,513},{384,128},{3... | collective-permute-start | bytes 786440 | tf_op jit(solution)/shard_map/ppermute | solution.py:243
  55.8 16.1 %collective-permute-start.4 = (bf16[512,256]{1,0:T(8,128)(2,1)S(1)}, bf16[512,256]{1,0:T(8,128)(2,1)S(1)}, u32[]{:S(2)}, u32[]{:S(2)}) collective-permute-start(bf16[512,256]{1,0:T(8,128)(2,1)S(1)} %collective-permute-done.1.refs_3_), channel_id=1, source_target_pairs={{0,128},{128,256},{256,384},{384,512},{512,640},{640,768},{768,896... | collective-permute-start | bytes 786440 | tf_op jit(solution)/shard_map/ppermute | solution.py:238
  60.5 1.9 %copy-start = (bf16[1,96,128,128]{3,2,1,0:T(8,128)(2,1)S(1)}, bf16[1,96,128,128]{3,2,1,0:T(8,128)(2,1)}, u32[]{:S(2)}) copy-start(bf16[1,96,128,128]{3,2,1,0:T(8,128)(2,1)} %param.12) | copy-start | bytes 9437188
  62.4 9.5 %copy-start.1 = (bf16[1,96,128,128]{3,2,1,0:T(8,128)(2,1)S(1)}, bf16[1,96,128,128]{3,2,1,0:T(8,128)(2,1)}, u32[]{:S(2)}) copy-start(bf16[1,96,128,128]{3,2,1,0:T(8,128)(2,1)} %param.12) | copy-start | bytes 9437188
  73.2 5.8 %collective-permute-start.7 = (bf16[16,128,256]{2,1,0:T(8,128)(2,1)S(1)}, bf16[16,128,256]{2,1,0:T(8,128)(2,1)S(1)}, u32[]{:S(2)}, u32[]{:S(2)}) collective-permute-start(bf16[16,128,256]{2,1,0:T(8,128)(2,1)S(1)} %last_away.1), channel_id=1, source_target_pairs={{0,1},{1,0},{2,3},{3,2},{4,5},{5,4},{6,7},{7,6},{8,9},{9,8},{10,11... | collective-permute-start | bytes 3145736 | tf_op jit(solution)/shard_map/ppermute | solution.py:262
  79.3 35.5 %copy-start.2 = (bf16[256,256]{1,0:T(8,128)(2,1)S(1)}, bf16[256,256]{1,0:T(8,128)(2,1)}, u32[]{:S(2)}) copy-start(bf16[256,256]{1,0:T(8,128)(2,1)} %weight.1) | copy-start | bytes 393220
  79.3 35.5 %copy-start.3 = (bf16[128,256]{1,0:T(8,128)(2,1)S(1)}, bf16[128,256]{1,0:T(8,128)(2,1)}, u32[]{:S(2)}) copy-start(bf16[128,256]{1,0:T(8,128)(2,1)} %out_grad.1) | copy-start | bytes 196612
  79.3 35.5 %copy-start.4 = (s32[1,128]{1,0:T(1,128)S(1)}, s32[1,128]{1,0:T(1,128)}, u32[]{:S(2)}) copy-start(s32[1,128]{1,0:T(1,128)} %order.3) | copy-start | bytes 1540
  79.3 35.5 %copy-start.5 = (f32[256]{0:T(256)S(1)}, f32[256]{0:T(256)}, u32[]{:S(2)}) copy-start(f32[256]{0:T(256)} %param.14) | copy-start | bytes 3076
  115.8 4.6 %collective-permute-start.8 = (f32[32,1,1152]{2,1,0:T(1,128)S(1)}, f32[32,1,1152]{2,1,0:T(1,128)S(1)}, u32[]{:S(2)}, u32[]{:S(2)}) collective-permute-start(f32[32,1,1152]{2,1,0:T(1,128)S(1)} %get-tuple-element.16), channel_id=1, source_target_pairs={{0,1},{1,0},{2,3},{3,2},{4,5},{5,4},{6,7},{7,6},{8,9},{9,8},{10,11... | collective-permute-start | bytes 442376 | tf_op jit(solution)/shard_map/ppermute | solution.py:270
  166.1 7.0 %collective-permute-start.9 = (f32[32,1,1152]{2,1,0:T(1,128)S(1)}, f32[32,1,1152]{2,1,0:T(1,128)S(1)}, u32[]{:S(2)}, u32[]{:S(2)}) collective-permute-start(f32[32,1,1152]{2,1,0:T(1,128)S(1)} %all_to_all.23.mine), channel_id=1, source_target_pairs={{0,1},{1,0},{2,3},{3,2},{4,5},{5,4},{6,7},{7,6},{8,9},{9,8},{10,11... | collective-permute-start | bytes 442376 | tf_op jit(solution)/shard_map/ppermute | solution.py:274

commit v8 on v7

--- a/solution.py
+++ b/solution.py
@@ -74,7 +74,7 @@
             row, col = at >> 5, at & 31
             back = (here - (col >> 2)) & 7
             away = (row & 1) ^ core
-            to = away * (GRID // 2) + (row >> 1)
+            to = away * (GRID // 2) + ((row >> 1) & 3) * 4 + (row >> 3)
             entry = k + (back * 4 + (col & 3)) * 128 + to * 4096
             for held, n in zip(lists, counts):
                 held[n] = entry
@@ -262,7 +262,7 @@
     away = lax.ppermute(last_sums(GRID // 2, BF, away_later, begun, vals, late), "core", swap)
     own = last_sums(0, F32, own_later, begun, vals, late)
     paired = (own + away.astype(F32)).astype(BF)
-    parts = lax.all_to_all(paired, ("x", "zl"), 0, 0, tiled=True)
+    parts = lax.all_to_all(paired, ("zl", "x"), 0, 0, tiled=True)
     core = core.reshape(1)
     activated, mine, other = finish(
         core, parts, node_order, weight, out_bias.reshape(1, F), out_grad

time: 174 us -> 175 us (level)
    all_to_all x1, blocking collectives: 35.4 us -> 33.3 us  [local(): parts = lax.all_to_all(paired, ('zl', 'x'), 0, 0, tiled=True)]
  transfers between devices with their start and end apart: 10 -> 10, of which waited for: 7 -> 7; matrix products, arithmetic and copies ran while one was open for 0% -> 0% of each run, Pallas kernels for 2% -> 3%
where the time goes in v8:
time: 175 us; the launch traced here: 174 us
  blocking collectives  109 us (62%)
  starting transfers between devices  39.2 us (22%)
  waiting for transfers between devices  10.9 us (6%)
  Pallas kernels  10.2 us (6%)
  local copies, waits for them, and re-layouts  2.03 us (1%)
    all_to_all x1, blocking collectives, local(): parts = lax.all_to_all(paired, ('zl', 'x'), 0, 0, tiled=True)  33.3 us
    all_to_all x2, blocking collectives, spread(): return lax.all_to_all(repeated, axes, 0, 0, tiled=True)  31.3 us
    all_gather x1, blocking collectives, local(): near = lax.all_gather(clustered, 'zh', axis=0, tiled=True)  29 us
    ppermute x6, starting transfers between devices, shift(): return lax.ppermute(block, 'y', [(i, (i + by) % 8) for i in range(8)])  21.8 us
    all_to_all x1, blocking collectives, local(): block = lax.all_to_all(half, ('y', 'x'), 0, 0, tiled=True).sum(axis=0)  14.9 us
    ppermute x6, waiting for transfers between devices, shift(): return lax.ppermute(block, 'y', [(i, (i + by) % 8) for i in range(8)])  7.01 us
    ppermute x1, starting transfers between devices, local(): lax.ppermute(half, 'core', swap)  6 us
    ppermute x1, starting transfers between devices, local(): half = mine + lax.ppermute(other, 'core', swap)  4.61 us
  transfers between devices with their start and end apart: 10, of which 7 were waited for; matrix products, arithmetic and copies ran while one was open for 0% of the time, Pallas kernels for 3%

profile of v8, /device:TPU:1, one launch (start us, length us, event | category | flops | bytes accessed | tf_op | source)
XLA Modules:
  0.0 173.8 jit_solution(10630353939025958091)
XLA Ops:
  0.6 1.7 cluster.1
  2.3 29.0 %all_gather.3.refs_1_ = bf16[512,256]{1,0:T(8,128)(2,1)S(1)} all-gather(bf16[128,256]{1,0:T(8,128)(2,1)} %cluster.1), channel_id=1, replica_groups=mesh['y'=8,'zh'=4,'x'=4,'zl'=4,'core'=2] {'zh'}, dimensions={0}, use_global_device_ids=true | all-gather | bytes 327680 | tf_op jit(solution)/shard_map/all_gather | solution.py:257
  31.3 7.4 %collective-permute-start.2 = (bf16[512,256]{1,0:T(8,128)(2,1)S(1)}, bf16[512,256]{1,0:T(8,128)(2,1)S(1)}, u32[]{:S(2)}, u32[]{:S(2)}) collective-permute-start(bf16[512,256]{1,0:T(8,128)(2,1)S(1)} %all_gather.3.refs_1_), channel_id=1, source_target_pairs={{0,768},{128,896},{256,0},{384,128},{512,256},{640,384},{768,512},... | collective-permute-start | bytes 786440 | tf_op jit(solution)/shard_map/ppermute | solution.py:238
  38.8 1.9 %collective-permute-start.1 = (bf16[512,256]{1,0:T(8,128)(2,1)S(1)}, bf16[512,256]{1,0:T(8,128)(2,1)S(1)}, u32[]{:S(2)}, u32[]{:S(2)}) collective-permute-start(bf16[512,256]{1,0:T(8,128)(2,1)S(1)} %all_gather.3.refs_1_), channel_id=1, source_target_pairs={{0,256},{128,384},{256,512},{384,640},{512,768},{640,896},{768,0},... | collective-permute-start | bytes 786440 | tf_op jit(solution)/shard_map/ppermute | solution.py:238
  40.7 4.7 %collective-permute-start.3 = (bf16[512,256]{1,0:T(8,128)(2,1)S(1)}, bf16[512,256]{1,0:T(8,128)(2,1)S(1)}, u32[]{:S(2)}, u32[]{:S(2)}) collective-permute-start(bf16[512,256]{1,0:T(8,128)(2,1)S(1)} %all_gather.3.refs_1_), channel_id=1, source_target_pairs={{0,896},{128,0},{256,128},{384,256},{512,384},{640,512},{768,640},... | collective-permute-start | bytes 786440 | tf_op jit(solution)/shard_map/ppermute | solution.py:238
  45.4 1.9 %collective-permute-start = (bf16[512,256]{1,0:T(8,128)(2,1)S(1)}, bf16[512,256]{1,0:T(8,128)(2,1)S(1)}, u32[]{:S(2)}, u32[]{:S(2)}) collective-permute-start(bf16[512,256]{1,0:T(8,128)(2,1)S(1)} %all_gather.3.refs_1_), channel_id=1, source_target_pairs={{0,128},{128,256},{256,384},{384,512},{512,640},{640,768},{768,896... | collective-permute-start | bytes 786440 | tf_op jit(solution)/shard_map/ppermute | solution.py:238
  47.3 2.1 %collective-permute-done.2.refs_4_ = bf16[512,256]{1,0:T(8,128)(2,1)S(1)} collective-permute-done((bf16[512,256]{1,0:T(8,128)(2,1)S(1)}, bf16[512,256]{1,0:T(8,128)(2,1)S(1)}, u32[]{:S(2)}, u32[]{:S(2)}) %collective-permute-start.2) | collective-permute-done | bytes 262176 | tf_op jit(solution)/shard_map/ppermute | solution.py:238
  49.5 2.5 %collective-permute-start.6 = (bf16[512,256]{1,0:T(8,128)(2,1)S(1)}, bf16[512,256]{1,0:T(8,128)(2,1)S(1)}, u32[]{:S(2)}, u32[]{:S(2)}) collective-permute-start(bf16[512,256]{1,0:T(8,128)(2,1)S(1)} %collective-permute-done.2.refs_4_), channel_id=1, source_target_pairs={{0,896},{128,0},{256,128},{384,256},{512,384},{640,512},{768,640},... | collective-permute-start | bytes 786440 | tf_op jit(solution)/shard_map/ppermute | solution.py:238
  51.9 0.5 collective-permute-done.1.refs_3_
  52.4 3.3 %collective-permute-start.5 = (bf16[512,256]{1,0:T(8,128)(2,1)S(1)}, bf16[512,256]{1,0:T(8,128)(2,1)S(1)}, u32[]{:S(2)}, u32[]{:S(2)}) collective-permute-start(bf16[512,256]{1,0:T(8,128)(2,1)S(1)} %broadcast_select_fusion), channel_id=1, source_target_pairs={{0,768},{1,257},{128,896},{129,385},{256,0},{257,513},{384,128},{3... | collective-permute-start | bytes 786440 | tf_op jit(solution)/shard_map/ppermute | solution.py:243
  55.8 3.4 %collective-permute-start.4 = (bf16[512,256]{1,0:T(8,128)(2,1)S(1)}, bf16[512,256]{1,0:T(8,128)(2,1)S(1)}, u32[]{:S(2)}, u32[]{:S(2)}) collective-permute-start(bf16[512,256]{1,0:T(8,128)(2,1)S(1)} %collective-permute-done.1.refs_3_), channel_id=1, source_target_pairs={{0,128},{128,256},{256,384},{384,512},{512,640},{640,768},{768,896... | collective-permute-start | bytes 786440 | tf_op jit(solution)/shard_map/ppermute | solution.py:238
  59.8 0.7 pad_add_fusion.ints
  60.5 0.0 collective-permute-done.3.refs_5_
  60.5 0.0 collective-permute-done.refs_2_
  60.5 0.0 copy-start
  60.5 1.9 %copy-done = bf16[1,96,128,128]{3,2,1,0:T(8,128)(2,1)S(1)} copy-done((bf16[1,96,128,128]{3,2,1,0:T(8,128)(2,1)S(1)}, bf16[1,96,128,128]{3,2,1,0:T(8,128)(2,1)}, u32[]{:S(2)}) %copy-start) | copy-done | bytes 3145752
  62.4 0.0 copy-start.1
  62.4 3.8 %first_sums.1 = (f32[33,128,256]{2,1,0:T(8,128)S(1)}, s32[128]{0:T(128)S(1)}, s32[128]{0:T(128)S(1)}) custom-call(s32[99]{0:T(128)S(1)} %pad_add_fusion.ints, bf16[96,128,128]{2,1,0:T(8,128)(2,1)S(1)} %bitcast.6, bf16[512,256]{1,0:T(8,128)(2,1)S(1)} %all_gather.3.refs_1_, bf16[512,256]{1,0:T(8,128)(2,1)S(1)} %collective-permute-done.refs_2_, ...), custom_call_target="tpu_custom_call" | custom-call | flops 805306368 | bytes 8388608 | tf_op jit(solution)/shard_map/first_sums/pallas_call | solution.py:99
  66.2 0.0 collective-permute-done.6.refs_2_
  66.2 1.3 collective-permute-done.5.refs_1_
  67.5 4.4 %collective-permute-done.4.refs_0_ = bf16[512,256]{1,0:T(8,128)(2,1)S(1)} collective-permute-done((bf16[512,256]{1,0:T(8,128)(2,1)S(1)}, bf16[512,256]{1,0:T(8,128)(2,1)S(1)}, u32[]{:S(2)}, u32[]{:S(2)}) %collective-permute-start.4) | collective-permute-done | bytes 262176 | tf_op jit(solution)/shard_map/ppermute | solution.py:238
  71.9 0.0 copy-done.1
  71.9 1.3 last_away.1
  73.2 3.5 %collective-permute-start.7 = (bf16[16,128,256]{2,1,0:T(8,128)(2,1)S(1)}, bf16[16,128,256]{2,1,0:T(8,128)(2,1)S(1)}, u32[]{:S(2)}, u32[]{:S(2)}) collective-permute-start(bf16[16,128,256]{2,1,0:T(8,128)(2,1)S(1)} %last_away.1), channel_id=1, source_target_pairs={{0,1},{1,0},{2,3},{3,2},{4,5},{5,4},{6,7},{7,6},{8,9},{9,8},{10,11... | collective-permute-start | bytes 3145736 | tf_op jit(solution)/shard_map/ppermute | solution.py:262
  76.7 1.6 last_own.1
  78.3 0.7 collective-permute-done.7
  79.0 0.3 add_convert_fusion
  79.3 0.0 copy-start.2
  79.3 0.0 copy-start.3
  79.3 0.0 copy-start.4
  79.3 0.0 copy-start.5
  79.3 33.3 %all_to_all.20.parts = bf16[16,128,256]{2,1,0:T(8,128)(2,1)S(1)} all-to-all(bf16[16,128,256]{2,1,0:T(8,128)(2,1)S(1)} %add_convert_fusion), channel_id=1, replica_groups=mesh['y'=8,'zh'=4,'x'=4,'zl'=4,'core'=2] {'zl','x'}, dimensions={0} | all-to-all | bytes 2097152 | tf_op jit(solution)/shard_map/all_to_all | solution.py:265
  112.6 0.0 copy-done.2
  112.7 0.0 copy-done.3
  112.7 0.0 copy-done.4
  112.7 0.0 copy-done.5
  112.7 1.1 finish.1
  113.7 4.6 %collective-permute-start.8 = (f32[32,1,1152]{2,1,0:T(1,128)S(1)}, f32[32,1,1152]{2,1,0:T(1,128)S(1)}, u32[]{:S(2)}, u32[]{:S(2)}) collective-permute-start(f32[32,1,1152]{2,1,0:T(1,128)S(1)} %get-tuple-element.16), channel_id=1, source_target_pairs={{0,1},{1,0},{2,3},{3,2},{4,5},{5,4},{6,7},{7,6},{8,9},{9,8},{10,11... | collective-permute-start | bytes 442376 | tf_op jit(solution)/shard_map/ppermute | solution.py:270
  118.3 1.0 collective-permute-done.8
  119.3 0.2 add.7
  119.5 14.9 %all_to_all.21 = f32[32,1,1152]{2,1,0:T(1,128)S(1)} all-to-all(f32[32,1,1152]{2,1,0:T(1,128)S(1)} %add.7), channel_id=1, replica_groups=mesh['y'=8,'zh'=4,'x'=4,'zl'=4,'core'=2] {'y','x'}, dimensions={0} | all-to-all | bytes 294912 | tf_op jit(solution)/shard_map/all_to_all | solution.py:271
  134.4 0.1 reduce_sum.18
  134.5 17.9 %all_to_all.22 = f32[16,1,1152]{2,1,0:T(1,128)S(1)} all-to-all(f32[16,1,1152]{2,1,0:T(1,128)S(1)} %broadcast_in_dim.4), channel_id=1, replica_groups=mesh['y'=8,'zh'=4,'x'=4,'zl'=4,'core'=2] {'zh','zl'}, dimensions={0} | all-to-all | bytes 147456 | tf_op jit(solution)/shard_map/all_to_all | solution.py:249
  152.5 0.1 reduce_sum.19
  152.5 0.1 broadcast_in_dim.5
  152.6 13.4 %all_to_all.23.mine = f32[32,1,1152]{2,1,0:T(1,128)S(1)} all-to-all(f32[32,1,1152]{2,1,0:T(1,128)S(1)} %broadcast_in_dim.5), channel_id=1, replica_groups=mesh['y'=8,'zh'=4,'x'=4,'zl'=4,'core'=2] {'y','x'}, dimensions={0} | all-to-all | bytes 294912 | tf_op jit(solution)/shard_map/all_to_all | solution.py:249
  166.0 6.0 %collective-permute-start.9 = (f32[32,1,1152]{2,1,0:T(1,128)S(1)}, f32[32,1,1152]{2,1,0:T(1,128)S(1)}, u32[]{:S(2)}, u32[]{:S(2)}) collective-permute-start(f32[32,1,1152]{2,1,0:T(1,128)S(1)} %all_to_all.23.mine), channel_id=1, source_target_pairs={{0,1},{1,0},{2,3},{3,2},{4,5},{5,4},{6,7},{7,6},{8,9},{9,8},{10,11... | collective-permute-start | bytes 442376 | tf_op jit(solution)/shard_map/ppermute | solution.py:274
  172.0 1.0 collective-permute-done.9.other
  173.0 0.8 unpack.1
  (2 shorter events, 0.1 us)
Async XLA Ops:
  31.3 18.1 %collective-permute-start.2 = (bf16[512,256]{1,0:T(8,128)(2,1)S(1)}, bf16[512,256]{1,0:T(8,128)(2,1)S(1)}, u32[]{:S(2)}, u32[]{:S(2)}) collective-permute-start(bf16[512,256]{1,0:T(8,128)(2,1)S(1)} %all_gather.3.refs_1_), channel_id=1, source_target_pairs={{0,768},{128,896},{256,0},{384,128},{512,256},{640,384},{768,512},... | collective-permute-start | bytes 786440 | tf_op jit(solution)/shard_map/ppermute | solution.py:238
  38.8 13.6 %collective-permute-start.1 = (bf16[512,256]{1,0:T(8,128)(2,1)S(1)}, bf16[512,256]{1,0:T(8,128)(2,1)S(1)}, u32[]{:S(2)}, u32[]{:S(2)}) collective-permute-start(bf16[512,256]{1,0:T(8,128)(2,1)S(1)} %all_gather.3.refs_1_), channel_id=1, source_target_pairs={{0,256},{128,384},{256,512},{384,640},{512,768},{640,896},{768,0},... | collective-permute-start | bytes 786440 | tf_op jit(solution)/shard_map/ppermute | solution.py:238
  40.7 19.8 %collective-permute-start.3 = (bf16[512,256]{1,0:T(8,128)(2,1)S(1)}, bf16[512,256]{1,0:T(8,128)(2,1)S(1)}, u32[]{:S(2)}, u32[]{:S(2)}) collective-permute-start(bf16[512,256]{1,0:T(8,128)(2,1)S(1)} %all_gather.3.refs_1_), channel_id=1, source_target_pairs={{0,896},{128,0},{256,128},{384,256},{512,384},{640,512},{768,640},... | collective-permute-start | bytes 786440 | tf_op jit(solution)/shard_map/ppermute | solution.py:238
  45.4 15.1 %collective-permute-start = (bf16[512,256]{1,0:T(8,128)(2,1)S(1)}, bf16[512,256]{1,0:T(8,128)(2,1)S(1)}, u32[]{:S(2)}, u32[]{:S(2)}) collective-permute-start(bf16[512,256]{1,0:T(8,128)(2,1)S(1)} %all_gather.3.refs_1_), channel_id=1, source_target_pairs={{0,128},{128,256},{256,384},{384,512},{512,640},{640,768},{768,896... | collective-permute-start | bytes 786440 | tf_op jit(solution)/shard_map/ppermute | solution.py:238
  49.5 16.7 %collective-permute-start.6 = (bf16[512,256]{1,0:T(8,128)(2,1)S(1)}, bf16[512,256]{1,0:T(8,128)(2,1)S(1)}, u32[]{:S(2)}, u32[]{:S(2)}) collective-permute-start(bf16[512,256]{1,0:T(8,128)(2,1)S(1)} %collective-permute-done.2.refs_4_), channel_id=1, source_target_pairs={{0,896},{128,0},{256,128},{384,256},{512,384},{640,512},{768,640},... | collective-permute-start | bytes 786440 | tf_op jit(solution)/shard_map/ppermute | solution.py:238
  52.4 15.1 %collective-permute-start.5 = (bf16[512,256]{1,0:T(8,128)(2,1)S(1)}, bf16[512,256]{1,0:T(8,128)(2,1)S(1)}, u32[]{:S(2)}, u32[]{:S(2)}) collective-permute-start(bf16[512,256]{1,0:T(8,128)(2,1)S(1)} %broadcast_select_fusion), channel_id=1, source_target_pairs={{0,768},{1,257},{128,896},{129,385},{256,0},{257,513},{384,128},{3... | collective-permute-start | bytes 786440 | tf_op jit(solution)/shard_map/ppermute | solution.py:243
  55.8 16.1 %collective-permute-start.4 = (bf16[512,256]{1,0:T(8,128)(2,1)S(1)}, bf16[512,256]{1,0:T(8,128)(2,1)S(1)}, u32[]{:S(2)}, u32[]{:S(2)}) collective-permute-start(bf16[512,256]{1,0:T(8,128)(2,1)S(1)} %collective-permute-done.1.refs_3_), channel_id=1, source_target_pairs={{0,128},{128,256},{256,384},{384,512},{512,640},{640,768},{768,896... | collective-permute-start | bytes 786440 | tf_op jit(solution)/shard_map/ppermute | solution.py:238
  60.5 1.9 %copy-start = (bf16[1,96,128,128]{3,2,1,0:T(8,128)(2,1)S(1)}, bf16[1,96,128,128]{3,2,1,0:T(8,128)(2,1)}, u32[]{:S(2)}) copy-start(bf16[1,96,128,128]{3,2,1,0:T(8,128)(2,1)} %param.12) | copy-start | bytes 9437188
  62.4 9.5 %copy-start.1 = (bf16[1,96,128,128]{3,2,1,0:T(8,128)(2,1)S(1)}, bf16[1,96,128,128]{3,2,1,0:T(8,128)(2,1)}, u32[]{:S(2)}) copy-start(bf16[1,96,128,128]{3,2,1,0:T(8,128)(2,1)} %param.12) | copy-start | bytes 9437188
  73.2 5.8 %collective-permute-start.7 = (bf16[16,128,256]{2,1,0:T(8,128)(2,1)S(1)}, bf16[16,128,256]{2,1,0:T(8,128)(2,1)S(1)}, u32[]{:S(2)}, u32[]{:S(2)}) collective-permute-start(bf16[16,128,256]{2,1,0:T(8,128)(2,1)S(1)} %last_away.1), channel_id=1, source_target_pairs={{0,1},{1,0},{2,3},{3,2},{4,5},{5,4},{6,7},{7,6},{8,9},{9,8},{10,11... | collective-permute-start | bytes 3145736 | tf_op jit(solution)/shard_map/ppermute | solution.py:262
  79.3 33.4 %copy-start.2 = (bf16[256,256]{1,0:T(8,128)(2,1)S(1)}, bf16[256,256]{1,0:T(8,128)(2,1)}, u32[]{:S(2)}) copy-start(bf16[256,256]{1,0:T(8,128)(2,1)} %weight.1) | copy-start | bytes 393220
  79.3 33.4 %copy-start.3 = (bf16[128,256]{1,0:T(8,128)(2,1)S(1)}, bf16[128,256]{1,0:T(8,128)(2,1)}, u32[]{:S(2)}) copy-start(bf16[128,256]{1,0:T(8,128)(2,1)} %out_grad.1) | copy-start | bytes 196612
  79.3 33.4 %copy-start.4 = (s32[1,128]{1,0:T(1,128)S(1)}, s32[1,128]{1,0:T(1,128)}, u32[]{:S(2)}) copy-start(s32[1,128]{1,0:T(1,128)} %order.3) | copy-start | bytes 1540
  79.3 33.4 %copy-start.5 = (f32[256]{0:T(256)S(1)}, f32[256]{0:T(256)}, u32[]{:S(2)}) copy-start(f32[256]{0:T(256)} %param.14) | copy-start | bytes 3076
  113.7 5.6 %collective-permute-start.8 = (f32[32,1,1152]{2,1,0:T(1,128)S(1)}, f32[32,1,1152]{2,1,0:T(1,128)S(1)}, u32[]{:S(2)}, u32[]{:S(2)}) collective-permute-start(f32[32,1,1152]{2,1,0:T(1,128)S(1)} %get-tuple-element.16), channel_id=1, source_target_pairs={{0,1},{1,0},{2,3},{3,2},{4,5},{5,4},{6,7},{7,6},{8,9},{9,8},{10,11... | collective-permute-start | bytes 442376 | tf_op jit(solution)/shard_map/ppermute | solution.py:270
  166.0 7.0 %collective-permute-start.9 = (f32[32,1,1152]{2,1,0:T(1,128)S(1)}, f32[32,1,1152]{2,1,0:T(1,128)S(1)}, u32[]{:S(2)}, u32[]{:S(2)}) collective-permute-start(f32[32,1,1152]{2,1,0:T(1,128)S(1)} %all_to_all.23.mine), channel_id=1, source_target_pairs={{0,1},{1,0},{2,3},{3,2},{4,5},{5,4},{6,7},{7,6},{8,9},{9,8},{10,11... | collective-permute-start | bytes 442376 | tf_op jit(solution)/shard_map/ppermute | solution.py:274
